TPU v7x, 256 devices: a whole 4x4x8 slice. The times are simulated.
256 devices in a mesh: dp: 32 (over y, z), tensor: 8 (over x, core).
Axes of the slice: x: 4, y: 4, z: 8, core: 2. Of those that a mesh axis runs over, the one named last changes fastest.
Arguments:
- hidden: bfloat16 [8192, 14336], P('dp', 'tensor'), may hold values from -6 to 6
- cotangent: bfloat16 [8192, 4096], P(('dp', 'tensor')), may hold values from -0.375 to 0.375
- error_buf: bfloat16 [14336, 4096], P('tensor', 'dp'), may hold values from -24 to 24
- q_start: float32 [4096, 64], replicated, may hold values from -6 to 6
Outputs:
- scaled_basis: float32 [14336, 64], P('tensor')
- q_new: float32 [4096, 64], replicated
All inputs are finite; a program needn't handle non-finite values.
Results may differ from a plain program's by a relative error of at most 0.0003.
Values may be sent and summed in bfloat16 or wider, within the bound.
No kernel may reach another device: no remote copies, remote signals or barrier semaphores. Data moves between devices by JAX's collectives and lax.ppermute only.
A program may use at most 128 MiB of HBM per device.

v0:
```python
import functools
import math

import jax
import jax.numpy as jnp
from jax import lax
from jax.experimental import pallas as pl
from jax.experimental.pallas import tpu as pltpu
from jax.sharding import Mesh
from jax.sharding import PartitionSpec as P

FF = 14336
D = 4096
RANK = 64
N_DP = 32
TOK = 256
NY, NZ, NX, NC = 4, 8, 4, 2
FB = FF // (NX * NC)
CB = D // NX
EB = D // N_DP
TB = TOK // (NX * NC)
f32, bf16 = jnp.float32, jnp.bfloat16
HIGHEST = lax.Precision.HIGHEST
NN = (((1,), (0,)), ((), ()))
NT = (((1,), (1,)), ((), ()))


def split3(a):
    hi = a.astype(bf16)
    rest = a - hi.astype(f32)
    mid = rest.astype(bf16)
    low = (rest - mid.astype(f32)).astype(bf16)
    return jnp.concatenate([hi, mid, low], axis=0)


def add3(a):
    n = a.shape[0] // 3
    return a[:n] + (a[n : 2 * n] + a[2 * n :])


def dot3(a, b, dims):
    return add3(lax.dot_general(a, b, dims, preferred_element_type=f32))


def gram3(a3):
    g = lax.dot_general(a3, a3, NT, preferred_element_type=f32)
    r = RANK
    g00, g01, g02 = g[:r, :r], g[:r, r : 2 * r], g[:r, 2 * r :]
    g10, g11, g20 = g[r : 2 * r, :r], g[r : 2 * r, r : 2 * r], g[2 * r :, :r]
    return g00 + ((g01 + g10) + (g11 + (g02 + g20)))


def wide(column):
    return jnp.broadcast_to(column, (8, 2 * RANK))


def inverse_factor(gram):
    rows = lax.broadcasted_iota(jnp.int32, (RANK, RANK), 0)
    cols = lax.broadcasted_iota(jnp.int32, (RANK, RANK), 1)
    both = jnp.concatenate([gram, jnp.where(rows == cols, 1.0, 0.0).astype(f32)], axis=1)
    sub = lax.broadcasted_iota(jnp.int32, (8, 2 * RANK), 0)
    count = RANK // 8
    tiles = [both[8 * i : 8 * i + 8] for i in range(count)]
    for p in range(count):
        columns = [[wide(tiles[i][:, 8 * p + j : 8 * p + j + 1]) for j in range(8)] for i in range(p, count)]
        panel, own, pivots, scales = tiles[p], columns[0], jnp.ones((8, 2 * RANK), f32), []
        for s in range(8):
            pivot = own[s][s : s + 1]
            scales.append(1.0 / pivot)
            pivots = jnp.where(sub == s, pivot, pivots)
            factor = jnp.where(sub > s, own[s] * scales[s], 0.0)
            panel = panel - factor * panel[s : s + 1]
            for j in range(s + 1, 8):
                own[j] = own[j] - factor * own[j][s : s + 1]
        for i in range(p + 1, count):
            below, tile = columns[i - p], tiles[i]
            for s in range(8):
                factor = below[s] * scales[s]
                tile = tile - factor * panel[s : s + 1]
                for j in range(s + 1, 8):
                    below[j] = below[j] - factor * own[j][s : s + 1]
            tiles[i] = tile
        tiles[p] = panel * lax.rsqrt(pivots)
    return jnp.concatenate(tiles, axis=0)[:, RANK:]


def near_inverse_factor(off):
    rows = lax.broadcasted_iota(jnp.int32, (RANK, RANK), 0)
    cols = lax.broadcasted_iota(jnp.int32, (RANK, RANK), 1)
    lower = jnp.where(rows > cols, 1.0, jnp.where(rows == cols, 0.5, 0.0)).astype(f32)
    first = off * lower
    second = -lower * lax.dot_general(first, first, NT, precision=HIGHEST, preferred_element_type=f32)
    square = jnp.dot(first, first, precision=HIGHEST, preferred_element_type=f32)
    eye = jnp.where(rows == cols, 1.0, 0.0).astype(f32)
    return eye - first + (square - second)


def dot6(a, b3):
    hi = a.astype(bf16).astype(f32)
    mid = (a - hi).astype(bf16).astype(f32)
    low = a - hi - mid
    one = jnp.concatenate([hi, hi, hi, mid], axis=1).astype(bf16)
    two = jnp.concatenate([mid, low], axis=1).astype(bf16)
    high, middle = b3[:RANK], b3[RANK : 2 * RANK]
    out = jnp.dot(one, jnp.concatenate([b3, high], axis=0), preferred_element_type=f32)
    return out + jnp.dot(two, jnp.concatenate([middle, high], axis=0), preferred_element_type=f32)


def pack(square):
    return jnp.concatenate([square[: RANK // 2], square[RANK // 2 :]], axis=1)


def unpack(packed):
    return jnp.concatenate([packed[:, :RANK], packed[:, RANK:]], axis=0)


def call(kernel, out_shape, *args, scratch=(), hbm=(), unread=(), out_hbm=False):
    vmem, far, anywhere = (pl.BlockSpec(memory_space=m) for m in (pltpu.VMEM, pltpu.HBM, pl.ANY))
    many = isinstance(out_shape, list)
    shapes = [jax.ShapeDtypeStruct(*s) for s in (out_shape if many else [out_shape])]
    return pl.pallas_call(
        kernel,
        out_shape=shapes if many else shapes[0],
        in_specs=[far if i in hbm else anywhere if i in unread else vmem for i in range(len(args))],
        out_specs=[far if out_hbm else vmem] * len(shapes) if many else vmem,
        scratch_shapes=list(scratch),
        compiler_params=pltpu.CompilerParams(vmem_limit_bytes=32 * 1024 * 1024),
    )(*args)


DEALT = (0, 2, 1, 3)


def rows_at(index, size):
    return pl.ds(pl.multiple_of(index * size, size), size)


def in_order(index, refs, ks=(0, 1, 3, 2)):
    for k, ref in zip(ks, refs, strict=True):
        yield lax.rem(index + 4 - k, 4), ref


def sum_in_order(slots_ref, index, refs, ks=(0, 1, 3, 2)):
    for place, ref in in_order(index, refs, ks):
        slots_ref[place] = ref[...]
    return (slots_ref[0] + slots_ref[1]) + (slots_ref[2] + slots_ref[3])


def scatter(whole_ref, index, refs):
    size = whole_ref.shape[0] // 4
    for k, ref in zip(DEALT, refs, strict=True):
        ref[...] = whole_ref[rows_at(lax.rem(index + k, 4), size), :]


def factor_kernel(qt_ref, q3_ref, own_ref, qt, sems):
    at, cut = lax.axis_index("y") * NZ + lax.axis_index("z"), 1024
    pairs = [(qt_ref.at[:, i : i + cut], qt.at[:, i : i + cut]) for i in range(0, D, cut)]
    pairs += [(qt_ref.at[:, rows_at(at, EB)], own_ref)]
    copies = [pltpu.make_async_copy(a, b, sems.at[i]) for i, (a, b) in enumerate(pairs)]
    for copy in copies:
        copy.start()
    for i in range(D // cut):
        copies[i].wait()
        q3_ref[:, i * cut : (i + 1) * cut] = split3(qt[:, i * cut : (i + 1) * cut])
    copies[-1].wait()


def project_kernel(cot_ref, other_ref, q3_ref, out_ref, both_ref):
    c = lax.axis_index("c")
    both_ref[rows_at(c, TB), :] = cot_ref[...]
    both_ref[rows_at(1 - c, TB), :] = other_ref[...]
    got = lax.dot_general(both_ref[...], q3_ref[...], NT, preferred_element_type=f32)
    got = got[:, :RANK] + (got[:, RANK : 2 * RANK] + got[:, 2 * RANK :])
    part = TB // 2
    for i in range(NC):
        own = got[i * TB : (i + 1) * TB]
        out_ref[i * part : (i + 1) * part, :] = jnp.concatenate([own[:part], own[part:]], axis=1)


def fetch_kernel(hidden_ref, err_ref, after_ref, h_ref, e_ref, sems):
    copies = [pltpu.make_async_copy(a, b, sems.at[i]) for i, (a, b) in enumerate(((hidden_ref, h_ref), (err_ref, e_ref)))]
    for copy in copies:
        copy.start()
    for copy in copies:
        copy.wait()


def columns_kernel(both_ref, after_ref, *out_refs):
    x = lax.axis_index("x")
    for k, ref in zip(DEALT, out_refs, strict=True):
        ref[...] = both_ref[:, rows_at(lax.rem(x + k, NX), CB)]


def left_kernel(
    got_ref, a_got_ref, b_got_ref, c_got_ref, hidden_ref, err_ref, q_ref,
    own_ref, a_ref, b_ref, c_ref, slots_ref, whole_ref,
):
    for place, ref in in_order(lax.axis_index("x"), (got_ref, a_got_ref, b_got_ref, c_got_ref)):
        slots_ref[place] = ref[...]
    packed = slots_ref[...].reshape(TOK // 2, 2 * RANK).T
    proj = jnp.concatenate([packed[:RANK], packed[RANK:]], axis=1)
    h = hidden_ref[...].reshape(NX * NC, 2, TB // 2, FB)
    h = jnp.concatenate([h[:, 0].reshape(TOK // 2, FB), h[:, 1].reshape(TOK // 2, FB)], axis=0)
    whole_ref[...] = dot3(split3(proj), h, NN) + dot3(split3(q_ref[...]), err_ref[...], NT)
    scatter(whole_ref, lax.axis_index("y"), (own_ref, a_ref, b_ref, c_ref))


def halve_kernel(own_ref, a_ref, b_ref, c_ref, after_ref, keep_ref, send_ref, slots_ref, both_ref):
    both_ref[...] = sum_in_order(slots_ref, lax.axis_index("y"), (own_ref, a_ref, b_ref, c_ref), DEALT)
    bit, half = lax.rem(lax.axis_index("z"), 2), keep_ref.shape[0]
    keep_ref[...] = both_ref[rows_at(bit, half), :]
    send_ref[...] = both_ref[rows_at(1 - bit, half), :]


def add_kernel(a_ref, b_ref, out_ref):
    out_ref[...] = a_ref[...] + b_ref[...]


def sum_z_kernel(own_ref, a_ref, b_ref, c_ref, out_ref, slots_ref):
    out_ref[...] = sum_in_order(slots_ref, lax.axis_index("z") // 2, (own_ref, a_ref, b_ref, c_ref))


def sum_z_after_kernel(own_ref, a_ref, b_ref, c_ref, *rest):
    sum_z_kernel(own_ref, a_ref, b_ref, c_ref, *rest[-2:])


def sum_x_kernel(own_ref, a_ref, b_ref, c_ref, out_ref, slots_ref):
    out_ref[...] = sum_in_order(slots_ref, lax.axis_index("x"), (own_ref, a_ref, b_ref, c_ref))


def join_z_kernel(own_ref, other_ref, out_ref):
    bit, half = lax.rem(lax.axis_index("z"), 2), own_ref.shape[0]
    out_ref[rows_at(bit, half), :] = own_ref[...]
    out_ref[rows_at(1 - bit, half), :] = other_ref[...]


def mixed_kernel(own_ref, a_ref, b_ref, c_ref, hidden_ref, err_ref, after_ref, p3_ref, keep_ref, send_ref, p_ref, all_ref):
    for place, ref in in_order(lax.axis_index("y"), (own_ref, a_ref, b_ref, c_ref)):
        p_ref[rows_at(place, RANK // NY), :] = ref[...]
    p3 = split3(p_ref[...])
    p3_ref[...] = p3
    all_ref[:, :TOK] = dot3(p3, hidden_ref[...], NT)
    all_ref[:, TOK:] = dot3(p3, err_ref[...], NN)
    gram = pack(gram3(p3))
    c, half = lax.axis_index("c"), RANK // 2
    for ref, core in ((keep_ref, c), (send_ref, 1 - c)):
        ref[:, : TOK + EB] = all_ref[rows_at(core, half), :]
        ref[:, TOK + EB :] = gram


def right_kernel(mixed_ref, cot_ref, a_cot_ref, b_cot_ref, c_cot_ref, own_ref, a_ref, b_ref, c_ref, slots_ref, whole_ref):
    x, at = lax.axis_index("x"), lax.axis_index("y") * NZ + lax.axis_index("z")
    for place, ref in in_order(x, (cot_ref, a_cot_ref, b_cot_ref, c_cot_ref), DEALT):
        slots_ref[place] = ref[...]
    part = dot3(split3(mixed_ref[:, :TOK]), slots_ref[...].reshape(TOK, CB), NN)
    err_q = mixed_ref[:, TOK : TOK + EB]
    here = [jnp.where(at == x * (CB // EB) + i, err_q, 0.0) for i in range(CB // EB)]
    whole_ref[...] = part + jnp.concatenate(here, axis=1)
    scatter(whole_ref, lax.axis_index("y"), (own_ref, a_ref, b_ref, c_ref))


def first_kernel(mixed_ref, after_ref, inv_ref):
    inv_ref[...] = inverse_factor(unpack(mixed_ref[:, TOK + EB :]))


def basis_kernel(inv_ref, p3_ref, b3_ref, gram_ref):
    b3 = split3(dot6(inv_ref[...], p3_ref[...]))
    b3_ref[...] = b3
    gram_ref[...] = pack(gram3(b3))


def sum_y_kernel(own_ref, a_ref, b_ref, c_ref, after_ref, out_ref, slots_ref):
    out_ref[...] = sum_in_order(slots_ref, lax.axis_index("y"), (own_ref, a_ref, b_ref, c_ref), DEALT)


def add_after_kernel(a_ref, b_ref, after_ref, out_ref):
    out_ref[...] = a_ref[...] + b_ref[...]


def block_kernel(own_ref, a_ref, b_ref, c_ref, gram_ref, other_ref, out_ref):
    for place, ref in in_order(lax.axis_index("y"), (own_ref, a_ref, b_ref, c_ref)):
        out_ref[rows_at(place, RANK // 2 // NY), :CB] = ref[...]
    out_ref[:, CB:] = gram_ref[...] + other_ref[...]


def second_kernel(own_ref, a_ref, b_ref, c_ref, inv_ref, total_ref, inverse_ref, slots_ref):
    for place, ref in in_order(lax.axis_index("x"), (own_ref, a_ref, b_ref, c_ref)):
        slots_ref[place] = ref[:, CB:]
    gram = unpack((slots_ref[0] + slots_ref[1]) + (slots_ref[2] + slots_ref[3]))
    rows = lax.broadcasted_iota(jnp.int32, (RANK, RANK), 0)
    cols = lax.broadcasted_iota(jnp.int32, (RANK, RANK), 1)
    off = gram - jnp.where(rows == cols, 1.0, 0.0).astype(f32)
    near = jnp.max(jnp.abs(off)) < 1e-3

    @pl.when(near)
    def _():
        inverse_ref[...] = near_inverse_factor(off)

    @pl.when(jnp.logical_not(near))
    def _():
        inverse_ref[...] = inverse_factor(gram)

    inverse = inverse_ref[...]
    total_ref[...] = jnp.dot(inverse, inv_ref[...], precision=HIGHEST, preferred_element_type=f32) * (1.0 / N_DP)


def new_kernel(*refs):
    total_ref, inverse_ref, b3_ref, out_ref, basis_ref, s_ref, whole_ref, scaled_ref, sems = refs[2 * NX :]
    x, c, half, total, copies = lax.axis_index("x"), lax.axis_index("c"), RANK // 2, total_ref[...], []
    for k, (place, ref) in enumerate(in_order(x, refs[:NX])):
        s_ref[k, rows_at(c, half), :] = ref[:, :CB]
        s_ref[k, rows_at(1 - c, half), :] = refs[NX + k][:, :CB]
        whole_ref[k] = dot6(total, split3(s_ref[k]))
        cols = rows_at(place, CB)
        copies.append(pltpu.make_async_copy(whole_ref.at[k], out_ref.at[:, cols], sems.at[k]))
        copies[-1].start()
        if k == 0:
            scaled_ref[...] = dot6(inverse_ref[...] * math.sqrt(FF), b3_ref[...])
            copies.append(pltpu.make_async_copy(scaled_ref, basis_ref, sems.at[NX]))
            copies[-1].start()
    for copy in copies:
        copy.wait()


def swap(a):
    return lax.ppermute(a, "c", [(0, 1), (1, 0)])


def swap_z(a):
    return lax.ppermute(a, "z", [(i, i ^ 1) for i in range(NZ)])


def shift(a, axis, k):
    size, step = {"y": (NY, 1), "z": (NZ, 2), "x": (NX, 1)}[axis]
    return lax.ppermute(a, axis, [(i, (i + k * step) % size) for i in range(size)])


def deal(blocks, axis):
    return [blocks[0]] + [shift(block, axis, k) for k, block in zip(DEALT[1:], blocks[1:], strict=True)]


def share(block, axis):
    return [block] + [shift(block, axis, k) for k in (1, 3, 2)]


def shards(hidden, cotangent, error_buf, q_start):
    qt = q_start.T
    dma, half = pltpu.SemaphoreType.DMA, RANK // 2
    qt, hid, err = (pltpu.with_memory_space_constraint(a, pltpu.HBM) for a in (q_start.T, hidden, error_buf))
    other = swap(cotangent)
    q3, q_own = call(
        factor_kernel, [((3 * RANK, D), bf16), ((RANK, EB), f32)], qt, scratch=[pltpu.VMEM((RANK, D), f32), dma((5,))], hbm=(0,)
    )
    proj, both = call(project_kernel, [((TB, 2 * RANK), f32), ((2 * TB, D), bf16)], cotangent, other, q3)
    hid, err = call(
        fetch_kernel, [((TOK, FB), bf16), ((FB, EB), bf16)], hid, err, proj, scratch=[dma((2,))], hbm=(0, 1), unread=(2,)
    )
    quarter, eighth = ((RANK // NY, FB), f32), ((RANK // NY // 2, FB), f32)
    parts = call(
        left_kernel, [quarter] * 4, *share(proj, "x"), hid, err, q_own,
        scratch=[pltpu.VMEM((4, TB, 2 * RANK), f32), pltpu.VMEM((RANK, FB), f32)],
    )

    parts = deal(parts, "y")
    blocks = call(columns_kernel, [((2 * TB, CB), bf16)] * NX, both, parts[2], unread=(1,))
    cot = deal(blocks, "x")
    keep, send = call(
        halve_kernel, [eighth, eighth], *parts, cot[0], scratch=[pltpu.VMEM((4, *quarter[0]), f32), pltpu.VMEM(*quarter)], unread=(4,)
    )
    p = call(add_kernel, eighth, keep, swap_z(send))
    p = call(
        sum_z_after_kernel, eighth, *share(p, "z"), cot[2], cot[3], scratch=[pltpu.VMEM((4, *eighth[0]), f32)], unread=(4, 5)
    )
    p = call(join_z_kernel, quarter, p, swap_z(p))

    halves = ((half, TOK + EB + 2 * RANK), f32)
    p3, keep, send = call(
        mixed_kernel, [((3 * RANK, FB), bf16), halves, halves], *share(p, "y"), hid, err, cot[1],
        scratch=[pltpu.VMEM((RANK, FB), f32), pltpu.VMEM((RANK, TOK + EB), f32)], unread=(6,),
    )
    mixed = call(add_kernel, halves, keep, swap(send))
    mixed = call(sum_x_kernel, halves, *share(mixed, "x"), scratch=[pltpu.VMEM((4, *halves[0]), f32)])

    piece = ((half // NY, CB), f32)
    parts = call(
        right_kernel, [piece] * 4, mixed, *cot, scratch=[pltpu.VMEM((4, 2 * TB, CB), bf16), pltpu.VMEM((half, CB), f32)]
    )
    inverse = call(first_kernel, ((RANK, RANK), f32), mixed, parts[0], unread=(1,))
    s = call(sum_y_kernel, piece, *deal(parts, "y"), inverse, scratch=[pltpu.VMEM((4, *piece[0]), f32)], unread=(4,))
    b3, gram = call(basis_kernel, [((3 * RANK, FB), bf16), ((half, 2 * RANK), f32)], inverse, p3)
    s = call(add_after_kernel, piece, s, swap_z(s), gram, unread=(2,))
    s = call(sum_z_kernel, piece, *share(s, "z"), scratch=[pltpu.VMEM((4, *piece[0]), f32)])
    s = call(block_kernel, ((half, CB + 2 * RANK), f32), *share(s, "y"), gram, swap(gram))
    blocks = share(s, "x")
    square = ((RANK, RANK), f32)
    total, second = call(second_kernel, [square, square], *blocks, inverse, scratch=[pltpu.VMEM((4, half, 2 * RANK), f32)])
    wide_block = pltpu.VMEM((NX, RANK, CB), f32)
    q_new, scaled = call(
        new_kernel, [((RANK, D), f32), ((RANK, FB), f32)], *blocks, *[swap(b) for b in blocks], total, second, b3,
        scratch=[wide_block, wide_block, pltpu.VMEM((RANK, FB), f32), dma((NX + 1,))], out_hbm=True,
    )
    return scaled.T, q_new.T


def solution(mesh):
    fine = Mesh(mesh.devices.reshape(NY, NZ, NX, NC), ("y", "z", "x", "c"))
    dp, tensor = ("y", "z"), ("x", "c")
    placed = (P(dp, tensor), P(dp + tensor, None), P(tensor, dp), P())
    return jax.shard_map(
        shards, mesh=fine, in_specs=placed, out_specs=(P(tensor, None), P()), check_vma=False
    )
```

profile of v0, /device:TPU:1, one launch (start us, length us, event | category | flops | bytes accessed | tf_op | source)
XLA Modules:
  0.0 110.9 jit_solution(16314991106109099701)
XLA Ops:
  0.6 3.3 %collective-permute-start = (bf16[32,4096]{1,0:T(8,128)(2,1)}, bf16[32,4096]{1,0:T(8,128)(2,1)S(1)}, u32[]{:S(2)}, u32[]{:S(2)}) collective-permute-start(bf16[32,4096]{1,0:T(8,128)(2,1)} %cot_ref.1), channel_id=1, source_target_pairs={{0,1},{1,0},{2,3},{3,2},{4,5},{5,4},{6,7},{7,6},{8,9},{9,8},{10,11... | collective-permute-start | bytes 786440 | tf_op jit(solution)/shard_map/ppermute | solution.py:326
  11.2 1.6 %collective-permute-done.1.a_got_ref = f32[32,128]{1,0:T(8,128)S(1)} collective-permute-done((f32[32,128]{1,0:T(8,128)S(1)}, f32[32,128]{1,0:T(8,128)S(1)}, u32[]{:S(2)}, u32[]{:S(2)}) %collective-permute-start.1) | collective-permute-done | bytes 16416 | tf_op jit(solution)/shard_map/ppermute | solution.py:335
  14.8 2.6 %collective-permute-start.4 = (f32[16,1792]{1,0:T(8,128)S(1)}, f32[16,1792]{1,0:T(8,128)S(1)}, u32[]{:S(2)}, u32[]{:S(2)}) collective-permute-start(f32[16,1792]{1,0:T(8,128)S(1)} %get-tuple-element.37), channel_id=1, source_target_pairs={{0,128},{64,192},{128,0},{192,64},{1,129},{65,193},{129,1},{193,65... | collective-permute-start | bytes 344072 | tf_op jit(solution)/shard_map/ppermute | solution.py:335
  18.6 2.7 %collective-permute-start.12 = (bf16[64,1024]{1,0:T(8,128)(2,1)S(1)}, bf16[64,1024]{1,0:T(8,128)(2,1)S(1)}, u32[]{:S(2)}, u32[]{:S(2)}) collective-permute-start(bf16[64,1024]{1,0:T(8,128)(2,1)S(1)} %get-tuple-element.45), channel_id=1, source_target_pairs={{0,6},{2,0},{4,2},{6,4},{1,7},{3,1},{5,3},{7,5},{8,14},{10,8},{12,... | collective-permute-start | bytes 393224 | tf_op jit(solution)/shard_map/ppermute | solution.py:335
  22.0 1.7 %collective-permute-start.7 = (f32[8,1792]{1,0:T(8,128)S(1)}, f32[8,1792]{1,0:T(8,128)S(1)}, u32[]{:S(2)}, u32[]{:S(2)}) collective-permute-start(f32[8,1792]{1,0:T(8,128)S(1)} %get-tuple-element.43), channel_id=1, source_target_pairs={{0,8},{8,0},{16,24},{24,16},{32,40},{40,32},{48,56},{56,48},{1,9},... | collective-permute-start | bytes 172040 | tf_op jit(solution)/shard_map/ppermute | solution.py:330
  25.3 6.8 %collective-permute-start.10 = (f32[8,1792]{1,0:T(8,128)S(1)}, f32[8,1792]{1,0:T(8,128)S(1)}, u32[]{:S(2)}, u32[]{:S(2)}) collective-permute-start(f32[8,1792]{1,0:T(8,128)S(1)} %shard_map.65.own_ref), channel_id=1, source_target_pairs={{0,32},{8,40},{16,48},{24,56},{32,0},{40,8},{48,16},{56,24},{1,33}... | collective-permute-start | bytes 172040 | tf_op jit(solution)/shard_map/ppermute | solution.py:335
  32.2 2.4 %collective-permute-start.8 = (f32[8,1792]{1,0:T(8,128)S(1)}, f32[8,1792]{1,0:T(8,128)S(1)}, u32[]{:S(2)}, u32[]{:S(2)}) collective-permute-start(f32[8,1792]{1,0:T(8,128)S(1)} %shard_map.65.own_ref), channel_id=1, source_target_pairs={{0,16},{8,24},{16,32},{24,40},{32,48},{40,56},{48,0},{56,8},{1,17}... | collective-permute-start | bytes 172040 | tf_op jit(solution)/shard_map/ppermute | solution.py:335
  34.5 2.2 %collective-permute-done.9.b_ref = f32[8,1792]{1,0:T(8,128)S(1)} collective-permute-done((f32[8,1792]{1,0:T(8,128)S(1)}, f32[8,1792]{1,0:T(8,128)S(1)}, u32[]{:S(2)}, u32[]{:S(2)}) %collective-permute-start.9) | collective-permute-done | bytes 57376 | tf_op jit(solution)/shard_map/ppermute | solution.py:335
  39.1 1.7 %collective-permute-start.17 = (bf16[64,1024]{1,0:T(8,128)(2,1)S(1)}, bf16[64,1024]{1,0:T(8,128)(2,1)S(1)}, u32[]{:S(2)}, u32[]{:S(2)}) collective-permute-start(bf16[64,1024]{1,0:T(8,128)(2,1)S(1)} %get-tuple-element.46), channel_id=1, source_target_pairs={{0,4},{2,6},{4,0},{6,2},{1,5},{3,7},{5,1},{7,3},{8,12},{10,14},{12... | collective-permute-start | bytes 393224 | tf_op jit(solution)/shard_map/ppermute | solution.py:335
  41.9 1.9 %collective-permute-start.16 = (f32[16,1792]{1,0:T(8,128)S(1)}, f32[16,1792]{1,0:T(8,128)S(1)}, u32[]{:S(2)}, u32[]{:S(2)}) collective-permute-start(f32[16,1792]{1,0:T(8,128)S(1)} %shard_map.67.own_ref), channel_id=1, source_target_pairs={{0,128},{64,192},{128,0},{192,64},{1,129},{65,193},{129,1},{193,65... | collective-permute-start | bytes 344072 | tf_op jit(solution)/shard_map/ppermute | solution.py:335
  45.5 1.6 %collective-permute-done.16.c_ref = f32[16,1792]{1,0:T(8,128)S(1)} collective-permute-done((f32[16,1792]{1,0:T(8,128)S(1)}, f32[16,1792]{1,0:T(8,128)S(1)}, u32[]{:S(2)}, u32[]{:S(2)}) %collective-permute-start.16) | collective-permute-done | bytes 114720 | tf_op jit(solution)/shard_map/ppermute | solution.py:335
  47.2 1.8 %collective-permute-done.15.b_ref = f32[16,1792]{1,0:T(8,128)S(1)} collective-permute-done((f32[16,1792]{1,0:T(8,128)S(1)}, f32[16,1792]{1,0:T(8,128)S(1)}, u32[]{:S(2)}, u32[]{:S(2)}) %collective-permute-start.15) | collective-permute-done | bytes 114720 | tf_op jit(solution)/shard_map/ppermute | solution.py:335
  51.1 8.2 %collective-permute-start.18 = (f32[32,512]{1,0:T(8,128)S(1)}, f32[32,512]{1,0:T(8,128)S(1)}, u32[]{:S(2)}, u32[]{:S(2)}) collective-permute-start(f32[32,512]{1,0:T(8,128)S(1)} %get-tuple-element.48), channel_id=1, source_target_pairs={{0,1},{1,0},{2,3},{3,2},{4,5},{5,4},{6,7},{7,6},{8,9},{9,8},{10,11... | collective-permute-start | bytes 196616 | tf_op jit(solution)/shard_map/ppermute | solution.py:326
  61.9 3.1 %collective-permute-done.21.c_ref = f32[32,512]{1,0:T(8,128)S(1)} collective-permute-done((f32[32,512]{1,0:T(8,128)S(1)}, f32[32,512]{1,0:T(8,128)S(1)}, u32[]{:S(2)}, u32[]{:S(2)}) %collective-permute-start.21) | collective-permute-done | bytes 65568 | tf_op jit(solution)/shard_map/ppermute | solution.py:335
  67.2 2.7 %collective-permute-start.24 = (f32[8,1024]{1,0:T(8,128)S(1)}, f32[8,1024]{1,0:T(8,128)S(1)}, u32[]{:S(2)}, u32[]{:S(2)}) collective-permute-start(f32[8,1024]{1,0:T(8,128)S(1)} %get-tuple-element.52), channel_id=1, source_target_pairs={{0,192},{64,0},{128,64},{192,128},{1,193},{65,1},{129,65},{193,129... | collective-permute-start | bytes 98312 | tf_op jit(solution)/shard_map/ppermute | solution.py:335
  69.9 1.9 %shard_map.72.after_ref.inv_ref = f32[64,64]{1,0:T(8,128)S(1)} custom-call(f32[32,512]{1,0:T(8,128)S(1)} %shard_map.70.mixed_ref, f32[8,1024]{1,0:T(8,128)S(1)} %get-tuple-element.49.after_ref.own_ref), custom_call_target="tpu_custom_call" | custom-call | tf_op jit(solution)/shard_map/pallas_call | solution.py:121
  74.7 4.2 %collective-permute-start.28 = (f32[8,1024]{1,0:T(8,128)S(1)}, f32[8,1024]{1,0:T(8,128)S(1)}, u32[]{:S(2)}, u32[]{:S(2)}) collective-permute-start(f32[8,1024]{1,0:T(8,128)S(1)} %shard_map.75.own_ref), channel_id=1, source_target_pairs={{0,32},{8,40},{16,48},{24,56},{32,0},{40,8},{48,16},{56,24},{1,33}... | collective-permute-start | bytes 98312 | tf_op jit(solution)/shard_map/ppermute | solution.py:335
  82.6 2.1 %collective-permute-done.26.a_ref = f32[8,1024]{1,0:T(8,128)S(1)} collective-permute-done((f32[8,1024]{1,0:T(8,128)S(1)}, f32[8,1024]{1,0:T(8,128)S(1)}, u32[]{:S(2)}, u32[]{:S(2)}) %collective-permute-start.26) | collective-permute-done | bytes 32800 | tf_op jit(solution)/shard_map/ppermute | solution.py:335
  84.7 1.7 %collective-permute-start.31 = (f32[8,1024]{1,0:T(8,128)S(1)}, f32[8,1024]{1,0:T(8,128)S(1)}, u32[]{:S(2)}, u32[]{:S(2)}) collective-permute-start(f32[8,1024]{1,0:T(8,128)S(1)} %shard_map.76.own_ref), channel_id=1, source_target_pairs={{0,128},{64,192},{128,0},{192,64},{1,129},{65,193},{129,1},{193,65... | collective-permute-start | bytes 98312 | tf_op jit(solution)/shard_map/ppermute | solution.py:335
  86.3 1.9 %collective-permute-start.30 = (f32[8,1024]{1,0:T(8,128)S(1)}, f32[8,1024]{1,0:T(8,128)S(1)}, u32[]{:S(2)}, u32[]{:S(2)}) collective-permute-start(f32[8,1024]{1,0:T(8,128)S(1)} %shard_map.76.own_ref), channel_id=1, source_target_pairs={{0,192},{64,0},{128,64},{192,128},{1,193},{65,1},{129,65},{193,129... | collective-permute-start | bytes 98312 | tf_op jit(solution)/shard_map/ppermute | solution.py:335
  88.3 6.1 %collective-permute-start.32 = (f32[32,128]{1,0:T(8,128)S(1)}, f32[32,128]{1,0:T(8,128)S(1)}, u32[]{:S(2)}, u32[]{:S(2)}) collective-permute-start(f32[32,128]{1,0:T(8,128)S(1)} %get-tuple-element.54.after_ref.gram_ref), channel_id=1, source_target_pairs={{0,1},{1,0},{2,3},{3,2},{4,5},{5,4},{6,7},{7,6},{8,9},{9,8},{10,11... | collective-permute-start | bytes 49160 | tf_op jit(solution)/shard_map/ppermute | solution.py:326
  97.5 5.1 %collective-permute-start.36 = (f32[32,1152]{1,0:T(8,128)S(1)}, f32[32,1152]{1,0:T(8,128)S(1)}, u32[]{:S(2)}, u32[]{:S(2)}) collective-permute-start(f32[32,1152]{1,0:T(8,128)S(1)} %shard_map.77.own_ref.refs_0_), channel_id=1, source_target_pairs={{0,1},{1,0},{2,3},{3,2},{4,5},{5,4},{6,7},{7,6},{8,9},{9,8},{10,11... | collective-permute-start | bytes 442376 | tf_op jit(solution)/shard_map/ppermute | solution.py:326
  102.6 3.7 %collective-permute-start.39 = (f32[32,1152]{1,0:T(8,128)S(1)}, f32[32,1152]{1,0:T(8,128)S(1)}, u32[]{:S(2)}, u32[]{:S(2)}) collective-permute-start(f32[32,1152]{1,0:T(8,128)S(1)} %collective-permute-done.35.c_ref.refs_3_), channel_id=1, source_target_pairs={{0,1},{1,0},{2,3},{3,2},{4,5},{5,4},{6,7},{7,6},{8,9},{9,8},{10,11... | collective-permute-start | bytes 442376 | tf_op jit(solution)/shard_map/ppermute | solution.py:326
  109.0 1.7 %shard_map.79 = (f32[64,4096]{1,0:T(8,128)}, f32[64,1792]{1,0:T(8,128)}) custom-call(f32[32,1152]{1,0:T(8,128)S(1)} %shard_map.77.own_ref.refs_0_, f32[32,1152]{1,0:T(8,128)S(1)} %collective-permute-done.33.a_ref.refs_1_, f32[32,1152]{1,0:T(8,128)S(1)} %collective-permute-done.34.b_ref.refs_2_, f32[32,1152]{1,0:T(8,128)S(1)} %collective-permute-done.35.c_ref.refs_3_, ...), custom_call_target="tpu_custom_call" | custom-call | tf_op jit(solution)/shard_map/pallas_call | solution.py:121
  (79 shorter events, 37.2 us)
Async XLA Ops:
  13.4 5.1 %collective-permute-start.5 = (f32[16,1792]{1,0:T(8,128)S(1)}, f32[16,1792]{1,0:T(8,128)S(1)}, u32[]{:S(2)}, u32[]{:S(2)}) collective-permute-start(f32[16,1792]{1,0:T(8,128)S(1)} %get-tuple-element.38), channel_id=1, source_target_pairs={{0,64},{64,128},{128,192},{192,0},{1,65},{65,129},{129,193},{193,1... | collective-permute-start | bytes 344072 | tf_op jit(solution)/shard_map/ppermute | solution.py:335
  14.8 6.5 %collective-permute-start.4 = (f32[16,1792]{1,0:T(8,128)S(1)}, f32[16,1792]{1,0:T(8,128)S(1)}, u32[]{:S(2)}, u32[]{:S(2)}) collective-permute-start(f32[16,1792]{1,0:T(8,128)S(1)} %get-tuple-element.37), channel_id=1, source_target_pairs={{0,128},{64,192},{128,0},{192,64},{1,129},{65,193},{129,1},{193,65... | collective-permute-start | bytes 344072 | tf_op jit(solution)/shard_map/ppermute | solution.py:335
  18.6 19.0 %collective-permute-start.11 = (bf16[64,1024]{1,0:T(8,128)(2,1)S(1)}, bf16[64,1024]{1,0:T(8,128)(2,1)S(1)}, u32[]{:S(2)}, u32[]{:S(2)}) collective-permute-start(bf16[64,1024]{1,0:T(8,128)(2,1)S(1)} %get-tuple-element.44), channel_id=1, source_target_pairs={{0,2},{2,4},{4,6},{6,0},{1,3},{3,5},{5,7},{7,1},{8,10},{10,12},{12... | collective-permute-start | bytes 393224 | tf_op jit(solution)/shard_map/ppermute | solution.py:335
  18.6 18.9 %collective-permute-start.12 = (bf16[64,1024]{1,0:T(8,128)(2,1)S(1)}, bf16[64,1024]{1,0:T(8,128)(2,1)S(1)}, u32[]{:S(2)}, u32[]{:S(2)}) collective-permute-start(bf16[64,1024]{1,0:T(8,128)(2,1)S(1)} %get-tuple-element.45), channel_id=1, source_target_pairs={{0,6},{2,0},{4,2},{6,4},{1,7},{3,1},{5,3},{7,5},{8,14},{10,8},{12,... | collective-permute-start | bytes 393224 | tf_op jit(solution)/shard_map/ppermute | solution.py:335
  25.3 9.2 %collective-permute-start.10 = (f32[8,1792]{1,0:T(8,128)S(1)}, f32[8,1792]{1,0:T(8,128)S(1)}, u32[]{:S(2)}, u32[]{:S(2)}) collective-permute-start(f32[8,1792]{1,0:T(8,128)S(1)} %shard_map.65.own_ref), channel_id=1, source_target_pairs={{0,32},{8,40},{16,48},{24,56},{32,0},{40,8},{48,16},{56,24},{1,33}... | collective-permute-start | bytes 172040 | tf_op jit(solution)/shard_map/ppermute | solution.py:335
  32.2 5.4 %collective-permute-start.8 = (f32[8,1792]{1,0:T(8,128)S(1)}, f32[8,1792]{1,0:T(8,128)S(1)}, u32[]{:S(2)}, u32[]{:S(2)}) collective-permute-start(f32[8,1792]{1,0:T(8,128)S(1)} %shard_map.65.own_ref), channel_id=1, source_target_pairs={{0,16},{8,24},{16,32},{24,40},{32,48},{40,56},{48,0},{56,8},{1,17}... | collective-permute-start | bytes 172040 | tf_op jit(solution)/shard_map/ppermute | solution.py:335
  39.1 6.5 %collective-permute-start.17 = (bf16[64,1024]{1,0:T(8,128)(2,1)S(1)}, bf16[64,1024]{1,0:T(8,128)(2,1)S(1)}, u32[]{:S(2)}, u32[]{:S(2)}) collective-permute-start(bf16[64,1024]{1,0:T(8,128)(2,1)S(1)} %get-tuple-element.46), channel_id=1, source_target_pairs={{0,4},{2,6},{4,0},{6,2},{1,5},{3,7},{5,1},{7,3},{8,12},{10,14},{12... | collective-permute-start | bytes 393224 | tf_op jit(solution)/shard_map/ppermute | solution.py:335
  41.9 5.2 %collective-permute-start.16 = (f32[16,1792]{1,0:T(8,128)S(1)}, f32[16,1792]{1,0:T(8,128)S(1)}, u32[]{:S(2)}, u32[]{:S(2)}) collective-permute-start(f32[16,1792]{1,0:T(8,128)S(1)} %shard_map.67.own_ref), channel_id=1, source_target_pairs={{0,128},{64,192},{128,0},{192,64},{1,129},{65,193},{129,1},{193,65... | collective-permute-start | bytes 344072 | tf_op jit(solution)/shard_map/ppermute | solution.py:335
  43.9 5.1 %collective-permute-start.15 = (f32[16,1792]{1,0:T(8,128)S(1)}, f32[16,1792]{1,0:T(8,128)S(1)}, u32[]{:S(2)}, u32[]{:S(2)}) collective-permute-start(f32[16,1792]{1,0:T(8,128)S(1)} %shard_map.67.own_ref), channel_id=1, source_target_pairs={{0,192},{64,0},{128,64},{192,128},{1,193},{65,1},{129,65},{193,129... | collective-permute-start | bytes 344072 | tf_op jit(solution)/shard_map/ppermute | solution.py:335
  45.2 4.9 %collective-permute-start.14 = (f32[16,1792]{1,0:T(8,128)S(1)}, f32[16,1792]{1,0:T(8,128)S(1)}, u32[]{:S(2)}, u32[]{:S(2)}) collective-permute-start(f32[16,1792]{1,0:T(8,128)S(1)} %shard_map.67.own_ref), channel_id=1, source_target_pairs={{0,64},{64,128},{128,192},{192,0},{1,65},{65,129},{129,193},{193,1... | collective-permute-start | bytes 344072 | tf_op jit(solution)/shard_map/ppermute | solution.py:335
  51.1 9.2 %collective-permute-start.18 = (f32[32,512]{1,0:T(8,128)S(1)}, f32[32,512]{1,0:T(8,128)S(1)}, u32[]{:S(2)}, u32[]{:S(2)}) collective-permute-start(f32[32,512]{1,0:T(8,128)S(1)} %get-tuple-element.48), channel_id=1, source_target_pairs={{0,1},{1,0},{2,3},{3,2},{4,5},{5,4},{6,7},{7,6},{8,9},{9,8},{10,11... | collective-permute-start | bytes 196616 | tf_op jit(solution)/shard_map/ppermute | solution.py:326
  60.3 4.7 %collective-permute-start.21 = (f32[32,512]{1,0:T(8,128)S(1)}, f32[32,512]{1,0:T(8,128)S(1)}, u32[]{:S(2)}, u32[]{:S(2)}) collective-permute-start(f32[32,512]{1,0:T(8,128)S(1)} %shard_map.69.own_ref), channel_id=1, source_target_pairs={{0,4},{2,6},{4,0},{6,2},{1,5},{3,7},{5,1},{7,3},{8,12},{10,14},{12... | collective-permute-start | bytes 196616 | tf_op jit(solution)/shard_map/ppermute | solution.py:335
  66.8 4.9 %collective-permute-start.22 = (f32[8,1024]{1,0:T(8,128)S(1)}, f32[8,1024]{1,0:T(8,128)S(1)}, u32[]{:S(2)}, u32[]{:S(2)}) collective-permute-start(f32[8,1024]{1,0:T(8,128)S(1)} %get-tuple-element.50), channel_id=1, source_target_pairs={{0,128},{64,192},{128,0},{192,64},{1,129},{65,193},{129,1},{193,65... | collective-permute-start | bytes 98312 | tf_op jit(solution)/shard_map/ppermute | solution.py:335
  74.7 6.7 %collective-permute-start.28 = (f32[8,1024]{1,0:T(8,128)S(1)}, f32[8,1024]{1,0:T(8,128)S(1)}, u32[]{:S(2)}, u32[]{:S(2)}) collective-permute-start(f32[8,1024]{1,0:T(8,128)S(1)} %shard_map.75.own_ref), channel_id=1, source_target_pairs={{0,32},{8,40},{16,48},{24,56},{32,0},{40,8},{48,16},{56,24},{1,33}... | collective-permute-start | bytes 98312 | tf_op jit(solution)/shard_map/ppermute | solution.py:335
  79.8 4.9 %collective-permute-start.26 = (f32[8,1024]{1,0:T(8,128)S(1)}, f32[8,1024]{1,0:T(8,128)S(1)}, u32[]{:S(2)}, u32[]{:S(2)}) collective-permute-start(f32[8,1024]{1,0:T(8,128)S(1)} %shard_map.75.own_ref), channel_id=1, source_target_pairs={{0,16},{8,24},{16,32},{24,40},{32,48},{40,56},{48,0},{56,8},{1,17}... | collective-permute-start | bytes 98312 | tf_op jit(solution)/shard_map/ppermute | solution.py:335
  84.7 10.6 %collective-permute-start.31 = (f32[8,1024]{1,0:T(8,128)S(1)}, f32[8,1024]{1,0:T(8,128)S(1)}, u32[]{:S(2)}, u32[]{:S(2)}) collective-permute-start(f32[8,1024]{1,0:T(8,128)S(1)} %shard_map.76.own_ref), channel_id=1, source_target_pairs={{0,128},{64,192},{128,0},{192,64},{1,129},{65,193},{129,1},{193,65... | collective-permute-start | bytes 98312 | tf_op jit(solution)/shard_map/ppermute | solution.py:335
  86.3 8.9 %collective-permute-start.30 = (f32[8,1024]{1,0:T(8,128)S(1)}, f32[8,1024]{1,0:T(8,128)S(1)}, u32[]{:S(2)}, u32[]{:S(2)}) collective-permute-start(f32[8,1024]{1,0:T(8,128)S(1)} %shard_map.76.own_ref), channel_id=1, source_target_pairs={{0,192},{64,0},{128,64},{192,128},{1,193},{65,1},{129,65},{193,129... | collective-permute-start | bytes 98312 | tf_op jit(solution)/shard_map/ppermute | solution.py:335
  88.3 6.9 %collective-permute-start.29 = (f32[8,1024]{1,0:T(8,128)S(1)}, f32[8,1024]{1,0:T(8,128)S(1)}, u32[]{:S(2)}, u32[]{:S(2)}) collective-permute-start(f32[8,1024]{1,0:T(8,128)S(1)} %shard_map.76.own_ref), channel_id=1, source_target_pairs={{0,64},{64,128},{128,192},{192,0},{1,65},{65,129},{129,193},{193,1... | collective-permute-start | bytes 98312 | tf_op jit(solution)/shard_map/ppermute | solution.py:335
  88.3 6.9 %collective-permute-start.32 = (f32[32,128]{1,0:T(8,128)S(1)}, f32[32,128]{1,0:T(8,128)S(1)}, u32[]{:S(2)}, u32[]{:S(2)}) collective-permute-start(f32[32,128]{1,0:T(8,128)S(1)} %get-tuple-element.54.after_ref.gram_ref), channel_id=1, source_target_pairs={{0,1},{1,0},{2,3},{3,2},{4,5},{5,4},{6,7},{7,6},{8,9},{9,8},{10,11... | collective-permute-start | bytes 49160 | tf_op jit(solution)/shard_map/ppermute | solution.py:326
  95.3 7.3 %collective-permute-start.35 = (f32[32,1152]{1,0:T(8,128)S(1)}, f32[32,1152]{1,0:T(8,128)S(1)}, u32[]{:S(2)}, u32[]{:S(2)}) collective-permute-start(f32[32,1152]{1,0:T(8,128)S(1)} %shard_map.77.own_ref.refs_0_), channel_id=1, source_target_pairs={{0,4},{2,6},{4,0},{6,2},{1,5},{3,7},{5,1},{7,3},{8,12},{10,14},{12... | collective-permute-start | bytes 442376 | tf_op jit(solution)/shard_map/ppermute | solution.py:335
  96.0 10.2 %collective-permute-start.34 = (f32[32,1152]{1,0:T(8,128)S(1)}, f32[32,1152]{1,0:T(8,128)S(1)}, u32[]{:S(2)}, u32[]{:S(2)}) collective-permute-start(f32[32,1152]{1,0:T(8,128)S(1)} %shard_map.77.own_ref.refs_0_), channel_id=1, source_target_pairs={{0,6},{2,0},{4,2},{6,4},{1,7},{3,1},{5,3},{7,5},{8,14},{10,8},{12,... | collective-permute-start | bytes 442376 | tf_op jit(solution)/shard_map/ppermute | solution.py:335
  96.8 9.8 %collective-permute-start.33 = (f32[32,1152]{1,0:T(8,128)S(1)}, f32[32,1152]{1,0:T(8,128)S(1)}, u32[]{:S(2)}, u32[]{:S(2)}) collective-permute-start(f32[32,1152]{1,0:T(8,128)S(1)} %shard_map.77.own_ref.refs_0_), channel_id=1, source_target_pairs={{0,2},{2,4},{4,6},{6,0},{1,3},{3,5},{5,7},{7,1},{8,10},{10,12},{12... | collective-permute-start | bytes 442376 | tf_op jit(solution)/shard_map/ppermute | solution.py:335
  97.5 11.1 %collective-permute-start.36 = (f32[32,1152]{1,0:T(8,128)S(1)}, f32[32,1152]{1,0:T(8,128)S(1)}, u32[]{:S(2)}, u32[]{:S(2)}) collective-permute-start(f32[32,1152]{1,0:T(8,128)S(1)} %shard_map.77.own_ref.refs_0_), channel_id=1, source_target_pairs={{0,1},{1,0},{2,3},{3,2},{4,5},{5,4},{6,7},{7,6},{8,9},{9,8},{10,11... | collective-permute-start | bytes 442376 | tf_op jit(solution)/shard_map/ppermute | solution.py:326
  102.6 6.0 %collective-permute-start.39 = (f32[32,1152]{1,0:T(8,128)S(1)}, f32[32,1152]{1,0:T(8,128)S(1)}, u32[]{:S(2)}, u32[]{:S(2)}) collective-permute-start(f32[32,1152]{1,0:T(8,128)S(1)} %collective-permute-done.35.c_ref.refs_3_), channel_id=1, source_target_pairs={{0,1},{1,0},{2,3},{3,2},{4,5},{5,4},{6,7},{7,6},{8,9},{9,8},{10,11... | collective-permute-start | bytes 442376 | tf_op jit(solution)/shard_map/ppermute | solution.py:326
  (17 other events, 63.0 us)
where the time goes:
time: 111 us
  starting transfers between devices  74 us (67%)
  waiting for transfers between devices  24.2 us (22%)
  Pallas kernels  10.8 us (10%)
    ppermute x30, starting transfers between devices, shift(): lax.ppermute(a, axis, [(i, (i + k * step) % size) for i in range(size)])  42 us
    ppermute x7, starting transfers between devices, swap(): return lax.ppermute(a, 'c', [(0, 1), (1, 0)])  28.2 us
    ppermute x30, waiting for transfers between devices, shift(): lax.ppermute(a, axis, [(i, (i + k * step) % size) for i in range(size)])  18.1 us
    pallas_call x21, Pallas kernels, call(): pl.pallas_call(kernel, out_shape=shapes if many else shapes[0], in_specs=...  10.8 us
    ppermute x3, waiting for transfers between devices, swap_z(): return lax.ppermute(a, 'z', [(i, i ^ 1) for i in range(NZ)])  3.9 us
    ppermute x3, starting transfers between devices, swap_z(): return lax.ppermute(a, 'z', [(i, i ^ 1) for i in range(NZ)])  3.86 us
  transfers between devices with their start and end apart: 40, of which 20 were waited for; matrix products, arithmetic and copies ran while one was open for 0% of the time, Pallas kernels for 6%

commit v1 on v0

--- a/solution.py
+++ b/solution.py
@@ -152,16 +152,17 @@
         ref[...] = whole_ref[rows_at(lax.rem(index + k, 4), size), :]
 
 
-def factor_kernel(qt_ref, q3_ref, own_ref, qt, sems):
+def factor_kernel(qt_ref, cot_ref, q3_ref, own_ref, cot_out_ref, qt, sems):
     at, cut = lax.axis_index("y") * NZ + lax.axis_index("z"), 1024
     pairs = [(qt_ref.at[:, i : i + cut], qt.at[:, i : i + cut]) for i in range(0, D, cut)]
-    pairs += [(qt_ref.at[:, rows_at(at, EB)], own_ref)]
+    pairs += [(qt_ref.at[:, rows_at(at, EB)], own_ref), (cot_ref, cot_out_ref)]
     copies = [pltpu.make_async_copy(a, b, sems.at[i]) for i, (a, b) in enumerate(pairs)]
     for copy in copies:
         copy.start()
     for i in range(D // cut):
         copies[i].wait()
         q3_ref[:, i * cut : (i + 1) * cut] = split3(qt[:, i * cut : (i + 1) * cut])
+    copies[-2].wait()
     copies[-1].wait()
 
 
@@ -191,12 +192,16 @@
         ref[...] = both_ref[:, rows_at(lax.rem(x + k, NX), CB)]
 
 
-def left_kernel(
-    got_ref, a_got_ref, b_got_ref, c_got_ref, hidden_ref, err_ref, q_ref,
-    own_ref, a_ref, b_ref, c_ref, slots_ref, whole_ref,
-):
-    for place, ref in in_order(lax.axis_index("x"), (got_ref, a_got_ref, b_got_ref, c_got_ref)):
-        slots_ref[place] = ref[...]
+def join_x_kernel(own_ref, other_ref, out_ref):
+    bit = lax.rem(lax.axis_index("x"), 2)
+    out_ref[bit] = own_ref[...]
+    out_ref[1 - bit] = other_ref[...]
+
+
+def left_kernel(pair_ref, far_ref, hidden_ref, err_ref, q_ref, own_ref, a_ref, b_ref, c_ref, slots_ref, whole_ref):
+    at = lax.axis_index("x") // 2
+    slots_ref[at] = pair_ref[...]
+    slots_ref[1 - at] = far_ref[...]
     packed = slots_ref[...].reshape(TOK // 2, 2 * RANK).T
     proj = jnp.concatenate([packed[:RANK], packed[RANK:]], axis=1)
     h = hidden_ref[...].reshape(NX * NC, 2, TB // 2, FB)
@@ -326,6 +331,10 @@
     return lax.ppermute(a, "c", [(0, 1), (1, 0)])
 
 
+def pair_x(a, partner):
+    return lax.ppermute(a, "x", [(x, partner(x)) for x in range(NX)])
+
+
 def swap_z(a):
     return lax.ppermute(a, "z", [(i, i ^ 1) for i in range(NZ)])
 
@@ -346,19 +355,21 @@
 def shards(hidden, cotangent, error_buf, q_start):
     qt = q_start.T
     dma, half = pltpu.SemaphoreType.DMA, RANK // 2
-    qt, hid, err = (pltpu.with_memory_space_constraint(a, pltpu.HBM) for a in (q_start.T, hidden, error_buf))
+    pinned = [pltpu.with_memory_space_constraint(a, pltpu.HBM) for a in (q_start.T, cotangent, hidden, error_buf)]
     other = swap(cotangent)
-    q3, q_own = call(
-        factor_kernel, [((3 * RANK, D), bf16), ((RANK, EB), f32)], qt, scratch=[pltpu.VMEM((RANK, D), f32), dma((5,))], hbm=(0,)
-    )
-    proj, both = call(project_kernel, [((TB, 2 * RANK), f32), ((2 * TB, D), bf16)], cotangent, other, q3)
+    q3, q_own, cot = call(
+        factor_kernel, [((3 * RANK, D), bf16), ((RANK, EB), f32), ((TB, D), bf16)], *pinned[:2],
+        scratch=[pltpu.VMEM((RANK, D), f32), dma((6,))], hbm=(0, 1),
+    )
+    proj, both = call(project_kernel, [((TB, 2 * RANK), f32), ((2 * TB, D), bf16)], cot, other, q3)
     hid, err = call(
-        fetch_kernel, [((TOK, FB), bf16), ((FB, EB), bf16)], hid, err, proj, scratch=[dma((2,))], hbm=(0, 1), unread=(2,)
-    )
+        fetch_kernel, [((TOK, FB), bf16), ((FB, EB), bf16)], *pinned[2:], proj, scratch=[dma((2,))], hbm=(0, 1), unread=(2,)
+    )
+    pair = call(join_x_kernel, ((2, TB, 2 * RANK), f32), proj, pair_x(proj, lambda x: x ^ 1))
     quarter, eighth = ((RANK // NY, FB), f32), ((RANK // NY // 2, FB), f32)
     parts = call(
-        left_kernel, [quarter] * 4, *share(proj, "x"), hid, err, q_own,
-        scratch=[pltpu.VMEM((4, TB, 2 * RANK), f32), pltpu.VMEM((RANK, FB), f32)],
+        left_kernel, [quarter] * 4, pair, pair_x(pair, lambda x: NX - 1 - x), hid, err, q_own,
+        scratch=[pltpu.VMEM((2, 2, TB, 2 * RANK), f32), pltpu.VMEM((RANK, FB), f32)],
     )
 
     parts = deal(parts, "y")

time: 111 us -> 111 us (level)
  waiting for transfers between devices: 24.2 us -> 29.6 us
  starting transfers between devices: 74 us -> 69.3 us
    ppermute x30 -> x27, starting transfers between devices: 42 us -> 36.7 us  [shift(): lax.ppermute(a, axis, [(i, (i + k * step) % size) for i in range(size)])]
    ppermute x0 -> x2, waiting for transfers between devices: none -> 4.49 us  [pair_x(): return lax.ppermute(a, 'x', [(x, partner(x)) for x in range(NX)])]
    ppermute x3, starting transfers between devices: 3.86 us -> 2.35 us  [swap_z(): return lax.ppermute(a, 'z', [(i, i ^ 1) for i in range(NZ)])]
    ppermute x3, waiting for transfers between devices: 3.9 us -> 5.21 us  [swap_z(): return lax.ppermute(a, 'z', [(i, i ^ 1) for i in range(NZ)])]
    ppermute x7, starting transfers between devices: 28.2 us -> 29.5 us  [swap(): return lax.ppermute(a, 'c', [(0, 1), (1, 0)])]
    ppermute x30 -> x27, waiting for transfers between devices: 18.1 us -> 17.7 us  [shift(): lax.ppermute(a, axis, [(i, (i + k * step) % size) for i in range(size)])]
    pallas_call x21 -> x22, Pallas kernels: 10.8 us -> 10.8 us  [call(): pl.pallas_call(kernel, out_shape=shapes if many else shapes[0], in_specs=...]
  transfers between devices with their start and end apart: 40 -> 39, of which waited for: 20 -> 21; matrix products, arithmetic and copies ran while one was open for 0% -> 0% of each run, Pallas kernels for 6% -> 6%
where the time goes in v1:
time: 111 us
  starting transfers between devices  69.3 us (62%)
  waiting for transfers between devices  29.6 us (27%)
  Pallas kernels  10.8 us (10%)
    ppermute x27, starting transfers between devices, shift(): lax.ppermute(a, axis, [(i, (i + k * step) % size) for i in range(size)])  36.7 us
    ppermute x7, starting transfers between devices, swap(): return lax.ppermute(a, 'c', [(0, 1), (1, 0)])  29.5 us
    ppermute x27, waiting for transfers between devices, shift(): lax.ppermute(a, axis, [(i, (i + k * step) % size) for i in range(size)])  17.7 us
    pallas_call x22, Pallas kernels, call(): pl.pallas_call(kernel, out_shape=shapes if many else shapes[0], in_specs=...  10.8 us
    ppermute x3, waiting for transfers between devices, swap_z(): return lax.ppermute(a, 'z', [(i, i ^ 1) for i in range(NZ)])  5.21 us
    ppermute x2, waiting for transfers between devices, pair_x(): return lax.ppermute(a, 'x', [(x, partner(x)) for x in range(NX)])  4.49 us
    ppermute x3, starting transfers between devices, swap_z(): return lax.ppermute(a, 'z', [(i, i ^ 1) for i in range(NZ)])  2.35 us
  transfers between devices with their start and end apart: 39, of which 21 were waited for; matrix products, arithmetic and copies ran while one was open for 0% of the time, Pallas kernels for 6%

profile of v1, /device:TPU:1, one launch (start us, length us, event | category | flops | bytes accessed | tf_op | source)
XLA Modules:
  0.0 110.7 jit_solution(5984918779497830390)
XLA Ops:
  0.6 3.3 %collective-permute-start = (bf16[32,4096]{1,0:T(8,128)(2,1)}, bf16[32,4096]{1,0:T(8,128)(2,1)S(1)}, u32[]{:S(2)}, u32[]{:S(2)}) collective-permute-start(bf16[32,4096]{1,0:T(8,128)(2,1)} %cot_ref.1), channel_id=1, source_target_pairs={{0,1},{1,0},{2,3},{3,2},{4,5},{5,4},{6,7},{7,6},{8,9},{9,8},{10,11... | collective-permute-start | bytes 786440 | tf_op jit(solution)/shard_map/ppermute | solution.py:331
  6.2 2.6 %collective-permute-done.1.other_ref = f32[32,128]{1,0:T(8,128)S(1)} collective-permute-done((f32[32,128]{1,0:T(8,128)S(1)}, f32[32,128]{1,0:T(8,128)S(1)}, u32[]{:S(2)}, u32[]{:S(2)}) %collective-permute-start.1) | collective-permute-done | bytes 16416 | tf_op jit(solution)/shard_map/ppermute | solution.py:335
  10.9 1.9 %collective-permute-done.2.far_ref = f32[2,32,128]{2,1,0:T(8,128)S(1)} collective-permute-done((f32[2,32,128]{2,1,0:T(8,128)S(1)}, f32[2,32,128]{2,1,0:T(8,128)S(1)}, u32[]{:S(2)}, u32[]{:S(2)}) %collective-permute-start.2) | collective-permute-done | bytes 32800 | tf_op jit(solution)/shard_map/ppermute | solution.py:335
  13.5 2.2 %collective-permute-start.3 = (f32[16,1792]{1,0:T(8,128)S(1)}, f32[16,1792]{1,0:T(8,128)S(1)}, u32[]{:S(2)}, u32[]{:S(2)}) collective-permute-start(f32[16,1792]{1,0:T(8,128)S(1)} %get-tuple-element.39), channel_id=1, source_target_pairs={{0,128},{64,192},{128,0},{192,64},{1,129},{65,193},{129,1},{193,65... | collective-permute-start | bytes 344072 | tf_op jit(solution)/shard_map/ppermute | solution.py:344
  16.7 2.8 %collective-permute-done.4.after_ref.b_ref = f32[16,1792]{1,0:T(8,128)S(1)} collective-permute-done((f32[16,1792]{1,0:T(8,128)S(1)}, f32[16,1792]{1,0:T(8,128)S(1)}, u32[]{:S(2)}, u32[]{:S(2)}) %collective-permute-start.4) | collective-permute-done | bytes 114720 | tf_op jit(solution)/shard_map/ppermute | solution.py:344
  19.7 2.7 %collective-permute-start.11 = (bf16[64,1024]{1,0:T(8,128)(2,1)S(1)}, bf16[64,1024]{1,0:T(8,128)(2,1)S(1)}, u32[]{:S(2)}, u32[]{:S(2)}) collective-permute-start(bf16[64,1024]{1,0:T(8,128)(2,1)S(1)} %get-tuple-element.47), channel_id=1, source_target_pairs={{0,6},{2,0},{4,2},{6,4},{1,7},{3,1},{5,3},{7,5},{8,14},{10,8},{12,... | collective-permute-start | bytes 393224 | tf_op jit(solution)/shard_map/ppermute | solution.py:344
  22.5 3.0 %collective-permute-done.6.b_ref = f32[8,1792]{1,0:T(8,128)S(1)} collective-permute-done((f32[8,1792]{1,0:T(8,128)S(1)}, f32[8,1792]{1,0:T(8,128)S(1)}, u32[]{:S(2)}, u32[]{:S(2)}) %collective-permute-start.6) | collective-permute-done | bytes 57376 | tf_op jit(solution)/shard_map/ppermute | solution.py:339
  25.6 4.6 %collective-permute-start.9 = (f32[8,1792]{1,0:T(8,128)S(1)}, f32[8,1792]{1,0:T(8,128)S(1)}, u32[]{:S(2)}, u32[]{:S(2)}) collective-permute-start(f32[8,1792]{1,0:T(8,128)S(1)} %shard_map.66.own_ref), channel_id=1, source_target_pairs={{0,32},{8,40},{16,48},{24,56},{32,0},{40,8},{48,16},{56,24},{1,33}... | collective-permute-start | bytes 172040 | tf_op jit(solution)/shard_map/ppermute | solution.py:344
  30.1 2.4 %collective-permute-start.7 = (f32[8,1792]{1,0:T(8,128)S(1)}, f32[8,1792]{1,0:T(8,128)S(1)}, u32[]{:S(2)}, u32[]{:S(2)}) collective-permute-start(f32[8,1792]{1,0:T(8,128)S(1)} %shard_map.66.own_ref), channel_id=1, source_target_pairs={{0,16},{8,24},{16,32},{24,40},{32,48},{40,56},{48,0},{56,8},{1,17}... | collective-permute-start | bytes 172040 | tf_op jit(solution)/shard_map/ppermute | solution.py:344
  32.6 2.1 %collective-permute-done.8.b_ref = f32[8,1792]{1,0:T(8,128)S(1)} collective-permute-done((f32[8,1792]{1,0:T(8,128)S(1)}, f32[8,1792]{1,0:T(8,128)S(1)}, u32[]{:S(2)}, u32[]{:S(2)}) %collective-permute-start.8) | collective-permute-done | bytes 57376 | tf_op jit(solution)/shard_map/ppermute | solution.py:344
  37.0 1.8 %collective-permute-start.16 = (bf16[64,1024]{1,0:T(8,128)(2,1)S(1)}, bf16[64,1024]{1,0:T(8,128)(2,1)S(1)}, u32[]{:S(2)}, u32[]{:S(2)}) collective-permute-start(bf16[64,1024]{1,0:T(8,128)(2,1)S(1)} %get-tuple-element.48), channel_id=1, source_target_pairs={{0,4},{2,6},{4,0},{6,2},{1,5},{3,7},{5,1},{7,3},{8,12},{10,14},{12... | collective-permute-start | bytes 393224 | tf_op jit(solution)/shard_map/ppermute | solution.py:344
  39.9 2.0 %collective-permute-start.15 = (f32[16,1792]{1,0:T(8,128)S(1)}, f32[16,1792]{1,0:T(8,128)S(1)}, u32[]{:S(2)}, u32[]{:S(2)}) collective-permute-start(f32[16,1792]{1,0:T(8,128)S(1)} %shard_map.68.own_ref), channel_id=1, source_target_pairs={{0,128},{64,192},{128,0},{192,64},{1,129},{65,193},{129,1},{193,65... | collective-permute-start | bytes 344072 | tf_op jit(solution)/shard_map/ppermute | solution.py:344
  43.4 1.7 %collective-permute-done.15.c_ref = f32[16,1792]{1,0:T(8,128)S(1)} collective-permute-done((f32[16,1792]{1,0:T(8,128)S(1)}, f32[16,1792]{1,0:T(8,128)S(1)}, u32[]{:S(2)}, u32[]{:S(2)}) %collective-permute-start.15) | collective-permute-done | bytes 114720 | tf_op jit(solution)/shard_map/ppermute | solution.py:344
  48.9 9.0 %collective-permute-start.17 = (f32[32,512]{1,0:T(8,128)S(1)}, f32[32,512]{1,0:T(8,128)S(1)}, u32[]{:S(2)}, u32[]{:S(2)}) collective-permute-start(f32[32,512]{1,0:T(8,128)S(1)} %get-tuple-element.50), channel_id=1, source_target_pairs={{0,1},{1,0},{2,3},{3,2},{4,5},{5,4},{6,7},{7,6},{8,9},{9,8},{10,11... | collective-permute-start | bytes 196616 | tf_op jit(solution)/shard_map/ppermute | solution.py:331
  66.6 2.3 %collective-permute-start.23 = (f32[8,1024]{1,0:T(8,128)S(1)}, f32[8,1024]{1,0:T(8,128)S(1)}, u32[]{:S(2)}, u32[]{:S(2)}) collective-permute-start(f32[8,1024]{1,0:T(8,128)S(1)} %get-tuple-element.54), channel_id=1, source_target_pairs={{0,192},{64,0},{128,64},{192,128},{1,193},{65,1},{129,65},{193,129... | collective-permute-start | bytes 98312 | tf_op jit(solution)/shard_map/ppermute | solution.py:344
  68.9 1.9 %shard_map.73.after_ref.inv_ref = f32[64,64]{1,0:T(8,128)S(1)} custom-call(f32[32,512]{1,0:T(8,128)S(1)} %shard_map.71.mixed_ref, f32[8,1024]{1,0:T(8,128)S(1)} %get-tuple-element.51.after_ref.own_ref), custom_call_target="tpu_custom_call" | custom-call | tf_op jit(solution)/shard_map/pallas_call | solution.py:121
  73.7 4.2 %collective-permute-start.27 = (f32[8,1024]{1,0:T(8,128)S(1)}, f32[8,1024]{1,0:T(8,128)S(1)}, u32[]{:S(2)}, u32[]{:S(2)}) collective-permute-start(f32[8,1024]{1,0:T(8,128)S(1)} %shard_map.76.own_ref), channel_id=1, source_target_pairs={{0,32},{8,40},{16,48},{24,56},{32,0},{40,8},{48,16},{56,24},{1,33}... | collective-permute-start | bytes 98312 | tf_op jit(solution)/shard_map/ppermute | solution.py:344
  81.6 2.3 %collective-permute-done.25.a_ref = f32[8,1024]{1,0:T(8,128)S(1)} collective-permute-done((f32[8,1024]{1,0:T(8,128)S(1)}, f32[8,1024]{1,0:T(8,128)S(1)}, u32[]{:S(2)}, u32[]{:S(2)}) %collective-permute-start.25) | collective-permute-done | bytes 32800 | tf_op jit(solution)/shard_map/ppermute | solution.py:344
  85.2 1.8 %collective-permute-start.29 = (f32[8,1024]{1,0:T(8,128)S(1)}, f32[8,1024]{1,0:T(8,128)S(1)}, u32[]{:S(2)}, u32[]{:S(2)}) collective-permute-start(f32[8,1024]{1,0:T(8,128)S(1)} %shard_map.77.own_ref), channel_id=1, source_target_pairs={{0,192},{64,0},{128,64},{192,128},{1,193},{65,1},{129,65},{193,129... | collective-permute-start | bytes 98312 | tf_op jit(solution)/shard_map/ppermute | solution.py:344
  87.0 7.0 %collective-permute-start.31 = (f32[32,128]{1,0:T(8,128)S(1)}, f32[32,128]{1,0:T(8,128)S(1)}, u32[]{:S(2)}, u32[]{:S(2)}) collective-permute-start(f32[32,128]{1,0:T(8,128)S(1)} %get-tuple-element.56.after_ref.gram_ref), channel_id=1, source_target_pairs={{0,1},{1,0},{2,3},{3,2},{4,5},{5,4},{6,7},{7,6},{8,9},{9,8},{10,11... | collective-permute-start | bytes 49160 | tf_op jit(solution)/shard_map/ppermute | solution.py:331
  97.6 5.0 %collective-permute-start.35 = (f32[32,1152]{1,0:T(8,128)S(1)}, f32[32,1152]{1,0:T(8,128)S(1)}, u32[]{:S(2)}, u32[]{:S(2)}) collective-permute-start(f32[32,1152]{1,0:T(8,128)S(1)} %shard_map.78.own_ref.refs_0_), channel_id=1, source_target_pairs={{0,1},{1,0},{2,3},{3,2},{4,5},{5,4},{6,7},{7,6},{8,9},{9,8},{10,11... | collective-permute-start | bytes 442376 | tf_op jit(solution)/shard_map/ppermute | solution.py:331
  102.7 3.3 %collective-permute-start.38 = (f32[32,1152]{1,0:T(8,128)S(1)}, f32[32,1152]{1,0:T(8,128)S(1)}, u32[]{:S(2)}, u32[]{:S(2)}) collective-permute-start(f32[32,1152]{1,0:T(8,128)S(1)} %collective-permute-done.34.c_ref.refs_3_), channel_id=1, source_target_pairs={{0,1},{1,0},{2,3},{3,2},{4,5},{5,4},{6,7},{7,6},{8,9},{9,8},{10,11... | collective-permute-start | bytes 442376 | tf_op jit(solution)/shard_map/ppermute | solution.py:331
  106.0 1.8 %collective-permute-start.36 = (f32[32,1152]{1,0:T(8,128)S(1)}, f32[32,1152]{1,0:T(8,128)S(1)}, u32[]{:S(2)}, u32[]{:S(2)}) collective-permute-start(f32[32,1152]{1,0:T(8,128)S(1)} %collective-permute-done.32.a_ref.refs_1_), channel_id=1, source_target_pairs={{0,1},{1,0},{2,3},{3,2},{4,5},{5,4},{6,7},{7,6},{8,9},{9,8},{10,11... | collective-permute-start | bytes 442376 | tf_op jit(solution)/shard_map/ppermute | solution.py:331
  108.8 1.7 %shard_map.80 = (f32[64,4096]{1,0:T(8,128)}, f32[64,1792]{1,0:T(8,128)}) custom-call(f32[32,1152]{1,0:T(8,128)S(1)} %shard_map.78.own_ref.refs_0_, f32[32,1152]{1,0:T(8,128)S(1)} %collective-permute-done.32.a_ref.refs_1_, f32[32,1152]{1,0:T(8,128)S(1)} %collective-permute-done.33.b_ref.refs_2_, f32[32,1152]{1,0:T(8,128)S(1)} %collective-permute-done.34.c_ref.refs_3_, ...), custom_call_target="tpu_custom_call" | custom-call | tf_op jit(solution)/shard_map/pallas_call | solution.py:121
  (76 shorter events, 36.3 us)
Async XLA Ops:
  13.4 6.2 %collective-permute-start.4 = (f32[16,1792]{1,0:T(8,128)S(1)}, f32[16,1792]{1,0:T(8,128)S(1)}, u32[]{:S(2)}, u32[]{:S(2)}) collective-permute-start(f32[16,1792]{1,0:T(8,128)S(1)} %get-tuple-element.40), channel_id=1, source_target_pairs={{0,64},{64,128},{128,192},{192,0},{1,65},{65,129},{129,193},{193,1... | collective-permute-start | bytes 344072 | tf_op jit(solution)/shard_map/ppermute | solution.py:344
  13.5 8.9 %collective-permute-start.3 = (f32[16,1792]{1,0:T(8,128)S(1)}, f32[16,1792]{1,0:T(8,128)S(1)}, u32[]{:S(2)}, u32[]{:S(2)}) collective-permute-start(f32[16,1792]{1,0:T(8,128)S(1)} %get-tuple-element.39), channel_id=1, source_target_pairs={{0,128},{64,192},{128,0},{192,64},{1,129},{65,193},{129,1},{193,65... | collective-permute-start | bytes 344072 | tf_op jit(solution)/shard_map/ppermute | solution.py:344
  15.7 6.7 %collective-permute-start.5 = (f32[16,1792]{1,0:T(8,128)S(1)}, f32[16,1792]{1,0:T(8,128)S(1)}, u32[]{:S(2)}, u32[]{:S(2)}) collective-permute-start(f32[16,1792]{1,0:T(8,128)S(1)} %get-tuple-element.41), channel_id=1, source_target_pairs={{0,192},{64,0},{128,64},{192,128},{1,193},{65,1},{129,65},{193,129... | collective-permute-start | bytes 344072 | tf_op jit(solution)/shard_map/ppermute | solution.py:344
  19.6 15.9 %collective-permute-start.10 = (bf16[64,1024]{1,0:T(8,128)(2,1)S(1)}, bf16[64,1024]{1,0:T(8,128)(2,1)S(1)}, u32[]{:S(2)}, u32[]{:S(2)}) collective-permute-start(bf16[64,1024]{1,0:T(8,128)(2,1)S(1)} %get-tuple-element.46), channel_id=1, source_target_pairs={{0,2},{2,4},{4,6},{6,0},{1,3},{3,5},{5,7},{7,1},{8,10},{10,12},{12... | collective-permute-start | bytes 393224 | tf_op jit(solution)/shard_map/ppermute | solution.py:344
  19.7 15.8 %collective-permute-start.11 = (bf16[64,1024]{1,0:T(8,128)(2,1)S(1)}, bf16[64,1024]{1,0:T(8,128)(2,1)S(1)}, u32[]{:S(2)}, u32[]{:S(2)}) collective-permute-start(bf16[64,1024]{1,0:T(8,128)(2,1)S(1)} %get-tuple-element.47), channel_id=1, source_target_pairs={{0,6},{2,0},{4,2},{6,4},{1,7},{3,1},{5,3},{7,5},{8,14},{10,8},{12,... | collective-permute-start | bytes 393224 | tf_op jit(solution)/shard_map/ppermute | solution.py:344
  25.6 7.0 %collective-permute-start.9 = (f32[8,1792]{1,0:T(8,128)S(1)}, f32[8,1792]{1,0:T(8,128)S(1)}, u32[]{:S(2)}, u32[]{:S(2)}) collective-permute-start(f32[8,1792]{1,0:T(8,128)S(1)} %shard_map.66.own_ref), channel_id=1, source_target_pairs={{0,32},{8,40},{16,48},{24,56},{32,0},{40,8},{48,16},{56,24},{1,33}... | collective-permute-start | bytes 172040 | tf_op jit(solution)/shard_map/ppermute | solution.py:344
  30.1 5.4 %collective-permute-start.7 = (f32[8,1792]{1,0:T(8,128)S(1)}, f32[8,1792]{1,0:T(8,128)S(1)}, u32[]{:S(2)}, u32[]{:S(2)}) collective-permute-start(f32[8,1792]{1,0:T(8,128)S(1)} %shard_map.66.own_ref), channel_id=1, source_target_pairs={{0,16},{8,24},{16,32},{24,40},{32,48},{40,56},{48,0},{56,8},{1,17}... | collective-permute-start | bytes 172040 | tf_op jit(solution)/shard_map/ppermute | solution.py:344
  37.0 6.4 %collective-permute-start.16 = (bf16[64,1024]{1,0:T(8,128)(2,1)S(1)}, bf16[64,1024]{1,0:T(8,128)(2,1)S(1)}, u32[]{:S(2)}, u32[]{:S(2)}) collective-permute-start(bf16[64,1024]{1,0:T(8,128)(2,1)S(1)} %get-tuple-element.48), channel_id=1, source_target_pairs={{0,4},{2,6},{4,0},{6,2},{1,5},{3,7},{5,1},{7,3},{8,12},{10,14},{12... | collective-permute-start | bytes 393224 | tf_op jit(solution)/shard_map/ppermute | solution.py:344
  39.9 5.2 %collective-permute-start.15 = (f32[16,1792]{1,0:T(8,128)S(1)}, f32[16,1792]{1,0:T(8,128)S(1)}, u32[]{:S(2)}, u32[]{:S(2)}) collective-permute-start(f32[16,1792]{1,0:T(8,128)S(1)} %shard_map.68.own_ref), channel_id=1, source_target_pairs={{0,128},{64,192},{128,0},{192,64},{1,129},{65,193},{129,1},{193,65... | collective-permute-start | bytes 344072 | tf_op jit(solution)/shard_map/ppermute | solution.py:344
  43.0 4.9 %collective-permute-start.13 = (f32[16,1792]{1,0:T(8,128)S(1)}, f32[16,1792]{1,0:T(8,128)S(1)}, u32[]{:S(2)}, u32[]{:S(2)}) collective-permute-start(f32[16,1792]{1,0:T(8,128)S(1)} %shard_map.68.own_ref), channel_id=1, source_target_pairs={{0,64},{64,128},{128,192},{192,0},{1,65},{65,129},{129,193},{193,1... | collective-permute-start | bytes 344072 | tf_op jit(solution)/shard_map/ppermute | solution.py:344
  48.9 9.9 %collective-permute-start.17 = (f32[32,512]{1,0:T(8,128)S(1)}, f32[32,512]{1,0:T(8,128)S(1)}, u32[]{:S(2)}, u32[]{:S(2)}) collective-permute-start(f32[32,512]{1,0:T(8,128)S(1)} %get-tuple-element.50), channel_id=1, source_target_pairs={{0,1},{1,0},{2,3},{3,2},{4,5},{5,4},{6,7},{7,6},{8,9},{9,8},{10,11... | collective-permute-start | bytes 196616 | tf_op jit(solution)/shard_map/ppermute | solution.py:331
  58.8 4.7 %collective-permute-start.20 = (f32[32,512]{1,0:T(8,128)S(1)}, f32[32,512]{1,0:T(8,128)S(1)}, u32[]{:S(2)}, u32[]{:S(2)}) collective-permute-start(f32[32,512]{1,0:T(8,128)S(1)} %shard_map.70.own_ref), channel_id=1, source_target_pairs={{0,4},{2,6},{4,0},{6,2},{1,5},{3,7},{5,1},{7,3},{8,12},{10,14},{12... | collective-permute-start | bytes 196616 | tf_op jit(solution)/shard_map/ppermute | solution.py:344
  66.1 4.7 %collective-permute-start.21 = (f32[8,1024]{1,0:T(8,128)S(1)}, f32[8,1024]{1,0:T(8,128)S(1)}, u32[]{:S(2)}, u32[]{:S(2)}) collective-permute-start(f32[8,1024]{1,0:T(8,128)S(1)} %get-tuple-element.52), channel_id=1, source_target_pairs={{0,128},{64,192},{128,0},{192,64},{1,129},{65,193},{129,1},{193,65... | collective-permute-start | bytes 98312 | tf_op jit(solution)/shard_map/ppermute | solution.py:344
  73.7 6.8 %collective-permute-start.27 = (f32[8,1024]{1,0:T(8,128)S(1)}, f32[8,1024]{1,0:T(8,128)S(1)}, u32[]{:S(2)}, u32[]{:S(2)}) collective-permute-start(f32[8,1024]{1,0:T(8,128)S(1)} %shard_map.76.own_ref), channel_id=1, source_target_pairs={{0,32},{8,40},{16,48},{24,56},{32,0},{40,8},{48,16},{56,24},{1,33}... | collective-permute-start | bytes 98312 | tf_op jit(solution)/shard_map/ppermute | solution.py:344
  79.0 4.9 %collective-permute-start.25 = (f32[8,1024]{1,0:T(8,128)S(1)}, f32[8,1024]{1,0:T(8,128)S(1)}, u32[]{:S(2)}, u32[]{:S(2)}) collective-permute-start(f32[8,1024]{1,0:T(8,128)S(1)} %shard_map.76.own_ref), channel_id=1, source_target_pairs={{0,16},{8,24},{16,32},{24,40},{32,48},{40,56},{48,0},{56,8},{1,17}... | collective-permute-start | bytes 98312 | tf_op jit(solution)/shard_map/ppermute | solution.py:344
  83.9 11.0 %collective-permute-start.30 = (f32[8,1024]{1,0:T(8,128)S(1)}, f32[8,1024]{1,0:T(8,128)S(1)}, u32[]{:S(2)}, u32[]{:S(2)}) collective-permute-start(f32[8,1024]{1,0:T(8,128)S(1)} %shard_map.77.own_ref), channel_id=1, source_target_pairs={{0,128},{64,192},{128,0},{192,64},{1,129},{65,193},{129,1},{193,65... | collective-permute-start | bytes 98312 | tf_op jit(solution)/shard_map/ppermute | solution.py:344
  85.2 9.7 %collective-permute-start.29 = (f32[8,1024]{1,0:T(8,128)S(1)}, f32[8,1024]{1,0:T(8,128)S(1)}, u32[]{:S(2)}, u32[]{:S(2)}) collective-permute-start(f32[8,1024]{1,0:T(8,128)S(1)} %shard_map.77.own_ref), channel_id=1, source_target_pairs={{0,192},{64,0},{128,64},{192,128},{1,193},{65,1},{129,65},{193,129... | collective-permute-start | bytes 98312 | tf_op jit(solution)/shard_map/ppermute | solution.py:344
  87.0 7.9 %collective-permute-start.28 = (f32[8,1024]{1,0:T(8,128)S(1)}, f32[8,1024]{1,0:T(8,128)S(1)}, u32[]{:S(2)}, u32[]{:S(2)}) collective-permute-start(f32[8,1024]{1,0:T(8,128)S(1)} %shard_map.77.own_ref), channel_id=1, source_target_pairs={{0,64},{64,128},{128,192},{192,0},{1,65},{65,129},{129,193},{193,1... | collective-permute-start | bytes 98312 | tf_op jit(solution)/shard_map/ppermute | solution.py:344
  87.0 7.9 %collective-permute-start.31 = (f32[32,128]{1,0:T(8,128)S(1)}, f32[32,128]{1,0:T(8,128)S(1)}, u32[]{:S(2)}, u32[]{:S(2)}) collective-permute-start(f32[32,128]{1,0:T(8,128)S(1)} %get-tuple-element.56.after_ref.gram_ref), channel_id=1, source_target_pairs={{0,1},{1,0},{2,3},{3,2},{4,5},{5,4},{6,7},{7,6},{8,9},{9,8},{10,11... | collective-permute-start | bytes 49160 | tf_op jit(solution)/shard_map/ppermute | solution.py:331
  95.0 7.7 %collective-permute-start.34 = (f32[32,1152]{1,0:T(8,128)S(1)}, f32[32,1152]{1,0:T(8,128)S(1)}, u32[]{:S(2)}, u32[]{:S(2)}) collective-permute-start(f32[32,1152]{1,0:T(8,128)S(1)} %shard_map.78.own_ref.refs_0_), channel_id=1, source_target_pairs={{0,4},{2,6},{4,0},{6,2},{1,5},{3,7},{5,1},{7,3},{8,12},{10,14},{12... | collective-permute-start | bytes 442376 | tf_op jit(solution)/shard_map/ppermute | solution.py:344
  96.2 9.8 %collective-permute-start.33 = (f32[32,1152]{1,0:T(8,128)S(1)}, f32[32,1152]{1,0:T(8,128)S(1)}, u32[]{:S(2)}, u32[]{:S(2)}) collective-permute-start(f32[32,1152]{1,0:T(8,128)S(1)} %shard_map.78.own_ref.refs_0_), channel_id=1, source_target_pairs={{0,6},{2,0},{4,2},{6,4},{1,7},{3,1},{5,3},{7,5},{8,14},{10,8},{12,... | collective-permute-start | bytes 442376 | tf_op jit(solution)/shard_map/ppermute | solution.py:344
  96.7 9.2 %collective-permute-start.32 = (f32[32,1152]{1,0:T(8,128)S(1)}, f32[32,1152]{1,0:T(8,128)S(1)}, u32[]{:S(2)}, u32[]{:S(2)}) collective-permute-start(f32[32,1152]{1,0:T(8,128)S(1)} %shard_map.78.own_ref.refs_0_), channel_id=1, source_target_pairs={{0,2},{2,4},{4,6},{6,0},{1,3},{3,5},{5,7},{7,1},{8,10},{10,12},{12... | collective-permute-start | bytes 442376 | tf_op jit(solution)/shard_map/ppermute | solution.py:344
  97.6 10.7 %collective-permute-start.35 = (f32[32,1152]{1,0:T(8,128)S(1)}, f32[32,1152]{1,0:T(8,128)S(1)}, u32[]{:S(2)}, u32[]{:S(2)}) collective-permute-start(f32[32,1152]{1,0:T(8,128)S(1)} %shard_map.78.own_ref.refs_0_), channel_id=1, source_target_pairs={{0,1},{1,0},{2,3},{3,2},{4,5},{5,4},{6,7},{7,6},{8,9},{9,8},{10,11... | collective-permute-start | bytes 442376 | tf_op jit(solution)/shard_map/ppermute | solution.py:331
  102.7 5.7 %collective-permute-start.38 = (f32[32,1152]{1,0:T(8,128)S(1)}, f32[32,1152]{1,0:T(8,128)S(1)}, u32[]{:S(2)}, u32[]{:S(2)}) collective-permute-start(f32[32,1152]{1,0:T(8,128)S(1)} %collective-permute-done.34.c_ref.refs_3_), channel_id=1, source_target_pairs={{0,1},{1,0},{2,3},{3,2},{4,5},{5,4},{6,7},{7,6},{8,9},{9,8},{10,11... | collective-permute-start | bytes 442376 | tf_op jit(solution)/shard_map/ppermute | solution.py:331
  (15 other events, 56.9 us)

commit v2 on v1

--- a/solution.py
+++ b/solution.py
@@ -229,8 +229,9 @@
     sum_z_kernel(own_ref, a_ref, b_ref, c_ref, *rest[-2:])
 
 
-def sum_x_kernel(own_ref, a_ref, b_ref, c_ref, out_ref, slots_ref):
+def sum_x_kernel(own_ref, a_ref, b_ref, c_ref, out_ref, gram_ref, slots_ref):
     out_ref[...] = sum_in_order(slots_ref, lax.axis_index("x"), (own_ref, a_ref, b_ref, c_ref))
+    gram_ref[...] = out_ref[3 * RANK :, :]
 
 
 def join_z_kernel(own_ref, other_ref, out_ref):
@@ -239,33 +240,32 @@
     out_ref[rows_at(1 - bit, half), :] = other_ref[...]
 
 
-def mixed_kernel(own_ref, a_ref, b_ref, c_ref, hidden_ref, err_ref, after_ref, p3_ref, keep_ref, send_ref, p_ref, all_ref):
+def mixed_kernel(own_ref, a_ref, b_ref, c_ref, hidden_ref, err_ref, after_ref, p3_ref, all_ref, p_ref):
     for place, ref in in_order(lax.axis_index("y"), (own_ref, a_ref, b_ref, c_ref)):
         p_ref[rows_at(place, RANK // NY), :] = ref[...]
     p3 = split3(p_ref[...])
     p3_ref[...] = p3
-    all_ref[:, :TOK] = dot3(p3, hidden_ref[...], NT)
-    all_ref[:, TOK:] = dot3(p3, err_ref[...], NN)
-    gram = pack(gram3(p3))
-    c, half = lax.axis_index("c"), RANK // 2
-    for ref, core in ((keep_ref, c), (send_ref, 1 - c)):
-        ref[:, : TOK + EB] = all_ref[rows_at(core, half), :]
-        ref[:, TOK + EB :] = gram
+    mixed = dot3(p3, hidden_ref[...], NT)
+    all_ref[:RANK, :] = mixed[:, :EB]
+    all_ref[RANK : 2 * RANK, :] = mixed[:, EB:]
+    all_ref[2 * RANK : 3 * RANK, :] = dot3(p3, err_ref[...], NN)
+    all_ref[3 * RANK :, :] = pack(gram3(p3))
 
 
 def right_kernel(mixed_ref, cot_ref, a_cot_ref, b_cot_ref, c_cot_ref, own_ref, a_ref, b_ref, c_ref, slots_ref, whole_ref):
     x, at = lax.axis_index("x"), lax.axis_index("y") * NZ + lax.axis_index("z")
     for place, ref in in_order(x, (cot_ref, a_cot_ref, b_cot_ref, c_cot_ref), DEALT):
         slots_ref[place] = ref[...]
-    part = dot3(split3(mixed_ref[:, :TOK]), slots_ref[...].reshape(TOK, CB), NN)
-    err_q = mixed_ref[:, TOK : TOK + EB]
+    mixed = jnp.concatenate([mixed_ref[:RANK, :], mixed_ref[RANK : 2 * RANK, :]], axis=1)
+    part = dot3(split3(mixed), slots_ref[...].reshape(TOK, CB), NN)
+    err_q = mixed_ref[2 * RANK : 3 * RANK, :]
     here = [jnp.where(at == x * (CB // EB) + i, err_q, 0.0) for i in range(CB // EB)]
     whole_ref[...] = part + jnp.concatenate(here, axis=1)
     scatter(whole_ref, lax.axis_index("y"), (own_ref, a_ref, b_ref, c_ref))
 
 
-def first_kernel(mixed_ref, after_ref, inv_ref):
-    inv_ref[...] = inverse_factor(unpack(mixed_ref[:, TOK + EB :]))
+def first_kernel(own_ref, other_ref, after_ref, inv_ref):
+    inv_ref[...] = inverse_factor(unpack(jnp.where(lax.axis_index("c") == 1, own_ref[...], other_ref[...])))
 
 
 def basis_kernel(inv_ref, p3_ref, b3_ref, gram_ref):
@@ -284,13 +284,16 @@
 
 def block_kernel(own_ref, a_ref, b_ref, c_ref, gram_ref, other_ref, out_ref):
     for place, ref in in_order(lax.axis_index("y"), (own_ref, a_ref, b_ref, c_ref)):
-        out_ref[rows_at(place, RANK // 2 // NY), :CB] = ref[...]
-    out_ref[:, CB:] = gram_ref[...] + other_ref[...]
-
-
-def second_kernel(own_ref, a_ref, b_ref, c_ref, inv_ref, total_ref, inverse_ref, slots_ref):
-    for place, ref in in_order(lax.axis_index("x"), (own_ref, a_ref, b_ref, c_ref)):
-        slots_ref[place] = ref[:, CB:]
+        out_ref[rows_at(place, RANK // NY), :CB] = ref[...]
+    out_ref[: RANK // 2, CB:] = gram_ref[...] + other_ref[...]
+    out_ref[RANK // 2 :, CB:] = jnp.zeros((RANK // 2, 2 * RANK), f32)
+
+
+def second_kernel(*refs):
+    inv_ref, total_ref, inverse_ref, slots_ref = refs[2 * NX :]
+    core = lax.axis_index("c") == 1
+    for k, (place, ref) in enumerate(in_order(lax.axis_index("x"), refs[:NX])):
+        slots_ref[place] = jnp.where(core, ref[: RANK // 2, CB:], refs[NX + k][: RANK // 2, CB:])
     gram = unpack((slots_ref[0] + slots_ref[1]) + (slots_ref[2] + slots_ref[3]))
     rows = lax.broadcasted_iota(jnp.int32, (RANK, RANK), 0)
     cols = lax.broadcasted_iota(jnp.int32, (RANK, RANK), 1)
@@ -310,12 +313,11 @@
 
 
 def new_kernel(*refs):
-    total_ref, inverse_ref, b3_ref, out_ref, basis_ref, s_ref, whole_ref, scaled_ref, sems = refs[2 * NX :]
-    x, c, half, total, copies = lax.axis_index("x"), lax.axis_index("c"), RANK // 2, total_ref[...], []
+    total_ref, inverse_ref, b3_ref, out_ref, basis_ref, whole_ref, scaled_ref, sems = refs[2 * NX :]
+    x, core, total, copies = lax.axis_index("x"), lax.axis_index("c") == 1, total_ref[...], []
     for k, (place, ref) in enumerate(in_order(x, refs[:NX])):
-        s_ref[k, rows_at(c, half), :] = ref[:, :CB]
-        s_ref[k, rows_at(1 - c, half), :] = refs[NX + k][:, :CB]
-        whole_ref[k] = dot6(total, split3(s_ref[k]))
+        block = jnp.where(core, ref[:, :CB], refs[NX + k][:, :CB])
+        whole_ref[k] = dot6(total, split3(block))
         cols = rows_at(place, CB)
         copies.append(pltpu.make_async_copy(whole_ref.at[k], out_ref.at[:, cols], sems.at[k]))
         copies[-1].start()
@@ -335,6 +337,28 @@
     return lax.ppermute(a, "x", [(x, partner(x)) for x in range(NX)])
 
 
+def lead(a, step, idle):
+    places = [(y, z, x) for y in range(NY) for z in range(NZ) for x in range(NX)]
+    number = {place: i * NC for i, place in enumerate(places)}
+    pairs = [(number[p] + c, number[move(*p)] + c) for p in places for c, move in ((0, idle), (1, step))]
+    return lax.ppermute(a, ("y", "z", "x", "c"), pairs)
+
+
+def lead_shift(a, axis, k):
+    hop = 1 if k == 3 else -1
+    if axis == "x":
+        return lead(a, lambda y, z, x: (y, z, (x + k) % NX), lambda y, z, x: ((y + hop) % NY, z, x))
+
+    def step(y, z, x):
+        return ((y + k) % NY, z, x) if axis == "y" else (y, (z + 2 * k) % NZ, x)
+
+    return lead(a, step, lambda y, z, x: (y, z, (x + hop) % NX))
+
+
+def lead_swap_z(a):
+    return lead(a, lambda y, z, x: (y, z ^ 1, x), lambda y, z, x: (y, z, x ^ 1))
+
+
 def swap_z(a):
     return lax.ppermute(a, "z", [(i, i ^ 1) for i in range(NZ)])
 
@@ -344,11 +368,11 @@
     return lax.ppermute(a, axis, [(i, (i + k * step) % size) for i in range(size)])
 
 
-def deal(blocks, axis):
+def deal(blocks, axis, shift=shift):
     return [blocks[0]] + [shift(block, axis, k) for k, block in zip(DEALT[1:], blocks[1:], strict=True)]
 
 
-def share(block, axis):
+def share(block, axis, shift=shift):
     return [block] + [shift(block, axis, k) for k in (1, 3, 2)]
 
 
@@ -384,31 +408,30 @@
     )
     p = call(join_z_kernel, quarter, p, swap_z(p))
 
-    halves = ((half, TOK + EB + 2 * RANK), f32)
-    p3, keep, send = call(
-        mixed_kernel, [((3 * RANK, FB), bf16), halves, halves], *share(p, "y"), hid, err, cot[1],
-        scratch=[pltpu.VMEM((RANK, FB), f32), pltpu.VMEM((RANK, TOK + EB), f32)], unread=(6,),
-    )
-    mixed = call(add_kernel, halves, keep, swap(send))
-    mixed = call(sum_x_kernel, halves, *share(mixed, "x"), scratch=[pltpu.VMEM((4, *halves[0]), f32)])
-
-    piece = ((half // NY, CB), f32)
+    mix, small = ((3 * RANK + half, EB), f32), ((half, 2 * RANK), f32)
+    p3, mixed = call(
+        mixed_kernel, [((3 * RANK, FB), bf16), mix], *share(p, "y"), hid, err, cot[1], scratch=[pltpu.VMEM((RANK, FB), f32)], unread=(6,)
+    )
+    mixed = call(add_kernel, mix, mixed, swap(mixed))
+    mixed, gram = call(sum_x_kernel, [mix, small], *share(mixed, "x", lead_shift), scratch=[pltpu.VMEM((4, *mix[0]), f32)])
+
+    piece, slots = ((RANK // NY, CB), f32), pltpu.VMEM((4, RANK // NY, CB), f32)
     parts = call(
-        right_kernel, [piece] * 4, mixed, *cot, scratch=[pltpu.VMEM((4, 2 * TB, CB), bf16), pltpu.VMEM((half, CB), f32)]
-    )
-    inverse = call(first_kernel, ((RANK, RANK), f32), mixed, parts[0], unread=(1,))
-    s = call(sum_y_kernel, piece, *deal(parts, "y"), inverse, scratch=[pltpu.VMEM((4, *piece[0]), f32)], unread=(4,))
-    b3, gram = call(basis_kernel, [((3 * RANK, FB), bf16), ((half, 2 * RANK), f32)], inverse, p3)
-    s = call(add_after_kernel, piece, s, swap_z(s), gram, unread=(2,))
-    s = call(sum_z_kernel, piece, *share(s, "z"), scratch=[pltpu.VMEM((4, *piece[0]), f32)])
-    s = call(block_kernel, ((half, CB + 2 * RANK), f32), *share(s, "y"), gram, swap(gram))
-    blocks = share(s, "x")
+        right_kernel, [piece] * 4, mixed, *cot, scratch=[pltpu.VMEM((4, 2 * TB, CB), bf16), pltpu.VMEM((RANK, CB), f32)]
+    )
+    inverse = call(first_kernel, ((RANK, RANK), f32), gram, swap(gram), parts[0], unread=(2,))
+    s = call(sum_y_kernel, piece, *deal(parts, "y", lead_shift), inverse, scratch=[slots], unread=(4,))
+    b3, gram = call(basis_kernel, [((3 * RANK, FB), bf16), small], inverse, p3)
+    s = call(add_after_kernel, piece, s, lead_swap_z(s), gram, unread=(2,))
+    s = call(sum_z_kernel, piece, *share(s, "z", lead_shift), scratch=[slots])
+    s = call(block_kernel, ((RANK, CB + 2 * RANK), f32), *share(s, "y", lead_shift), gram, swap(gram))
+    blocks = share(s, "x", lead_shift)
+    blocks += [swap(b) for b in blocks]
     square = ((RANK, RANK), f32)
-    total, second = call(second_kernel, [square, square], *blocks, inverse, scratch=[pltpu.VMEM((4, half, 2 * RANK), f32)])
-    wide_block = pltpu.VMEM((NX, RANK, CB), f32)
+    total, second = call(second_kernel, [square, square], *blocks, inverse, scratch=[pltpu.VMEM((4, *small[0]), f32)])
     q_new, scaled = call(
-        new_kernel, [((RANK, D), f32), ((RANK, FB), f32)], *blocks, *[swap(b) for b in blocks], total, second, b3,
-        scratch=[wide_block, wide_block, pltpu.VMEM((RANK, FB), f32), dma((NX + 1,))], out_hbm=True,
+        new_kernel, [((RANK, D), f32), ((RANK, FB), f32)], *blocks, total, second, b3,
+        scratch=[pltpu.VMEM((NX, RANK, CB), f32), pltpu.VMEM((RANK, FB), f32), dma((NX + 1,))], out_hbm=True,
     )
     return scaled.T, q_new.T
 

time: 111 us -> 110 us (level)
  starting transfers between devices: 69.3 us -> 58.3 us
  waiting for transfers between devices: 29.6 us -> 39.2 us
    ppermute x27 -> x12, starting transfers between devices: 36.7 us -> 18.3 us  [shift(): lax.ppermute(a, axis, [(i, (i + k * step) % size) for i in range(size)])]
    ppermute x0 -> x16, starting transfers between devices: none -> 18.2 us  [lead(): return lax.ppermute(a, ('y', 'z', 'x', 'c'), pairs)]
    ppermute x0 -> x16, waiting for transfers between devices: none -> 16 us  [lead(): return lax.ppermute(a, ('y', 'z', 'x', 'c'), pairs)]
    ppermute x7 -> x8, starting transfers between devices: 29.5 us -> 19.5 us  [swap(): return lax.ppermute(a, 'c', [(0, 1), (1, 0)])]
    ppermute x27 -> x12, waiting for transfers between devices: 17.7 us -> 10.3 us  [shift(): lax.ppermute(a, axis, [(i, (i + k * step) % size) for i in range(size)])]
    ppermute x7 -> x8, waiting for transfers between devices: 2.14 us -> 4.25 us  [swap(): return lax.ppermute(a, 'c', [(0, 1), (1, 0)])]
    ppermute x3 -> x2, waiting for transfers between devices: 5.21 us -> 4.1 us  [swap_z(): return lax.ppermute(a, 'z', [(i, i ^ 1) for i in range(NZ)])]
    ppermute x3 -> x2, starting transfers between devices: 2.35 us -> 1.52 us  [swap_z(): return lax.ppermute(a, 'z', [(i, i ^ 1) for i in range(NZ)])]
  transfers between devices with their start and end apart: 39 -> 40, of which waited for: 21 -> 28; matrix products, arithmetic and copies ran while one was open for 0% -> 0% of each run, Pallas kernels for 6% -> 5%
where the time goes in v2:
time: 110 us; the launch traced here: 109 us
  starting transfers between devices  58.3 us (53%)
  waiting for transfers between devices  39.2 us (36%)
  Pallas kernels  10.9 us (10%)
    ppermute x8, starting transfers between devices, swap(): return lax.ppermute(a, 'c', [(0, 1), (1, 0)])  19.5 us
    ppermute x12, starting transfers between devices, shift(): lax.ppermute(a, axis, [(i, (i + k * step) % size) for i in range(size)])  18.3 us
    ppermute x16, starting transfers between devices, lead(): return lax.ppermute(a, ('y', 'z', 'x', 'c'), pairs)  18.2 us
    ppermute x16, waiting for transfers between devices, lead(): return lax.ppermute(a, ('y', 'z', 'x', 'c'), pairs)  16 us
    pallas_call x22, Pallas kernels, call(): pl.pallas_call(kernel, out_shape=shapes if many else shapes[0], in_specs=...  10.9 us
    ppermute x12, waiting for transfers between devices, shift(): lax.ppermute(a, axis, [(i, (i + k * step) % size) for i in range(size)])  10.3 us
    ppermute x2, waiting for transfers between devices, pair_x(): return lax.ppermute(a, 'x', [(x, partner(x)) for x in range(NX)])  4.49 us
    ppermute x8, waiting for transfers between devices, swap(): return lax.ppermute(a, 'c', [(0, 1), (1, 0)])  4.25 us
  transfers between devices with their start and end apart: 40, of which 28 were waited for; matrix products, arithmetic and copies ran while one was open for 0% of the time, Pallas kernels for 5%

profile of v2, /device:TPU:1, one launch (start us, length us, event | category | flops | bytes accessed | tf_op | source)
XLA Modules:
  0.0 109.4 jit_solution(11447319619008453348)
XLA Ops:
  0.6 3.3 %collective-permute-start = (bf16[32,4096]{1,0:T(8,128)(2,1)}, bf16[32,4096]{1,0:T(8,128)(2,1)S(1)}, u32[]{:S(2)}, u32[]{:S(2)}) collective-permute-start(bf16[32,4096]{1,0:T(8,128)(2,1)} %cot_ref.1), channel_id=1, source_target_pairs={{0,1},{1,0},{2,3},{3,2},{4,5},{5,4},{6,7},{7,6},{8,9},{9,8},{10,11... | collective-permute-start | bytes 786440 | tf_op jit(solution)/shard_map/ppermute | solution.py:333
  6.2 2.6 %collective-permute-done.1.other_ref = f32[32,128]{1,0:T(8,128)S(1)} collective-permute-done((f32[32,128]{1,0:T(8,128)S(1)}, f32[32,128]{1,0:T(8,128)S(1)}, u32[]{:S(2)}, u32[]{:S(2)}) %collective-permute-start.1) | collective-permute-done | bytes 16416 | tf_op jit(solution)/shard_map/ppermute | solution.py:337
  10.9 1.9 %collective-permute-done.2.far_ref = f32[2,32,128]{2,1,0:T(8,128)S(1)} collective-permute-done((f32[2,32,128]{2,1,0:T(8,128)S(1)}, f32[2,32,128]{2,1,0:T(8,128)S(1)}, u32[]{:S(2)}, u32[]{:S(2)}) %collective-permute-start.2) | collective-permute-done | bytes 32800 | tf_op jit(solution)/shard_map/ppermute | solution.py:337
  13.5 2.2 %collective-permute-start.3 = (f32[16,1792]{1,0:T(8,128)S(1)}, f32[16,1792]{1,0:T(8,128)S(1)}, u32[]{:S(2)}, u32[]{:S(2)}) collective-permute-start(f32[16,1792]{1,0:T(8,128)S(1)} %get-tuple-element.40), channel_id=1, source_target_pairs={{0,128},{64,192},{128,0},{192,64},{1,129},{65,193},{129,1},{193,65... | collective-permute-start | bytes 344072 | tf_op jit(solution)/shard_map/ppermute | solution.py:368
  16.7 2.8 %collective-permute-done.4.after_ref.b_ref = f32[16,1792]{1,0:T(8,128)S(1)} collective-permute-done((f32[16,1792]{1,0:T(8,128)S(1)}, f32[16,1792]{1,0:T(8,128)S(1)}, u32[]{:S(2)}, u32[]{:S(2)}) %collective-permute-start.4) | collective-permute-done | bytes 114720 | tf_op jit(solution)/shard_map/ppermute | solution.py:368
  19.7 2.7 %collective-permute-start.11 = (bf16[64,1024]{1,0:T(8,128)(2,1)S(1)}, bf16[64,1024]{1,0:T(8,128)(2,1)S(1)}, u32[]{:S(2)}, u32[]{:S(2)}) collective-permute-start(bf16[64,1024]{1,0:T(8,128)(2,1)S(1)} %get-tuple-element.48), channel_id=1, source_target_pairs={{0,6},{2,0},{4,2},{6,4},{1,7},{3,1},{5,3},{7,5},{8,14},{10,8},{12,... | collective-permute-start | bytes 393224 | tf_op jit(solution)/shard_map/ppermute | solution.py:368
  22.5 3.0 %collective-permute-done.6.b_ref = f32[8,1792]{1,0:T(8,128)S(1)} collective-permute-done((f32[8,1792]{1,0:T(8,128)S(1)}, f32[8,1792]{1,0:T(8,128)S(1)}, u32[]{:S(2)}, u32[]{:S(2)}) %collective-permute-start.6) | collective-permute-done | bytes 57376 | tf_op jit(solution)/shard_map/ppermute | solution.py:363
  25.6 4.6 %collective-permute-start.9 = (f32[8,1792]{1,0:T(8,128)S(1)}, f32[8,1792]{1,0:T(8,128)S(1)}, u32[]{:S(2)}, u32[]{:S(2)}) collective-permute-start(f32[8,1792]{1,0:T(8,128)S(1)} %shard_map.66.own_ref), channel_id=1, source_target_pairs={{0,32},{8,40},{16,48},{24,56},{32,0},{40,8},{48,16},{56,24},{1,33}... | collective-permute-start | bytes 172040 | tf_op jit(solution)/shard_map/ppermute | solution.py:368
  30.1 2.4 %collective-permute-start.7 = (f32[8,1792]{1,0:T(8,128)S(1)}, f32[8,1792]{1,0:T(8,128)S(1)}, u32[]{:S(2)}, u32[]{:S(2)}) collective-permute-start(f32[8,1792]{1,0:T(8,128)S(1)} %shard_map.66.own_ref), channel_id=1, source_target_pairs={{0,16},{8,24},{16,32},{24,40},{32,48},{40,56},{48,0},{56,8},{1,17}... | collective-permute-start | bytes 172040 | tf_op jit(solution)/shard_map/ppermute | solution.py:368
  32.6 2.1 %collective-permute-done.8.b_ref = f32[8,1792]{1,0:T(8,128)S(1)} collective-permute-done((f32[8,1792]{1,0:T(8,128)S(1)}, f32[8,1792]{1,0:T(8,128)S(1)}, u32[]{:S(2)}, u32[]{:S(2)}) %collective-permute-start.8) | collective-permute-done | bytes 57376 | tf_op jit(solution)/shard_map/ppermute | solution.py:368
  37.0 1.8 %collective-permute-start.16 = (bf16[64,1024]{1,0:T(8,128)(2,1)S(1)}, bf16[64,1024]{1,0:T(8,128)(2,1)S(1)}, u32[]{:S(2)}, u32[]{:S(2)}) collective-permute-start(bf16[64,1024]{1,0:T(8,128)(2,1)S(1)} %get-tuple-element.49), channel_id=1, source_target_pairs={{0,4},{2,6},{4,0},{6,2},{1,5},{3,7},{5,1},{7,3},{8,12},{10,14},{12... | collective-permute-start | bytes 393224 | tf_op jit(solution)/shard_map/ppermute | solution.py:368
  39.9 2.0 %collective-permute-start.15 = (f32[16,1792]{1,0:T(8,128)S(1)}, f32[16,1792]{1,0:T(8,128)S(1)}, u32[]{:S(2)}, u32[]{:S(2)}) collective-permute-start(f32[16,1792]{1,0:T(8,128)S(1)} %shard_map.68.own_ref), channel_id=1, source_target_pairs={{0,128},{64,192},{128,0},{192,64},{1,129},{65,193},{129,1},{193,65... | collective-permute-start | bytes 344072 | tf_op jit(solution)/shard_map/ppermute | solution.py:368
  48.9 9.0 %collective-permute-start.17 = (f32[224,128]{1,0:T(8,128)S(1)}, f32[224,128]{1,0:T(8,128)S(1)}, u32[]{:S(2)}, u32[]{:S(2)}) collective-permute-start(f32[224,128]{1,0:T(8,128)S(1)} %get-tuple-element.50.a_ref), channel_id=1, source_target_pairs={{0,1},{1,0},{2,3},{3,2},{4,5},{5,4},{6,7},{7,6},{8,9},{9,8},{10,11... | collective-permute-start | bytes 344072 | tf_op jit(solution)/shard_map/ppermute | solution.py:333
  62.0 2.1 %collective-permute-done.20.c_ref = f32[224,128]{1,0:T(8,128)S(1)} collective-permute-done((f32[224,128]{1,0:T(8,128)S(1)}, f32[224,128]{1,0:T(8,128)S(1)}, u32[]{:S(2)}, u32[]{:S(2)}) %collective-permute-start.20) | collective-permute-done | bytes 114720 | tf_op jit(solution)/shard_map/ppermute | solution.py:344
  67.2 2.3 %collective-permute-start.23 = (f32[16,1024]{1,0:T(8,128)S(1)}, f32[16,1024]{1,0:T(8,128)S(1)}, u32[]{:S(2)}, u32[]{:S(2)}) collective-permute-start(f32[16,1024]{1,0:T(8,128)S(1)} %get-tuple-element.55), channel_id=1, source_target_pairs={{0,2},{1,193},{2,4},{3,195},{4,6},{5,197},{6,0},{7,199},{8,10},{9,... | collective-permute-start | bytes 196616 | tf_op jit(solution)/shard_map/ppermute | solution.py:344
  69.6 1.8 %collective-permute-start.24 = (f32[32,128]{1,0:T(8,128)S(1)}, f32[32,128]{1,0:T(8,128)S(1)}, u32[]{:S(2)}, u32[]{:S(2)}) collective-permute-start(f32[32,128]{1,0:T(8,128)S(1)} %get-tuple-element.56.own_ref), channel_id=1, source_target_pairs={{0,1},{1,0},{2,3},{3,2},{4,5},{5,4},{6,7},{7,6},{8,9},{9,8},{10,11... | collective-permute-start | bytes 49160 | tf_op jit(solution)/shard_map/ppermute | solution.py:333
  72.2 1.9 %shard_map.73.after_ref.inv_ref.refs_8_ = f32[64,64]{1,0:T(8,128)S(1)} custom-call(f32[32,128]{1,0:T(8,128)S(1)} %get-tuple-element.56.own_ref, f32[32,128]{1,0:T(8,128)S(1)} %collective-permute-done.24.other_ref, f32[16,1024]{1,0:T(8,128)S(1)} %get-tuple-element.52.after_ref.own_ref), custom_call_target="tpu_custom_call" | custom-call | tf_op jit(solution)/shard_map/pallas_call | solution.py:121
  75.2 2.1 %collective-permute-done.25.b_ref = f32[16,1024]{1,0:T(8,128)S(1)} collective-permute-done((f32[16,1024]{1,0:T(8,128)S(1)}, f32[16,1024]{1,0:T(8,128)S(1)}, u32[]{:S(2)}, u32[]{:S(2)}) %collective-permute-start.25) | collective-permute-done | bytes 65568 | tf_op jit(solution)/shard_map/ppermute | solution.py:344
  77.3 4.2 %collective-permute-start.28 = (f32[16,1024]{1,0:T(8,128)S(1)}, f32[16,1024]{1,0:T(8,128)S(1)}, u32[]{:S(2)}, u32[]{:S(2)}) collective-permute-start(f32[16,1024]{1,0:T(8,128)S(1)} %shard_map.76.own_ref), channel_id=1, source_target_pairs={{0,6},{1,33},{2,0},{3,35},{4,2},{5,37},{6,4},{7,39},{8,14},{9,41},... | collective-permute-start | bytes 196616 | tf_op jit(solution)/shard_map/ppermute | solution.py:344
  88.6 2.1 %collective-permute-start.30 = (f32[16,1024]{1,0:T(8,128)S(1)}, f32[16,1024]{1,0:T(8,128)S(1)}, u32[]{:S(2)}, u32[]{:S(2)}) collective-permute-start(f32[16,1024]{1,0:T(8,128)S(1)} %shard_map.77.own_ref), channel_id=1, source_target_pairs={{0,2},{1,193},{2,4},{3,195},{4,6},{5,197},{6,0},{7,199},{8,10},{9,... | collective-permute-start | bytes 196616 | tf_op jit(solution)/shard_map/ppermute | solution.py:344
  95.1 2.1 %collective-permute-start.34 = (f32[64,1152]{1,0:T(8,128)S(1)}, f32[64,1152]{1,0:T(8,128)S(1)}, u32[]{:S(2)}, u32[]{:S(2)}) collective-permute-start(f32[64,1152]{1,0:T(8,128)S(1)} %shard_map.78.refs_0_), channel_id=1, source_target_pairs={{0,64},{1,7},{2,66},{3,1},{4,68},{5,3},{6,70},{7,5},{8,72},{9,15},... | collective-permute-start | bytes 884744 | tf_op jit(solution)/shard_map/ppermute | solution.py:344
  97.2 3.2 %collective-permute-start.36 = (f32[64,1152]{1,0:T(8,128)S(1)}, f32[64,1152]{1,0:T(8,128)S(1)}, u32[]{:S(2)}, u32[]{:S(2)}) collective-permute-start(f32[64,1152]{1,0:T(8,128)S(1)} %shard_map.78.refs_0_), channel_id=1, source_target_pairs={{0,1},{1,0},{2,3},{3,2},{4,5},{5,4},{6,7},{7,6},{8,9},{9,8},{10,11... | collective-permute-start | bytes 884744 | tf_op jit(solution)/shard_map/ppermute | solution.py:333
  100.5 1.8 %collective-permute-done.35.refs_3_ = f32[64,1152]{1,0:T(8,128)S(1)} collective-permute-done((f32[64,1152]{1,0:T(8,128)S(1)}, f32[64,1152]{1,0:T(8,128)S(1)}, u32[]{:S(2)}, u32[]{:S(2)}) %collective-permute-start.35) | collective-permute-done | bytes 294944 | tf_op jit(solution)/shard_map/ppermute | solution.py:344
  102.3 2.0 %collective-permute-done.34.refs_2_ = f32[64,1152]{1,0:T(8,128)S(1)} collective-permute-done((f32[64,1152]{1,0:T(8,128)S(1)}, f32[64,1152]{1,0:T(8,128)S(1)}, u32[]{:S(2)}, u32[]{:S(2)}) %collective-permute-start.34) | collective-permute-done | bytes 294944 | tf_op jit(solution)/shard_map/ppermute | solution.py:344
  (78 shorter events, 42.4 us)
Async XLA Ops:
  13.4 6.2 %collective-permute-start.4 = (f32[16,1792]{1,0:T(8,128)S(1)}, f32[16,1792]{1,0:T(8,128)S(1)}, u32[]{:S(2)}, u32[]{:S(2)}) collective-permute-start(f32[16,1792]{1,0:T(8,128)S(1)} %get-tuple-element.41), channel_id=1, source_target_pairs={{0,64},{64,128},{128,192},{192,0},{1,65},{65,129},{129,193},{193,1... | collective-permute-start | bytes 344072 | tf_op jit(solution)/shard_map/ppermute | solution.py:368
  13.5 8.9 %collective-permute-start.3 = (f32[16,1792]{1,0:T(8,128)S(1)}, f32[16,1792]{1,0:T(8,128)S(1)}, u32[]{:S(2)}, u32[]{:S(2)}) collective-permute-start(f32[16,1792]{1,0:T(8,128)S(1)} %get-tuple-element.40), channel_id=1, source_target_pairs={{0,128},{64,192},{128,0},{192,64},{1,129},{65,193},{129,1},{193,65... | collective-permute-start | bytes 344072 | tf_op jit(solution)/shard_map/ppermute | solution.py:368
  15.7 6.7 %collective-permute-start.5 = (f32[16,1792]{1,0:T(8,128)S(1)}, f32[16,1792]{1,0:T(8,128)S(1)}, u32[]{:S(2)}, u32[]{:S(2)}) collective-permute-start(f32[16,1792]{1,0:T(8,128)S(1)} %get-tuple-element.42), channel_id=1, source_target_pairs={{0,192},{64,0},{128,64},{192,128},{1,193},{65,1},{129,65},{193,129... | collective-permute-start | bytes 344072 | tf_op jit(solution)/shard_map/ppermute | solution.py:368
  19.6 15.9 %collective-permute-start.10 = (bf16[64,1024]{1,0:T(8,128)(2,1)S(1)}, bf16[64,1024]{1,0:T(8,128)(2,1)S(1)}, u32[]{:S(2)}, u32[]{:S(2)}) collective-permute-start(bf16[64,1024]{1,0:T(8,128)(2,1)S(1)} %get-tuple-element.47), channel_id=1, source_target_pairs={{0,2},{2,4},{4,6},{6,0},{1,3},{3,5},{5,7},{7,1},{8,10},{10,12},{12... | collective-permute-start | bytes 393224 | tf_op jit(solution)/shard_map/ppermute | solution.py:368
  19.7 15.8 %collective-permute-start.11 = (bf16[64,1024]{1,0:T(8,128)(2,1)S(1)}, bf16[64,1024]{1,0:T(8,128)(2,1)S(1)}, u32[]{:S(2)}, u32[]{:S(2)}) collective-permute-start(bf16[64,1024]{1,0:T(8,128)(2,1)S(1)} %get-tuple-element.48), channel_id=1, source_target_pairs={{0,6},{2,0},{4,2},{6,4},{1,7},{3,1},{5,3},{7,5},{8,14},{10,8},{12,... | collective-permute-start | bytes 393224 | tf_op jit(solution)/shard_map/ppermute | solution.py:368
  25.6 7.0 %collective-permute-start.9 = (f32[8,1792]{1,0:T(8,128)S(1)}, f32[8,1792]{1,0:T(8,128)S(1)}, u32[]{:S(2)}, u32[]{:S(2)}) collective-permute-start(f32[8,1792]{1,0:T(8,128)S(1)} %shard_map.66.own_ref), channel_id=1, source_target_pairs={{0,32},{8,40},{16,48},{24,56},{32,0},{40,8},{48,16},{56,24},{1,33}... | collective-permute-start | bytes 172040 | tf_op jit(solution)/shard_map/ppermute | solution.py:368
  30.1 5.4 %collective-permute-start.7 = (f32[8,1792]{1,0:T(8,128)S(1)}, f32[8,1792]{1,0:T(8,128)S(1)}, u32[]{:S(2)}, u32[]{:S(2)}) collective-permute-start(f32[8,1792]{1,0:T(8,128)S(1)} %shard_map.66.own_ref), channel_id=1, source_target_pairs={{0,16},{8,24},{16,32},{24,40},{32,48},{40,56},{48,0},{56,8},{1,17}... | collective-permute-start | bytes 172040 | tf_op jit(solution)/shard_map/ppermute | solution.py:368
  37.0 6.4 %collective-permute-start.16 = (bf16[64,1024]{1,0:T(8,128)(2,1)S(1)}, bf16[64,1024]{1,0:T(8,128)(2,1)S(1)}, u32[]{:S(2)}, u32[]{:S(2)}) collective-permute-start(bf16[64,1024]{1,0:T(8,128)(2,1)S(1)} %get-tuple-element.49), channel_id=1, source_target_pairs={{0,4},{2,6},{4,0},{6,2},{1,5},{3,7},{5,1},{7,3},{8,12},{10,14},{12... | collective-permute-start | bytes 393224 | tf_op jit(solution)/shard_map/ppermute | solution.py:368
  39.9 5.2 %collective-permute-start.15 = (f32[16,1792]{1,0:T(8,128)S(1)}, f32[16,1792]{1,0:T(8,128)S(1)}, u32[]{:S(2)}, u32[]{:S(2)}) collective-permute-start(f32[16,1792]{1,0:T(8,128)S(1)} %shard_map.68.own_ref), channel_id=1, source_target_pairs={{0,128},{64,192},{128,0},{192,64},{1,129},{65,193},{129,1},{193,65... | collective-permute-start | bytes 344072 | tf_op jit(solution)/shard_map/ppermute | solution.py:368
  43.0 4.9 %collective-permute-start.13 = (f32[16,1792]{1,0:T(8,128)S(1)}, f32[16,1792]{1,0:T(8,128)S(1)}, u32[]{:S(2)}, u32[]{:S(2)}) collective-permute-start(f32[16,1792]{1,0:T(8,128)S(1)} %shard_map.68.own_ref), channel_id=1, source_target_pairs={{0,64},{64,128},{128,192},{192,0},{1,65},{65,129},{129,193},{193,1... | collective-permute-start | bytes 344072 | tf_op jit(solution)/shard_map/ppermute | solution.py:368
  48.9 10.0 %collective-permute-start.17 = (f32[224,128]{1,0:T(8,128)S(1)}, f32[224,128]{1,0:T(8,128)S(1)}, u32[]{:S(2)}, u32[]{:S(2)}) collective-permute-start(f32[224,128]{1,0:T(8,128)S(1)} %get-tuple-element.50.a_ref), channel_id=1, source_target_pairs={{0,1},{1,0},{2,3},{3,2},{4,5},{5,4},{6,7},{7,6},{8,9},{9,8},{10,11... | collective-permute-start | bytes 344072 | tf_op jit(solution)/shard_map/ppermute | solution.py:333
  58.9 5.2 %collective-permute-start.20 = (f32[224,128]{1,0:T(8,128)S(1)}, f32[224,128]{1,0:T(8,128)S(1)}, u32[]{:S(2)}, u32[]{:S(2)}) collective-permute-start(f32[224,128]{1,0:T(8,128)S(1)} %shard_map.70.own_ref), channel_id=1, source_target_pairs={{0,192},{1,5},{2,194},{3,7},{4,196},{5,1},{6,198},{7,3},{8,200},{9... | collective-permute-start | bytes 344072 | tf_op jit(solution)/shard_map/ppermute | solution.py:344
  60.4 5.3 %collective-permute-start.19 = (f32[224,128]{1,0:T(8,128)S(1)}, f32[224,128]{1,0:T(8,128)S(1)}, u32[]{:S(2)}, u32[]{:S(2)}) collective-permute-start(f32[224,128]{1,0:T(8,128)S(1)} %shard_map.70.own_ref), channel_id=1, source_target_pairs={{0,64},{1,7},{2,66},{3,1},{4,68},{5,3},{6,70},{7,5},{8,72},{9,15},... | collective-permute-start | bytes 344072 | tf_op jit(solution)/shard_map/ppermute | solution.py:344
  66.7 7.3 %collective-permute-start.21 = (f32[16,1024]{1,0:T(8,128)S(1)}, f32[16,1024]{1,0:T(8,128)S(1)}, u32[]{:S(2)}, u32[]{:S(2)}) collective-permute-start(f32[16,1024]{1,0:T(8,128)S(1)} %get-tuple-element.53), channel_id=1, source_target_pairs={{0,6},{1,129},{2,0},{3,131},{4,2},{5,133},{6,4},{7,135},{8,14},{9,... | collective-permute-start | bytes 196616 | tf_op jit(solution)/shard_map/ppermute | solution.py:344
  66.9 7.2 %collective-permute-start.22 = (f32[16,1024]{1,0:T(8,128)S(1)}, f32[16,1024]{1,0:T(8,128)S(1)}, u32[]{:S(2)}, u32[]{:S(2)}) collective-permute-start(f32[16,1024]{1,0:T(8,128)S(1)} %get-tuple-element.54), channel_id=1, source_target_pairs={{0,6},{1,65},{2,0},{3,67},{4,2},{5,69},{6,4},{7,71},{8,14},{9,73},... | collective-permute-start | bytes 196616 | tf_op jit(solution)/shard_map/ppermute | solution.py:344
  67.2 6.8 %collective-permute-start.23 = (f32[16,1024]{1,0:T(8,128)S(1)}, f32[16,1024]{1,0:T(8,128)S(1)}, u32[]{:S(2)}, u32[]{:S(2)}) collective-permute-start(f32[16,1024]{1,0:T(8,128)S(1)} %get-tuple-element.55), channel_id=1, source_target_pairs={{0,2},{1,193},{2,4},{3,195},{4,6},{5,197},{6,0},{7,199},{8,10},{9,... | collective-permute-start | bytes 196616 | tf_op jit(solution)/shard_map/ppermute | solution.py:344
  77.3 7.8 %collective-permute-start.28 = (f32[16,1024]{1,0:T(8,128)S(1)}, f32[16,1024]{1,0:T(8,128)S(1)}, u32[]{:S(2)}, u32[]{:S(2)}) collective-permute-start(f32[16,1024]{1,0:T(8,128)S(1)} %shard_map.76.own_ref), channel_id=1, source_target_pairs={{0,6},{1,33},{2,0},{3,35},{4,2},{5,37},{6,4},{7,39},{8,14},{9,41},... | collective-permute-start | bytes 196616 | tf_op jit(solution)/shard_map/ppermute | solution.py:344
  82.3 5.2 %collective-permute-start.26 = (f32[16,1024]{1,0:T(8,128)S(1)}, f32[16,1024]{1,0:T(8,128)S(1)}, u32[]{:S(2)}, u32[]{:S(2)}) collective-permute-start(f32[16,1024]{1,0:T(8,128)S(1)} %shard_map.76.own_ref), channel_id=1, source_target_pairs={{0,6},{1,17},{2,0},{3,19},{4,2},{5,21},{6,4},{7,23},{8,14},{9,25},... | collective-permute-start | bytes 196616 | tf_op jit(solution)/shard_map/ppermute | solution.py:344
  87.6 5.6 %collective-permute-start.31 = (f32[16,1024]{1,0:T(8,128)S(1)}, f32[16,1024]{1,0:T(8,128)S(1)}, u32[]{:S(2)}, u32[]{:S(2)}) collective-permute-start(f32[16,1024]{1,0:T(8,128)S(1)} %shard_map.77.own_ref), channel_id=1, source_target_pairs={{0,6},{1,129},{2,0},{3,131},{4,2},{5,133},{6,4},{7,135},{8,14},{9,... | collective-permute-start | bytes 196616 | tf_op jit(solution)/shard_map/ppermute | solution.py:344
  88.6 5.0 %collective-permute-start.30 = (f32[16,1024]{1,0:T(8,128)S(1)}, f32[16,1024]{1,0:T(8,128)S(1)}, u32[]{:S(2)}, u32[]{:S(2)}) collective-permute-start(f32[16,1024]{1,0:T(8,128)S(1)} %shard_map.77.own_ref), channel_id=1, source_target_pairs={{0,2},{1,193},{2,4},{3,195},{4,6},{5,197},{6,0},{7,199},{8,10},{9,... | collective-permute-start | bytes 196616 | tf_op jit(solution)/shard_map/ppermute | solution.py:344
  95.0 7.3 %collective-permute-start.35 = (f32[64,1152]{1,0:T(8,128)S(1)}, f32[64,1152]{1,0:T(8,128)S(1)}, u32[]{:S(2)}, u32[]{:S(2)}) collective-permute-start(f32[64,1152]{1,0:T(8,128)S(1)} %shard_map.78.refs_0_), channel_id=1, source_target_pairs={{0,192},{1,5},{2,194},{3,7},{4,196},{5,1},{6,198},{7,3},{8,200},{9... | collective-permute-start | bytes 884744 | tf_op jit(solution)/shard_map/ppermute | solution.py:344
  95.1 9.2 %collective-permute-start.34 = (f32[64,1152]{1,0:T(8,128)S(1)}, f32[64,1152]{1,0:T(8,128)S(1)}, u32[]{:S(2)}, u32[]{:S(2)}) collective-permute-start(f32[64,1152]{1,0:T(8,128)S(1)} %shard_map.78.refs_0_), channel_id=1, source_target_pairs={{0,64},{1,7},{2,66},{3,1},{4,68},{5,3},{6,70},{7,5},{8,72},{9,15},... | collective-permute-start | bytes 884744 | tf_op jit(solution)/shard_map/ppermute | solution.py:344
  97.2 8.1 %collective-permute-start.33 = (f32[64,1152]{1,0:T(8,128)S(1)}, f32[64,1152]{1,0:T(8,128)S(1)}, u32[]{:S(2)}, u32[]{:S(2)}) collective-permute-start(f32[64,1152]{1,0:T(8,128)S(1)} %shard_map.78.refs_0_), channel_id=1, source_target_pairs={{0,192},{1,3},{2,194},{3,5},{4,196},{5,7},{6,198},{7,1},{8,200},{9... | collective-permute-start | bytes 884744 | tf_op jit(solution)/shard_map/ppermute | solution.py:344
  97.2 8.1 %collective-permute-start.36 = (f32[64,1152]{1,0:T(8,128)S(1)}, f32[64,1152]{1,0:T(8,128)S(1)}, u32[]{:S(2)}, u32[]{:S(2)}) collective-permute-start(f32[64,1152]{1,0:T(8,128)S(1)} %shard_map.78.refs_0_), channel_id=1, source_target_pairs={{0,1},{1,0},{2,3},{3,2},{4,5},{5,4},{6,7},{7,6},{8,9},{9,8},{10,11... | collective-permute-start | bytes 884744 | tf_op jit(solution)/shard_map/ppermute | solution.py:333
  (16 other events, 56.1 us)

commit v3 on v2

--- a/solution.py
+++ b/solution.py
@@ -268,7 +268,7 @@
     inv_ref[...] = inverse_factor(unpack(jnp.where(lax.axis_index("c") == 1, own_ref[...], other_ref[...])))
 
 
-def basis_kernel(inv_ref, p3_ref, b3_ref, gram_ref):
+def basis_kernel(inv_ref, p3_ref, after_ref, b3_ref, gram_ref):
     b3 = split3(dot6(inv_ref[...], p3_ref[...]))
     b3_ref[...] = b3
     gram_ref[...] = pack(gram3(b3))
@@ -282,18 +282,22 @@
     out_ref[...] = a_ref[...] + b_ref[...]
 
 
-def block_kernel(own_ref, a_ref, b_ref, c_ref, gram_ref, other_ref, out_ref):
+def block_kernel(own_ref, a_ref, b_ref, c_ref, after_ref, keep_ref, send_ref, whole_ref):
     for place, ref in in_order(lax.axis_index("y"), (own_ref, a_ref, b_ref, c_ref)):
-        out_ref[rows_at(place, RANK // NY), :CB] = ref[...]
-    out_ref[: RANK // 2, CB:] = gram_ref[...] + other_ref[...]
-    out_ref[RANK // 2 :, CB:] = jnp.zeros((RANK // 2, 2 * RANK), f32)
-
-
-def second_kernel(*refs):
-    inv_ref, total_ref, inverse_ref, slots_ref = refs[2 * NX :]
-    core = lax.axis_index("c") == 1
-    for k, (place, ref) in enumerate(in_order(lax.axis_index("x"), refs[:NX])):
-        slots_ref[place] = jnp.where(core, ref[: RANK // 2, CB:], refs[NX + k][: RANK // 2, CB:])
+        whole_ref[rows_at(place, RANK // NY), :] = ref[...]
+    c, half = lax.axis_index("c"), RANK // 2
+    keep_ref[...] = whole_ref[rows_at(c, half), :]
+    send_ref[...] = whole_ref[rows_at(1 - c, half), :]
+
+
+def hand_kernel(keep_ref, got_ref, gram_ref, other_ref, out_ref):
+    out_ref[:, :CB] = jnp.where(lax.axis_index("c") == 1, keep_ref[...], got_ref[...])
+    out_ref[:, CB:] = gram_ref[...] + other_ref[...]
+
+
+def second_kernel(own_ref, a_ref, b_ref, c_ref, inv_ref, total_ref, inverse_ref, slots_ref):
+    for place, ref in in_order(lax.axis_index("x"), (own_ref, a_ref, b_ref, c_ref)):
+        slots_ref[place] = ref[:, CB:]
     gram = unpack((slots_ref[0] + slots_ref[1]) + (slots_ref[2] + slots_ref[3]))
     rows = lax.broadcasted_iota(jnp.int32, (RANK, RANK), 0)
     cols = lax.broadcasted_iota(jnp.int32, (RANK, RANK), 1)
@@ -313,11 +317,12 @@
 
 
 def new_kernel(*refs):
-    total_ref, inverse_ref, b3_ref, out_ref, basis_ref, whole_ref, scaled_ref, sems = refs[2 * NX :]
-    x, core, total, copies = lax.axis_index("x"), lax.axis_index("c") == 1, total_ref[...], []
+    total_ref, inverse_ref, b3_ref, out_ref, basis_ref, s_ref, whole_ref, scaled_ref, sems = refs[2 * NX :]
+    x, c, half, total, copies = lax.axis_index("x"), lax.axis_index("c"), RANK // 2, total_ref[...], []
     for k, (place, ref) in enumerate(in_order(x, refs[:NX])):
-        block = jnp.where(core, ref[:, :CB], refs[NX + k][:, :CB])
-        whole_ref[k] = dot6(total, split3(block))
+        s_ref[k, rows_at(c, half), :] = ref[:, :CB]
+        s_ref[k, rows_at(1 - c, half), :] = refs[NX + k][:, :CB]
+        whole_ref[k] = dot6(total, split3(s_ref[k]))
         cols = rows_at(place, CB)
         copies.append(pltpu.make_async_copy(whole_ref.at[k], out_ref.at[:, cols], sems.at[k]))
         copies[-1].start()
@@ -419,19 +424,26 @@
     parts = call(
         right_kernel, [piece] * 4, mixed, *cot, scratch=[pltpu.VMEM((4, 2 * TB, CB), bf16), pltpu.VMEM((RANK, CB), f32)]
     )
-    inverse = call(first_kernel, ((RANK, RANK), f32), gram, swap(gram), parts[0], unread=(2,))
-    s = call(sum_y_kernel, piece, *deal(parts, "y", lead_shift), inverse, scratch=[slots], unread=(4,))
-    b3, gram = call(basis_kernel, [((3 * RANK, FB), bf16), small], inverse, p3)
-    s = call(add_after_kernel, piece, s, lead_swap_z(s), gram, unread=(2,))
-    s = call(sum_z_kernel, piece, *share(s, "z", lead_shift), scratch=[slots])
-    s = call(block_kernel, ((RANK, CB + 2 * RANK), f32), *share(s, "y", lead_shift), gram, swap(gram))
-    blocks = share(s, "x", lead_shift)
+    gram_other = swap(gram)
+    s = call(sum_y_kernel, piece, *deal(parts, "y", lead_shift), gram_other, scratch=[slots], unread=(4,))
+    inverse = call(first_kernel, ((RANK, RANK), f32), gram, gram_other, s, unread=(2,))
+    s = call(add_after_kernel, piece, s, lead_swap_z(s), inverse, unread=(2,))
+    b3, gram = call(basis_kernel, [((3 * RANK, FB), bf16), small], inverse, p3, s, unread=(2,))
+    s = call(sum_z_after_kernel, piece, *share(s, "z", lead_shift), gram, scratch=[slots], unread=(4,))
+    rows = ((half, CB), f32)
+    gram_other = swap(gram)
+    keep, send = call(
+        block_kernel, [rows, rows], *share(s, "y", lead_shift), gram_other, scratch=[pltpu.VMEM((RANK, CB), f32)], unread=(4,)
+    )
+    s = call(hand_kernel, ((half, CB + 2 * RANK), f32), keep, swap(send), gram, gram_other)
+    blocks = share(s, "x")
     blocks += [swap(b) for b in blocks]
     square = ((RANK, RANK), f32)
-    total, second = call(second_kernel, [square, square], *blocks, inverse, scratch=[pltpu.VMEM((4, *small[0]), f32)])
+    total, second = call(second_kernel, [square, square], *blocks[:NX], inverse, scratch=[pltpu.VMEM((4, *small[0]), f32)])
+    wide_block = pltpu.VMEM((NX, RANK, CB), f32)
     q_new, scaled = call(
         new_kernel, [((RANK, D), f32), ((RANK, FB), f32)], *blocks, total, second, b3,
-        scratch=[pltpu.VMEM((NX, RANK, CB), f32), pltpu.VMEM((RANK, FB), f32), dma((NX + 1,))], out_hbm=True,
+        scratch=[wide_block, wide_block, pltpu.VMEM((RANK, FB), f32), dma((NX + 1,))], out_hbm=True,
     )
     return scaled.T, q_new.T
 

time: 110 us -> 111 us (level)
  starting transfers between devices: 58.3 us -> 62.5 us
  waiting for transfers between devices: 39.2 us -> 35.9 us
    ppermute x16 -> x13, waiting for transfers between devices: 16 us -> 8.68 us  [lead(): return lax.ppermute(a, ('y', 'z', 'x', 'c'), pairs)]
    ppermute x12 -> x15, waiting for transfers between devices: 10.3 us -> 14.2 us  [shift(): lax.ppermute(a, axis, [(i, (i + k * step) % size) for i in range(size)])]
    ppermute x12 -> x15, starting transfers between devices: 18.3 us -> 21.9 us  [shift(): lax.ppermute(a, axis, [(i, (i + k * step) % size) for i in range(size)])]
    ppermute x8 -> x9, starting transfers between devices: 19.5 us -> 22 us  [swap(): return lax.ppermute(a, 'c', [(0, 1), (1, 0)])]
    ppermute x16 -> x13, starting transfers between devices: 18.2 us -> 16.3 us  [lead(): return lax.ppermute(a, ('y', 'z', 'x', 'c'), pairs)]
    ppermute x8 -> x9, waiting for transfers between devices: 4.25 us -> 4.39 us  [swap(): return lax.ppermute(a, 'c', [(0, 1), (1, 0)])]
    pallas_call x22 -> x23, Pallas kernels: 10.9 us -> 11 us  [call(): pl.pallas_call(kernel, out_shape=shapes if many else shapes[0], in_specs=...]
  transfers between devices with their start and end apart: 40 -> 41, of which waited for: 28 -> 26; matrix products, arithmetic and copies ran while one was open for 0% -> 0% of each run, Pallas kernels for 5% -> 6%
where the time goes in v3:
time: 111 us; the launch traced here: 110 us
  starting transfers between devices  62.5 us (56%)
  waiting for transfers between devices  35.9 us (32%)
  Pallas kernels  11 us (10%)
    ppermute x9, starting transfers between devices, swap(): return lax.ppermute(a, 'c', [(0, 1), (1, 0)])  22 us
    ppermute x15, starting transfers between devices, shift(): lax.ppermute(a, axis, [(i, (i + k * step) % size) for i in range(size)])  21.9 us
    ppermute x13, starting transfers between devices, lead(): return lax.ppermute(a, ('y', 'z', 'x', 'c'), pairs)  16.3 us
    ppermute x15, waiting for transfers between devices, shift(): lax.ppermute(a, axis, [(i, (i + k * step) % size) for i in range(size)])  14.2 us
    pallas_call x23, Pallas kernels, call(): pl.pallas_call(kernel, out_shape=shapes if many else shapes[0], in_specs=...  11 us
    ppermute x13, waiting for transfers between devices, lead(): return lax.ppermute(a, ('y', 'z', 'x', 'c'), pairs)  8.68 us
    ppermute x2, waiting for transfers between devices, pair_x(): return lax.ppermute(a, 'x', [(x, partner(x)) for x in range(NX)])  4.49 us
    ppermute x9, waiting for transfers between devices, swap(): return lax.ppermute(a, 'c', [(0, 1), (1, 0)])  4.39 us
  transfers between devices with their start and end apart: 41, of which 26 were waited for; matrix products, arithmetic and copies ran while one was open for 0% of the time, Pallas kernels for 6%

profile of v3, /device:TPU:1, one launch (start us, length us, event | category | flops | bytes accessed | tf_op | source)
XLA Modules:
  0.0 110.4 jit_solution(13541852348816117711)
XLA Ops:
  0.6 3.3 %collective-permute-start = (bf16[32,4096]{1,0:T(8,128)(2,1)}, bf16[32,4096]{1,0:T(8,128)(2,1)S(1)}, u32[]{:S(2)}, u32[]{:S(2)}) collective-permute-start(bf16[32,4096]{1,0:T(8,128)(2,1)} %cot_ref.1), channel_id=1, source_target_pairs={{0,1},{1,0},{2,3},{3,2},{4,5},{5,4},{6,7},{7,6},{8,9},{9,8},{10,11... | collective-permute-start | bytes 786440 | tf_op jit(solution)/shard_map/ppermute | solution.py:338
  6.2 2.6 %collective-permute-done.1.other_ref = f32[32,128]{1,0:T(8,128)S(1)} collective-permute-done((f32[32,128]{1,0:T(8,128)S(1)}, f32[32,128]{1,0:T(8,128)S(1)}, u32[]{:S(2)}, u32[]{:S(2)}) %collective-permute-start.1) | collective-permute-done | bytes 16416 | tf_op jit(solution)/shard_map/ppermute | solution.py:342
  10.9 1.9 %collective-permute-done.2.far_ref = f32[2,32,128]{2,1,0:T(8,128)S(1)} collective-permute-done((f32[2,32,128]{2,1,0:T(8,128)S(1)}, f32[2,32,128]{2,1,0:T(8,128)S(1)}, u32[]{:S(2)}, u32[]{:S(2)}) %collective-permute-start.2) | collective-permute-done | bytes 32800 | tf_op jit(solution)/shard_map/ppermute | solution.py:342
  13.5 2.2 %collective-permute-start.3 = (f32[16,1792]{1,0:T(8,128)S(1)}, f32[16,1792]{1,0:T(8,128)S(1)}, u32[]{:S(2)}, u32[]{:S(2)}) collective-permute-start(f32[16,1792]{1,0:T(8,128)S(1)} %get-tuple-element.42), channel_id=1, source_target_pairs={{0,128},{64,192},{128,0},{192,64},{1,129},{65,193},{129,1},{193,65... | collective-permute-start | bytes 344072 | tf_op jit(solution)/shard_map/ppermute | solution.py:373
  16.7 2.8 %collective-permute-done.4.after_ref.b_ref = f32[16,1792]{1,0:T(8,128)S(1)} collective-permute-done((f32[16,1792]{1,0:T(8,128)S(1)}, f32[16,1792]{1,0:T(8,128)S(1)}, u32[]{:S(2)}, u32[]{:S(2)}) %collective-permute-start.4) | collective-permute-done | bytes 114720 | tf_op jit(solution)/shard_map/ppermute | solution.py:373
  19.7 2.7 %collective-permute-start.11 = (bf16[64,1024]{1,0:T(8,128)(2,1)S(1)}, bf16[64,1024]{1,0:T(8,128)(2,1)S(1)}, u32[]{:S(2)}, u32[]{:S(2)}) collective-permute-start(bf16[64,1024]{1,0:T(8,128)(2,1)S(1)} %get-tuple-element.50), channel_id=1, source_target_pairs={{0,6},{2,0},{4,2},{6,4},{1,7},{3,1},{5,3},{7,5},{8,14},{10,8},{12,... | collective-permute-start | bytes 393224 | tf_op jit(solution)/shard_map/ppermute | solution.py:373
  22.5 3.0 %collective-permute-done.6.b_ref = f32[8,1792]{1,0:T(8,128)S(1)} collective-permute-done((f32[8,1792]{1,0:T(8,128)S(1)}, f32[8,1792]{1,0:T(8,128)S(1)}, u32[]{:S(2)}, u32[]{:S(2)}) %collective-permute-start.6) | collective-permute-done | bytes 57376 | tf_op jit(solution)/shard_map/ppermute | solution.py:368
  25.6 4.6 %collective-permute-start.9 = (f32[8,1792]{1,0:T(8,128)S(1)}, f32[8,1792]{1,0:T(8,128)S(1)}, u32[]{:S(2)}, u32[]{:S(2)}) collective-permute-start(f32[8,1792]{1,0:T(8,128)S(1)} %shard_map.66.own_ref), channel_id=1, source_target_pairs={{0,32},{8,40},{16,48},{24,56},{32,0},{40,8},{48,16},{56,24},{1,33}... | collective-permute-start | bytes 172040 | tf_op jit(solution)/shard_map/ppermute | solution.py:373
  30.1 2.4 %collective-permute-start.7 = (f32[8,1792]{1,0:T(8,128)S(1)}, f32[8,1792]{1,0:T(8,128)S(1)}, u32[]{:S(2)}, u32[]{:S(2)}) collective-permute-start(f32[8,1792]{1,0:T(8,128)S(1)} %shard_map.66.own_ref), channel_id=1, source_target_pairs={{0,16},{8,24},{16,32},{24,40},{32,48},{40,56},{48,0},{56,8},{1,17}... | collective-permute-start | bytes 172040 | tf_op jit(solution)/shard_map/ppermute | solution.py:373
  32.6 2.1 %collective-permute-done.8.b_ref = f32[8,1792]{1,0:T(8,128)S(1)} collective-permute-done((f32[8,1792]{1,0:T(8,128)S(1)}, f32[8,1792]{1,0:T(8,128)S(1)}, u32[]{:S(2)}, u32[]{:S(2)}) %collective-permute-start.8) | collective-permute-done | bytes 57376 | tf_op jit(solution)/shard_map/ppermute | solution.py:373
  37.0 1.8 %collective-permute-start.16 = (bf16[64,1024]{1,0:T(8,128)(2,1)S(1)}, bf16[64,1024]{1,0:T(8,128)(2,1)S(1)}, u32[]{:S(2)}, u32[]{:S(2)}) collective-permute-start(bf16[64,1024]{1,0:T(8,128)(2,1)S(1)} %get-tuple-element.51), channel_id=1, source_target_pairs={{0,4},{2,6},{4,0},{6,2},{1,5},{3,7},{5,1},{7,3},{8,12},{10,14},{12... | collective-permute-start | bytes 393224 | tf_op jit(solution)/shard_map/ppermute | solution.py:373
  39.9 2.0 %collective-permute-start.15 = (f32[16,1792]{1,0:T(8,128)S(1)}, f32[16,1792]{1,0:T(8,128)S(1)}, u32[]{:S(2)}, u32[]{:S(2)}) collective-permute-start(f32[16,1792]{1,0:T(8,128)S(1)} %shard_map.68.own_ref), channel_id=1, source_target_pairs={{0,128},{64,192},{128,0},{192,64},{1,129},{65,193},{129,1},{193,65... | collective-permute-start | bytes 344072 | tf_op jit(solution)/shard_map/ppermute | solution.py:373
  48.9 9.0 %collective-permute-start.17 = (f32[224,128]{1,0:T(8,128)S(1)}, f32[224,128]{1,0:T(8,128)S(1)}, u32[]{:S(2)}, u32[]{:S(2)}) collective-permute-start(f32[224,128]{1,0:T(8,128)S(1)} %get-tuple-element.52.a_ref), channel_id=1, source_target_pairs={{0,1},{1,0},{2,3},{3,2},{4,5},{5,4},{6,7},{7,6},{8,9},{9,8},{10,11... | collective-permute-start | bytes 344072 | tf_op jit(solution)/shard_map/ppermute | solution.py:338
  62.0 2.1 %collective-permute-done.20.c_ref = f32[224,128]{1,0:T(8,128)S(1)} collective-permute-done((f32[224,128]{1,0:T(8,128)S(1)}, f32[224,128]{1,0:T(8,128)S(1)}, u32[]{:S(2)}, u32[]{:S(2)}) %collective-permute-start.20) | collective-permute-done | bytes 114720 | tf_op jit(solution)/shard_map/ppermute | solution.py:349
  67.2 2.3 %collective-permute-start.23 = (f32[16,1024]{1,0:T(8,128)S(1)}, f32[16,1024]{1,0:T(8,128)S(1)}, u32[]{:S(2)}, u32[]{:S(2)}) collective-permute-start(f32[16,1024]{1,0:T(8,128)S(1)} %get-tuple-element.57), channel_id=1, source_target_pairs={{0,2},{1,193},{2,4},{3,195},{4,6},{5,197},{6,0},{7,199},{8,10},{9,... | collective-permute-start | bytes 196616 | tf_op jit(solution)/shard_map/ppermute | solution.py:349
  72.8 1.9 %shard_map.74.after_ref.inv_ref = f32[64,64]{1,0:T(8,128)S(1)} custom-call(f32[32,128]{1,0:T(8,128)S(1)} %get-tuple-element.58.own_ref, f32[32,128]{1,0:T(8,128)S(1)} %collective-permute-done.24.after_ref.other_ref, f32[16,1024]{1,0:T(8,128)S(1)} %shard_map.73.after_ref.a_ref), custom_call_target="tpu_custom_call" | custom-call | tf_op jit(solution)/shard_map/pallas_call | solution.py:121
  75.5 4.2 %collective-permute-start.28 = (f32[16,1024]{1,0:T(8,128)S(1)}, f32[16,1024]{1,0:T(8,128)S(1)}, u32[]{:S(2)}, u32[]{:S(2)}) collective-permute-start(f32[16,1024]{1,0:T(8,128)S(1)} %shard_map.75.after_ref.own_ref), channel_id=1, source_target_pairs={{0,6},{1,33},{2,0},{3,35},{4,2},{5,37},{6,4},{7,39},{8,14},{9,41},... | collective-permute-start | bytes 196616 | tf_op jit(solution)/shard_map/ppermute | solution.py:349
  83.7 2.0 %collective-permute-done.26.a_ref = f32[16,1024]{1,0:T(8,128)S(1)} collective-permute-done((f32[16,1024]{1,0:T(8,128)S(1)}, f32[16,1024]{1,0:T(8,128)S(1)}, u32[]{:S(2)}, u32[]{:S(2)}) %collective-permute-start.26) | collective-permute-done | bytes 65568 | tf_op jit(solution)/shard_map/ppermute | solution.py:349
  86.9 2.1 %collective-permute-start.30 = (f32[16,1024]{1,0:T(8,128)S(1)}, f32[16,1024]{1,0:T(8,128)S(1)}, u32[]{:S(2)}, u32[]{:S(2)}) collective-permute-start(f32[16,1024]{1,0:T(8,128)S(1)} %shard_map.77.own_ref), channel_id=1, source_target_pairs={{0,2},{1,193},{2,4},{3,195},{4,6},{5,197},{6,0},{7,199},{8,10},{9,... | collective-permute-start | bytes 196616 | tf_op jit(solution)/shard_map/ppermute | solution.py:349
  89.1 3.0 %collective-permute-start.32 = (f32[32,128]{1,0:T(8,128)S(1)}, f32[32,128]{1,0:T(8,128)S(1)}, u32[]{:S(2)}, u32[]{:S(2)}) collective-permute-start(f32[32,128]{1,0:T(8,128)S(1)} %get-tuple-element.60.rest_0_.gram_ref), channel_id=1, source_target_pairs={{0,1},{1,0},{2,3},{3,2},{4,5},{5,4},{6,7},{7,6},{8,9},{9,8},{10,11... | collective-permute-start | bytes 49160 | tf_op jit(solution)/shard_map/ppermute | solution.py:338
  96.8 1.9 %collective-permute-start.35 = (f32[32,1152]{1,0:T(8,128)S(1)}, f32[32,1152]{1,0:T(8,128)S(1)}, u32[]{:S(2)}, u32[]{:S(2)}) collective-permute-start(f32[32,1152]{1,0:T(8,128)S(1)} %shard_map.79.own_ref.refs_0_), channel_id=1, source_target_pairs={{0,6},{2,0},{4,2},{6,4},{1,7},{3,1},{5,3},{7,5},{8,14},{10,8},{12,... | collective-permute-start | bytes 442376 | tf_op jit(solution)/shard_map/ppermute | solution.py:373
  100.0 2.1 %collective-permute-done.36.c_ref.refs_3_ = f32[32,1152]{1,0:T(8,128)S(1)} collective-permute-done((f32[32,1152]{1,0:T(8,128)S(1)}, f32[32,1152]{1,0:T(8,128)S(1)}, u32[]{:S(2)}, u32[]{:S(2)}) %collective-permute-start.36) | collective-permute-done | bytes 147488 | tf_op jit(solution)/shard_map/ppermute | solution.py:373
  102.1 2.0 %collective-permute-start.40 = (f32[32,1152]{1,0:T(8,128)S(1)}, f32[32,1152]{1,0:T(8,128)S(1)}, u32[]{:S(2)}, u32[]{:S(2)}) collective-permute-start(f32[32,1152]{1,0:T(8,128)S(1)} %collective-permute-done.36.c_ref.refs_3_), channel_id=1, source_target_pairs={{0,1},{1,0},{2,3},{3,2},{4,5},{5,4},{6,7},{7,6},{8,9},{9,8},{10,11... | collective-permute-start | bytes 442376 | tf_op jit(solution)/shard_map/ppermute | solution.py:338
  104.1 1.8 %collective-permute-done.35.b_ref.refs_2_ = f32[32,1152]{1,0:T(8,128)S(1)} collective-permute-done((f32[32,1152]{1,0:T(8,128)S(1)}, f32[32,1152]{1,0:T(8,128)S(1)}, u32[]{:S(2)}, u32[]{:S(2)}) %collective-permute-start.35) | collective-permute-done | bytes 147488 | tf_op jit(solution)/shard_map/ppermute | solution.py:373
  (81 shorter events, 43.6 us)
Async XLA Ops:
  13.4 6.2 %collective-permute-start.4 = (f32[16,1792]{1,0:T(8,128)S(1)}, f32[16,1792]{1,0:T(8,128)S(1)}, u32[]{:S(2)}, u32[]{:S(2)}) collective-permute-start(f32[16,1792]{1,0:T(8,128)S(1)} %get-tuple-element.43), channel_id=1, source_target_pairs={{0,64},{64,128},{128,192},{192,0},{1,65},{65,129},{129,193},{193,1... | collective-permute-start | bytes 344072 | tf_op jit(solution)/shard_map/ppermute | solution.py:373
  13.5 8.9 %collective-permute-start.3 = (f32[16,1792]{1,0:T(8,128)S(1)}, f32[16,1792]{1,0:T(8,128)S(1)}, u32[]{:S(2)}, u32[]{:S(2)}) collective-permute-start(f32[16,1792]{1,0:T(8,128)S(1)} %get-tuple-element.42), channel_id=1, source_target_pairs={{0,128},{64,192},{128,0},{192,64},{1,129},{65,193},{129,1},{193,65... | collective-permute-start | bytes 344072 | tf_op jit(solution)/shard_map/ppermute | solution.py:373
  15.7 6.7 %collective-permute-start.5 = (f32[16,1792]{1,0:T(8,128)S(1)}, f32[16,1792]{1,0:T(8,128)S(1)}, u32[]{:S(2)}, u32[]{:S(2)}) collective-permute-start(f32[16,1792]{1,0:T(8,128)S(1)} %get-tuple-element.44), channel_id=1, source_target_pairs={{0,192},{64,0},{128,64},{192,128},{1,193},{65,1},{129,65},{193,129... | collective-permute-start | bytes 344072 | tf_op jit(solution)/shard_map/ppermute | solution.py:373
  19.6 15.9 %collective-permute-start.10 = (bf16[64,1024]{1,0:T(8,128)(2,1)S(1)}, bf16[64,1024]{1,0:T(8,128)(2,1)S(1)}, u32[]{:S(2)}, u32[]{:S(2)}) collective-permute-start(bf16[64,1024]{1,0:T(8,128)(2,1)S(1)} %get-tuple-element.49), channel_id=1, source_target_pairs={{0,2},{2,4},{4,6},{6,0},{1,3},{3,5},{5,7},{7,1},{8,10},{10,12},{12... | collective-permute-start | bytes 393224 | tf_op jit(solution)/shard_map/ppermute | solution.py:373
  19.7 15.8 %collective-permute-start.11 = (bf16[64,1024]{1,0:T(8,128)(2,1)S(1)}, bf16[64,1024]{1,0:T(8,128)(2,1)S(1)}, u32[]{:S(2)}, u32[]{:S(2)}) collective-permute-start(bf16[64,1024]{1,0:T(8,128)(2,1)S(1)} %get-tuple-element.50), channel_id=1, source_target_pairs={{0,6},{2,0},{4,2},{6,4},{1,7},{3,1},{5,3},{7,5},{8,14},{10,8},{12,... | collective-permute-start | bytes 393224 | tf_op jit(solution)/shard_map/ppermute | solution.py:373
  25.6 7.0 %collective-permute-start.9 = (f32[8,1792]{1,0:T(8,128)S(1)}, f32[8,1792]{1,0:T(8,128)S(1)}, u32[]{:S(2)}, u32[]{:S(2)}) collective-permute-start(f32[8,1792]{1,0:T(8,128)S(1)} %shard_map.66.own_ref), channel_id=1, source_target_pairs={{0,32},{8,40},{16,48},{24,56},{32,0},{40,8},{48,16},{56,24},{1,33}... | collective-permute-start | bytes 172040 | tf_op jit(solution)/shard_map/ppermute | solution.py:373
  30.1 5.4 %collective-permute-start.7 = (f32[8,1792]{1,0:T(8,128)S(1)}, f32[8,1792]{1,0:T(8,128)S(1)}, u32[]{:S(2)}, u32[]{:S(2)}) collective-permute-start(f32[8,1792]{1,0:T(8,128)S(1)} %shard_map.66.own_ref), channel_id=1, source_target_pairs={{0,16},{8,24},{16,32},{24,40},{32,48},{40,56},{48,0},{56,8},{1,17}... | collective-permute-start | bytes 172040 | tf_op jit(solution)/shard_map/ppermute | solution.py:373
  37.0 6.4 %collective-permute-start.16 = (bf16[64,1024]{1,0:T(8,128)(2,1)S(1)}, bf16[64,1024]{1,0:T(8,128)(2,1)S(1)}, u32[]{:S(2)}, u32[]{:S(2)}) collective-permute-start(bf16[64,1024]{1,0:T(8,128)(2,1)S(1)} %get-tuple-element.51), channel_id=1, source_target_pairs={{0,4},{2,6},{4,0},{6,2},{1,5},{3,7},{5,1},{7,3},{8,12},{10,14},{12... | collective-permute-start | bytes 393224 | tf_op jit(solution)/shard_map/ppermute | solution.py:373
  39.9 5.2 %collective-permute-start.15 = (f32[16,1792]{1,0:T(8,128)S(1)}, f32[16,1792]{1,0:T(8,128)S(1)}, u32[]{:S(2)}, u32[]{:S(2)}) collective-permute-start(f32[16,1792]{1,0:T(8,128)S(1)} %shard_map.68.own_ref), channel_id=1, source_target_pairs={{0,128},{64,192},{128,0},{192,64},{1,129},{65,193},{129,1},{193,65... | collective-permute-start | bytes 344072 | tf_op jit(solution)/shard_map/ppermute | solution.py:373
  48.9 10.0 %collective-permute-start.17 = (f32[224,128]{1,0:T(8,128)S(1)}, f32[224,128]{1,0:T(8,128)S(1)}, u32[]{:S(2)}, u32[]{:S(2)}) collective-permute-start(f32[224,128]{1,0:T(8,128)S(1)} %get-tuple-element.52.a_ref), channel_id=1, source_target_pairs={{0,1},{1,0},{2,3},{3,2},{4,5},{5,4},{6,7},{7,6},{8,9},{9,8},{10,11... | collective-permute-start | bytes 344072 | tf_op jit(solution)/shard_map/ppermute | solution.py:338
  58.9 5.2 %collective-permute-start.20 = (f32[224,128]{1,0:T(8,128)S(1)}, f32[224,128]{1,0:T(8,128)S(1)}, u32[]{:S(2)}, u32[]{:S(2)}) collective-permute-start(f32[224,128]{1,0:T(8,128)S(1)} %shard_map.70.own_ref), channel_id=1, source_target_pairs={{0,192},{1,5},{2,194},{3,7},{4,196},{5,1},{6,198},{7,3},{8,200},{9... | collective-permute-start | bytes 344072 | tf_op jit(solution)/shard_map/ppermute | solution.py:349
  60.4 5.3 %collective-permute-start.19 = (f32[224,128]{1,0:T(8,128)S(1)}, f32[224,128]{1,0:T(8,128)S(1)}, u32[]{:S(2)}, u32[]{:S(2)}) collective-permute-start(f32[224,128]{1,0:T(8,128)S(1)} %shard_map.70.own_ref), channel_id=1, source_target_pairs={{0,64},{1,7},{2,66},{3,1},{4,68},{5,3},{6,70},{7,5},{8,72},{9,15},... | collective-permute-start | bytes 344072 | tf_op jit(solution)/shard_map/ppermute | solution.py:349
  66.7 5.5 %collective-permute-start.21 = (f32[16,1024]{1,0:T(8,128)S(1)}, f32[16,1024]{1,0:T(8,128)S(1)}, u32[]{:S(2)}, u32[]{:S(2)}) collective-permute-start(f32[16,1024]{1,0:T(8,128)S(1)} %get-tuple-element.55), channel_id=1, source_target_pairs={{0,6},{1,129},{2,0},{3,131},{4,2},{5,133},{6,4},{7,135},{8,14},{9,... | collective-permute-start | bytes 196616 | tf_op jit(solution)/shard_map/ppermute | solution.py:349
  66.9 5.3 %collective-permute-start.22 = (f32[16,1024]{1,0:T(8,128)S(1)}, f32[16,1024]{1,0:T(8,128)S(1)}, u32[]{:S(2)}, u32[]{:S(2)}) collective-permute-start(f32[16,1024]{1,0:T(8,128)S(1)} %get-tuple-element.56), channel_id=1, source_target_pairs={{0,6},{1,65},{2,0},{3,67},{4,2},{5,69},{6,4},{7,71},{8,14},{9,73},... | collective-permute-start | bytes 196616 | tf_op jit(solution)/shard_map/ppermute | solution.py:349
  67.2 5.0 %collective-permute-start.23 = (f32[16,1024]{1,0:T(8,128)S(1)}, f32[16,1024]{1,0:T(8,128)S(1)}, u32[]{:S(2)}, u32[]{:S(2)}) collective-permute-start(f32[16,1024]{1,0:T(8,128)S(1)} %get-tuple-element.57), channel_id=1, source_target_pairs={{0,2},{1,193},{2,4},{3,195},{4,6},{5,197},{6,0},{7,199},{8,10},{9,... | collective-permute-start | bytes 196616 | tf_op jit(solution)/shard_map/ppermute | solution.py:349
  75.5 7.4 %collective-permute-start.28 = (f32[16,1024]{1,0:T(8,128)S(1)}, f32[16,1024]{1,0:T(8,128)S(1)}, u32[]{:S(2)}, u32[]{:S(2)}) collective-permute-start(f32[16,1024]{1,0:T(8,128)S(1)} %shard_map.75.after_ref.own_ref), channel_id=1, source_target_pairs={{0,6},{1,33},{2,0},{3,35},{4,2},{5,37},{6,4},{7,39},{8,14},{9,41},... | collective-permute-start | bytes 196616 | tf_op jit(solution)/shard_map/ppermute | solution.py:349
  80.4 5.3 %collective-permute-start.26 = (f32[16,1024]{1,0:T(8,128)S(1)}, f32[16,1024]{1,0:T(8,128)S(1)}, u32[]{:S(2)}, u32[]{:S(2)}) collective-permute-start(f32[16,1024]{1,0:T(8,128)S(1)} %shard_map.75.after_ref.own_ref), channel_id=1, source_target_pairs={{0,6},{1,17},{2,0},{3,19},{4,2},{5,21},{6,4},{7,23},{8,14},{9,25},... | collective-permute-start | bytes 196616 | tf_op jit(solution)/shard_map/ppermute | solution.py:349
  85.8 7.1 %collective-permute-start.31 = (f32[16,1024]{1,0:T(8,128)S(1)}, f32[16,1024]{1,0:T(8,128)S(1)}, u32[]{:S(2)}, u32[]{:S(2)}) collective-permute-start(f32[16,1024]{1,0:T(8,128)S(1)} %shard_map.77.own_ref), channel_id=1, source_target_pairs={{0,6},{1,129},{2,0},{3,131},{4,2},{5,133},{6,4},{7,135},{8,14},{9,... | collective-permute-start | bytes 196616 | tf_op jit(solution)/shard_map/ppermute | solution.py:349
  86.9 6.1 %collective-permute-start.30 = (f32[16,1024]{1,0:T(8,128)S(1)}, f32[16,1024]{1,0:T(8,128)S(1)}, u32[]{:S(2)}, u32[]{:S(2)}) collective-permute-start(f32[16,1024]{1,0:T(8,128)S(1)} %shard_map.77.own_ref), channel_id=1, source_target_pairs={{0,2},{1,193},{2,4},{3,195},{4,6},{5,197},{6,0},{7,199},{8,10},{9,... | collective-permute-start | bytes 196616 | tf_op jit(solution)/shard_map/ppermute | solution.py:349
  95.5 6.7 %collective-permute-start.36 = (f32[32,1152]{1,0:T(8,128)S(1)}, f32[32,1152]{1,0:T(8,128)S(1)}, u32[]{:S(2)}, u32[]{:S(2)}) collective-permute-start(f32[32,1152]{1,0:T(8,128)S(1)} %shard_map.79.own_ref.refs_0_), channel_id=1, source_target_pairs={{0,4},{2,6},{4,0},{6,2},{1,5},{3,7},{5,1},{7,3},{8,12},{10,14},{12... | collective-permute-start | bytes 442376 | tf_op jit(solution)/shard_map/ppermute | solution.py:373
  96.8 9.2 %collective-permute-start.35 = (f32[32,1152]{1,0:T(8,128)S(1)}, f32[32,1152]{1,0:T(8,128)S(1)}, u32[]{:S(2)}, u32[]{:S(2)}) collective-permute-start(f32[32,1152]{1,0:T(8,128)S(1)} %shard_map.79.own_ref.refs_0_), channel_id=1, source_target_pairs={{0,6},{2,0},{4,2},{6,4},{1,7},{3,1},{5,3},{7,5},{8,14},{10,8},{12,... | collective-permute-start | bytes 442376 | tf_op jit(solution)/shard_map/ppermute | solution.py:373
  98.6 8.5 %collective-permute-start.34 = (f32[32,1152]{1,0:T(8,128)S(1)}, f32[32,1152]{1,0:T(8,128)S(1)}, u32[]{:S(2)}, u32[]{:S(2)}) collective-permute-start(f32[32,1152]{1,0:T(8,128)S(1)} %shard_map.79.own_ref.refs_0_), channel_id=1, source_target_pairs={{0,2},{2,4},{4,6},{6,0},{1,3},{3,5},{5,7},{7,1},{8,10},{10,12},{12... | collective-permute-start | bytes 442376 | tf_op jit(solution)/shard_map/ppermute | solution.py:373
  99.1 8.6 %collective-permute-start.37 = (f32[32,1152]{1,0:T(8,128)S(1)}, f32[32,1152]{1,0:T(8,128)S(1)}, u32[]{:S(2)}, u32[]{:S(2)}) collective-permute-start(f32[32,1152]{1,0:T(8,128)S(1)} %shard_map.79.own_ref.refs_0_), channel_id=1, source_target_pairs={{0,1},{1,0},{2,3},{3,2},{4,5},{5,4},{6,7},{7,6},{8,9},{9,8},{10,11... | collective-permute-start | bytes 442376 | tf_op jit(solution)/shard_map/ppermute | solution.py:338
  102.1 5.6 %collective-permute-start.40 = (f32[32,1152]{1,0:T(8,128)S(1)}, f32[32,1152]{1,0:T(8,128)S(1)}, u32[]{:S(2)}, u32[]{:S(2)}) collective-permute-start(f32[32,1152]{1,0:T(8,128)S(1)} %collective-permute-done.36.c_ref.refs_3_), channel_id=1, source_target_pairs={{0,1},{1,0},{2,3},{3,2},{4,5},{5,4},{6,7},{7,6},{8,9},{9,8},{10,11... | collective-permute-start | bytes 442376 | tf_op jit(solution)/shard_map/ppermute | solution.py:338
  (17 other events, 61.0 us)

commit v4 on v2

--- a/solution.py
+++ b/solution.py
@@ -268,7 +268,7 @@
     inv_ref[...] = inverse_factor(unpack(jnp.where(lax.axis_index("c") == 1, own_ref[...], other_ref[...])))
 
 
-def basis_kernel(inv_ref, p3_ref, b3_ref, gram_ref):
+def basis_kernel(inv_ref, p3_ref, after_ref, b3_ref, gram_ref):
     b3 = split3(dot6(inv_ref[...], p3_ref[...]))
     b3_ref[...] = b3
     gram_ref[...] = pack(gram3(b3))
@@ -282,33 +282,47 @@
     out_ref[...] = a_ref[...] + b_ref[...]
 
 
-def block_kernel(own_ref, a_ref, b_ref, c_ref, gram_ref, other_ref, out_ref):
+def sum_z_gram_kernel(own_ref, a_ref, b_ref, c_ref, gram_ref, other_ref, out_ref, slots_ref):
+    total = sum_in_order(slots_ref, lax.axis_index("z") // 2, (own_ref, a_ref, b_ref, c_ref))
+    gram, rows = gram_ref[...] + other_ref[...], RANK // NY
+    gram = jnp.concatenate([gram[:rows], gram[rows:]], axis=1)
+    core, size = lax.axis_index("c") == 1, 4 * RANK
+    out_ref[:, :size] = jnp.where(core, total[:, :size], gram)
+    out_ref[:, size:] = total[:, size:]
+
+
+def block_kernel(own_ref, a_ref, b_ref, c_ref, out_ref):
     for place, ref in in_order(lax.axis_index("y"), (own_ref, a_ref, b_ref, c_ref)):
-        out_ref[rows_at(place, RANK // NY), :CB] = ref[...]
-    out_ref[: RANK // 2, CB:] = gram_ref[...] + other_ref[...]
-    out_ref[RANK // 2 :, CB:] = jnp.zeros((RANK // 2, 2 * RANK), f32)
-
-
-def second_kernel(*refs):
-    inv_ref, total_ref, inverse_ref, slots_ref = refs[2 * NX :]
-    core = lax.axis_index("c") == 1
-    for k, (place, ref) in enumerate(in_order(lax.axis_index("x"), refs[:NX])):
-        slots_ref[place] = jnp.where(core, ref[: RANK // 2, CB:], refs[NX + k][: RANK // 2, CB:])
-    gram = unpack((slots_ref[0] + slots_ref[1]) + (slots_ref[2] + slots_ref[3]))
+        out_ref[rows_at(place, RANK // NY), :] = ref[...]
+
+
+def second_kernel(own_ref, a_ref, b_ref, c_ref, inverse_ref, slots_ref):
+    for place, ref in in_order(lax.axis_index("x"), (own_ref, a_ref, b_ref, c_ref)):
+        slots_ref[place] = ref[:, : 4 * RANK]
+    gram = (slots_ref[0] + slots_ref[1]) + (slots_ref[2] + slots_ref[3])
+    gram = unpack(jnp.concatenate([gram[:, : 2 * RANK], gram[:, 2 * RANK :]], axis=0))
     rows = lax.broadcasted_iota(jnp.int32, (RANK, RANK), 0)
     cols = lax.broadcasted_iota(jnp.int32, (RANK, RANK), 1)
     off = gram - jnp.where(rows == cols, 1.0, 0.0).astype(f32)
-    near = jnp.max(jnp.abs(off)) < 1e-3
-
-    @pl.when(near)
+    here, near = lax.axis_index("c") == 0, jnp.max(jnp.abs(off)) < 1e-3
+
+    @pl.when(jnp.logical_and(here, near))
     def _():
         inverse_ref[...] = near_inverse_factor(off)
 
-    @pl.when(jnp.logical_not(near))
+    @pl.when(jnp.logical_and(here, jnp.logical_not(near)))
     def _():
         inverse_ref[...] = inverse_factor(gram)
 
-    inverse = inverse_ref[...]
+    @pl.when(jnp.logical_not(here))
+    def _():
+        inverse_ref[...] = jnp.zeros((RANK, RANK), f32)
+
+
+def total_kernel(own_ref, other_ref, inv_ref, block_ref, total_ref, inverse_ref, pass_ref):
+    pass_ref[...] = block_ref[...]
+    inverse = jnp.where(lax.axis_index("c") == 0, own_ref[...], other_ref[...])
+    inverse_ref[...] = inverse
     total_ref[...] = jnp.dot(inverse, inv_ref[...], precision=HIGHEST, preferred_element_type=f32) * (1.0 / N_DP)
 
 
@@ -316,7 +330,7 @@
     total_ref, inverse_ref, b3_ref, out_ref, basis_ref, whole_ref, scaled_ref, sems = refs[2 * NX :]
     x, core, total, copies = lax.axis_index("x"), lax.axis_index("c") == 1, total_ref[...], []
     for k, (place, ref) in enumerate(in_order(x, refs[:NX])):
-        block = jnp.where(core, ref[:, :CB], refs[NX + k][:, :CB])
+        block = jnp.where(core, ref[...], refs[NX + k][...])
         whole_ref[k] = dot6(total, split3(block))
         cols = rows_at(place, CB)
         copies.append(pltpu.make_async_copy(whole_ref.at[k], out_ref.at[:, cols], sems.at[k]))
@@ -348,11 +362,9 @@
     hop = 1 if k == 3 else -1
     if axis == "x":
         return lead(a, lambda y, z, x: (y, z, (x + k) % NX), lambda y, z, x: ((y + hop) % NY, z, x))
-
-    def step(y, z, x):
-        return ((y + k) % NY, z, x) if axis == "y" else (y, (z + 2 * k) % NZ, x)
-
-    return lead(a, step, lambda y, z, x: (y, z, (x + hop) % NX))
+    if axis == "y":
+        return lead(a, lambda y, z, x: ((y + k) % NY, z, x), lambda y, z, x: (y, z, (x + k) % NX))
+    return lead(a, lambda y, z, x: (y, (z + 2 * k) % NZ, x), lambda y, z, x: (y, z, (x + hop) % NX))
 
 
 def lead_swap_z(a):
@@ -419,16 +431,18 @@
     parts = call(
         right_kernel, [piece] * 4, mixed, *cot, scratch=[pltpu.VMEM((4, 2 * TB, CB), bf16), pltpu.VMEM((RANK, CB), f32)]
     )
-    inverse = call(first_kernel, ((RANK, RANK), f32), gram, swap(gram), parts[0], unread=(2,))
-    s = call(sum_y_kernel, piece, *deal(parts, "y", lead_shift), inverse, scratch=[slots], unread=(4,))
-    b3, gram = call(basis_kernel, [((3 * RANK, FB), bf16), small], inverse, p3)
-    s = call(add_after_kernel, piece, s, lead_swap_z(s), gram, unread=(2,))
-    s = call(sum_z_kernel, piece, *share(s, "z", lead_shift), scratch=[slots])
-    s = call(block_kernel, ((RANK, CB + 2 * RANK), f32), *share(s, "y", lead_shift), gram, swap(gram))
-    blocks = share(s, "x", lead_shift)
+    gram_other = swap(gram)
+    s = call(sum_y_kernel, piece, *deal(parts, "y", lead_shift), gram_other, scratch=[slots], unread=(4,))
+    inverse = call(first_kernel, ((RANK, RANK), f32), gram, gram_other, s, unread=(2,))
+    s = call(add_after_kernel, piece, s, lead_swap_z(s), inverse, unread=(2,))
+    b3, gram = call(basis_kernel, [((3 * RANK, FB), bf16), small], inverse, p3, s, unread=(2,))
+    s = call(sum_z_gram_kernel, piece, *share(s, "z", lead_shift), gram, swap(gram), scratch=[slots])
+    quarters, square, whole = share(s, "y", lead_shift), ((RANK, RANK), f32), ((RANK, CB), f32)
+    s = call(block_kernel, whole, *quarters)
+    second = call(second_kernel, square, *quarters, scratch=[pltpu.VMEM((4, RANK // NY, 4 * RANK), f32)])
+    total, second, own = call(total_kernel, [square, square, whole], second, swap(second), inverse, s)
+    blocks = [own] + share(s, "x", lead_shift)[1:]
     blocks += [swap(b) for b in blocks]
-    square = ((RANK, RANK), f32)
-    total, second = call(second_kernel, [square, square], *blocks, inverse, scratch=[pltpu.VMEM((4, *small[0]), f32)])
     q_new, scaled = call(
         new_kernel, [((RANK, D), f32), ((RANK, FB), f32)], *blocks, total, second, b3,
         scratch=[pltpu.VMEM((NX, RANK, CB), f32), pltpu.VMEM((RANK, FB), f32), dma((NX + 1,))], out_hbm=True,

time: 110 us -> 110 us (level)
  starting transfers between devices: 58.3 us -> 65 us
  waiting for transfers between devices: 39.2 us -> 33.2 us
    ppermute x16, waiting for transfers between devices: 16 us -> 9.22 us  [lead(): return lax.ppermute(a, ('y', 'z', 'x', 'c'), pairs)]
    ppermute x8 -> x9, starting transfers between devices: 19.5 us -> 26 us  [swap(): return lax.ppermute(a, 'c', [(0, 1), (1, 0)])]
    ppermute x8 -> x9, waiting for transfers between devices: 4.25 us -> 5.06 us  [swap(): return lax.ppermute(a, 'c', [(0, 1), (1, 0)])]
    pallas_call x22 -> x23, Pallas kernels: 10.9 us -> 10.7 us  [call(): pl.pallas_call(kernel, out_shape=shapes if many else shapes[0], in_specs=...]
  transfers between devices with their start and end apart: 40 -> 41, of which waited for: 28 -> 24; matrix products, arithmetic and copies ran while one was open for 0% -> 0% of each run, Pallas kernels for 5% -> 5%
where the time goes in v4:
time: 110 us
  starting transfers between devices  65 us (59%)
  waiting for transfers between devices  33.2 us (30%)
  Pallas kernels  10.7 us (10%)
    ppermute x9, starting transfers between devices, swap(): return lax.ppermute(a, 'c', [(0, 1), (1, 0)])  26 us
    ppermute x16, starting transfers between devices, lead(): return lax.ppermute(a, ('y', 'z', 'x', 'c'), pairs)  18.5 us
    ppermute x12, starting transfers between devices, shift(): lax.ppermute(a, axis, [(i, (i + k * step) % size) for i in range(size)])  18.3 us
    pallas_call x23, Pallas kernels, call(): pl.pallas_call(kernel, out_shape=shapes if many else shapes[0], in_specs=...  10.7 us
    ppermute x12, waiting for transfers between devices, shift(): lax.ppermute(a, axis, [(i, (i + k * step) % size) for i in range(size)])  10.3 us
    ppermute x16, waiting for transfers between devices, lead(): return lax.ppermute(a, ('y', 'z', 'x', 'c'), pairs)  9.22 us
    ppermute x9, waiting for transfers between devices, swap(): return lax.ppermute(a, 'c', [(0, 1), (1, 0)])  5.06 us
    ppermute x2, waiting for transfers between devices, pair_x(): return lax.ppermute(a, 'x', [(x, partner(x)) for x in range(NX)])  4.49 us
  transfers between devices with their start and end apart: 41, of which 24 were waited for; matrix products, arithmetic and copies ran while one was open for 0% of the time, Pallas kernels for 5%

profile of v4, /device:TPU:1, one launch (start us, length us, event | category | flops | bytes accessed | tf_op | source)
XLA Modules:
  0.0 109.9 jit_solution(5270780821464881774)
XLA Ops:
  0.6 3.3 %collective-permute-start = (bf16[32,4096]{1,0:T(8,128)(2,1)}, bf16[32,4096]{1,0:T(8,128)(2,1)S(1)}, u32[]{:S(2)}, u32[]{:S(2)}) collective-permute-start(bf16[32,4096]{1,0:T(8,128)(2,1)} %cot_ref.1), channel_id=1, source_target_pairs={{0,1},{1,0},{2,3},{3,2},{4,5},{5,4},{6,7},{7,6},{8,9},{9,8},{10,11... | collective-permute-start | bytes 786440 | tf_op jit(solution)/shard_map/ppermute | solution.py:347
  6.2 2.6 %collective-permute-done.1.other_ref = f32[32,128]{1,0:T(8,128)S(1)} collective-permute-done((f32[32,128]{1,0:T(8,128)S(1)}, f32[32,128]{1,0:T(8,128)S(1)}, u32[]{:S(2)}, u32[]{:S(2)}) %collective-permute-start.1) | collective-permute-done | bytes 16416 | tf_op jit(solution)/shard_map/ppermute | solution.py:351
  10.9 1.9 %collective-permute-done.2.far_ref = f32[2,32,128]{2,1,0:T(8,128)S(1)} collective-permute-done((f32[2,32,128]{2,1,0:T(8,128)S(1)}, f32[2,32,128]{2,1,0:T(8,128)S(1)}, u32[]{:S(2)}, u32[]{:S(2)}) %collective-permute-start.2) | collective-permute-done | bytes 32800 | tf_op jit(solution)/shard_map/ppermute | solution.py:351
  13.5 2.2 %collective-permute-start.3 = (f32[16,1792]{1,0:T(8,128)S(1)}, f32[16,1792]{1,0:T(8,128)S(1)}, u32[]{:S(2)}, u32[]{:S(2)}) collective-permute-start(f32[16,1792]{1,0:T(8,128)S(1)} %get-tuple-element.41), channel_id=1, source_target_pairs={{0,128},{64,192},{128,0},{192,64},{1,129},{65,193},{129,1},{193,65... | collective-permute-start | bytes 344072 | tf_op jit(solution)/shard_map/ppermute | solution.py:380
  16.7 2.8 %collective-permute-done.4.after_ref.b_ref = f32[16,1792]{1,0:T(8,128)S(1)} collective-permute-done((f32[16,1792]{1,0:T(8,128)S(1)}, f32[16,1792]{1,0:T(8,128)S(1)}, u32[]{:S(2)}, u32[]{:S(2)}) %collective-permute-start.4) | collective-permute-done | bytes 114720 | tf_op jit(solution)/shard_map/ppermute | solution.py:380
  19.7 2.7 %collective-permute-start.11 = (bf16[64,1024]{1,0:T(8,128)(2,1)S(1)}, bf16[64,1024]{1,0:T(8,128)(2,1)S(1)}, u32[]{:S(2)}, u32[]{:S(2)}) collective-permute-start(bf16[64,1024]{1,0:T(8,128)(2,1)S(1)} %get-tuple-element.49), channel_id=1, source_target_pairs={{0,6},{2,0},{4,2},{6,4},{1,7},{3,1},{5,3},{7,5},{8,14},{10,8},{12,... | collective-permute-start | bytes 393224 | tf_op jit(solution)/shard_map/ppermute | solution.py:380
  22.5 3.0 %collective-permute-done.6.b_ref = f32[8,1792]{1,0:T(8,128)S(1)} collective-permute-done((f32[8,1792]{1,0:T(8,128)S(1)}, f32[8,1792]{1,0:T(8,128)S(1)}, u32[]{:S(2)}, u32[]{:S(2)}) %collective-permute-start.6) | collective-permute-done | bytes 57376 | tf_op jit(solution)/shard_map/ppermute | solution.py:375
  25.6 4.6 %collective-permute-start.9 = (f32[8,1792]{1,0:T(8,128)S(1)}, f32[8,1792]{1,0:T(8,128)S(1)}, u32[]{:S(2)}, u32[]{:S(2)}) collective-permute-start(f32[8,1792]{1,0:T(8,128)S(1)} %shard_map.66.own_ref), channel_id=1, source_target_pairs={{0,32},{8,40},{16,48},{24,56},{32,0},{40,8},{48,16},{56,24},{1,33}... | collective-permute-start | bytes 172040 | tf_op jit(solution)/shard_map/ppermute | solution.py:380
  30.1 2.4 %collective-permute-start.7 = (f32[8,1792]{1,0:T(8,128)S(1)}, f32[8,1792]{1,0:T(8,128)S(1)}, u32[]{:S(2)}, u32[]{:S(2)}) collective-permute-start(f32[8,1792]{1,0:T(8,128)S(1)} %shard_map.66.own_ref), channel_id=1, source_target_pairs={{0,16},{8,24},{16,32},{24,40},{32,48},{40,56},{48,0},{56,8},{1,17}... | collective-permute-start | bytes 172040 | tf_op jit(solution)/shard_map/ppermute | solution.py:380
  32.6 2.1 %collective-permute-done.8.b_ref = f32[8,1792]{1,0:T(8,128)S(1)} collective-permute-done((f32[8,1792]{1,0:T(8,128)S(1)}, f32[8,1792]{1,0:T(8,128)S(1)}, u32[]{:S(2)}, u32[]{:S(2)}) %collective-permute-start.8) | collective-permute-done | bytes 57376 | tf_op jit(solution)/shard_map/ppermute | solution.py:380
  37.0 1.8 %collective-permute-start.16 = (bf16[64,1024]{1,0:T(8,128)(2,1)S(1)}, bf16[64,1024]{1,0:T(8,128)(2,1)S(1)}, u32[]{:S(2)}, u32[]{:S(2)}) collective-permute-start(bf16[64,1024]{1,0:T(8,128)(2,1)S(1)} %get-tuple-element.50), channel_id=1, source_target_pairs={{0,4},{2,6},{4,0},{6,2},{1,5},{3,7},{5,1},{7,3},{8,12},{10,14},{12... | collective-permute-start | bytes 393224 | tf_op jit(solution)/shard_map/ppermute | solution.py:380
  39.9 2.0 %collective-permute-start.15 = (f32[16,1792]{1,0:T(8,128)S(1)}, f32[16,1792]{1,0:T(8,128)S(1)}, u32[]{:S(2)}, u32[]{:S(2)}) collective-permute-start(f32[16,1792]{1,0:T(8,128)S(1)} %shard_map.68.own_ref), channel_id=1, source_target_pairs={{0,128},{64,192},{128,0},{192,64},{1,129},{65,193},{129,1},{193,65... | collective-permute-start | bytes 344072 | tf_op jit(solution)/shard_map/ppermute | solution.py:380
  48.9 9.0 %collective-permute-start.17 = (f32[224,128]{1,0:T(8,128)S(1)}, f32[224,128]{1,0:T(8,128)S(1)}, u32[]{:S(2)}, u32[]{:S(2)}) collective-permute-start(f32[224,128]{1,0:T(8,128)S(1)} %get-tuple-element.51.a_ref), channel_id=1, source_target_pairs={{0,1},{1,0},{2,3},{3,2},{4,5},{5,4},{6,7},{7,6},{8,9},{9,8},{10,11... | collective-permute-start | bytes 344072 | tf_op jit(solution)/shard_map/ppermute | solution.py:347
  62.0 2.1 %collective-permute-done.20.c_ref = f32[224,128]{1,0:T(8,128)S(1)} collective-permute-done((f32[224,128]{1,0:T(8,128)S(1)}, f32[224,128]{1,0:T(8,128)S(1)}, u32[]{:S(2)}, u32[]{:S(2)}) %collective-permute-start.20) | collective-permute-done | bytes 114720 | tf_op jit(solution)/shard_map/ppermute | solution.py:358
  67.3 2.3 %collective-permute-start.23 = (f32[16,1024]{1,0:T(8,128)S(1)}, f32[16,1024]{1,0:T(8,128)S(1)}, u32[]{:S(2)}, u32[]{:S(2)}) collective-permute-start(f32[16,1024]{1,0:T(8,128)S(1)} %get-tuple-element.56), channel_id=1, source_target_pairs={{0,6},{1,193},{2,0},{3,195},{4,2},{5,197},{6,4},{7,199},{8,14},{9,... | collective-permute-start | bytes 196616 | tf_op jit(solution)/shard_map/ppermute | solution.py:358
  69.6 2.0 %collective-permute-start.24 = (f32[32,128]{1,0:T(8,128)S(1)}, f32[32,128]{1,0:T(8,128)S(1)}, u32[]{:S(2)}, u32[]{:S(2)}) collective-permute-start(f32[32,128]{1,0:T(8,128)S(1)} %get-tuple-element.57.own_ref), channel_id=1, source_target_pairs={{0,1},{1,0},{2,3},{3,2},{4,5},{5,4},{6,7},{7,6},{8,9},{9,8},{10,11... | collective-permute-start | bytes 49160 | tf_op jit(solution)/shard_map/ppermute | solution.py:347
  73.1 1.9 %shard_map.74.after_ref.inv_ref = f32[64,64]{1,0:T(8,128)S(1)} custom-call(f32[32,128]{1,0:T(8,128)S(1)} %get-tuple-element.57.own_ref, f32[32,128]{1,0:T(8,128)S(1)} %collective-permute-done.24.after_ref.other_ref, f32[16,1024]{1,0:T(8,128)S(1)} %shard_map.73.after_ref.a_ref), custom_call_target="tpu_custom_call" | custom-call | tf_op jit(solution)/shard_map/pallas_call | solution.py:121
  75.8 4.2 %collective-permute-start.28 = (f32[16,1024]{1,0:T(8,128)S(1)}, f32[16,1024]{1,0:T(8,128)S(1)}, u32[]{:S(2)}, u32[]{:S(2)}) collective-permute-start(f32[16,1024]{1,0:T(8,128)S(1)} %shard_map.75.after_ref.own_ref), channel_id=1, source_target_pairs={{0,6},{1,33},{2,0},{3,35},{4,2},{5,37},{6,4},{7,39},{8,14},{9,41},... | collective-permute-start | bytes 196616 | tf_op jit(solution)/shard_map/ppermute | solution.py:358
  83.2 2.6 %collective-permute-start.29 = (f32[32,128]{1,0:T(8,128)S(1)}, f32[32,128]{1,0:T(8,128)S(1)}, u32[]{:S(2)}, u32[]{:S(2)}) collective-permute-start(f32[32,128]{1,0:T(8,128)S(1)} %get-tuple-element.59.gram_ref), channel_id=1, source_target_pairs={{0,1},{1,0},{2,3},{3,2},{4,5},{5,4},{6,7},{7,6},{8,9},{9,8},{10,11... | collective-permute-start | bytes 49160 | tf_op jit(solution)/shard_map/ppermute | solution.py:347
  87.3 2.1 %collective-permute-start.31 = (f32[16,1024]{1,0:T(8,128)S(1)}, f32[16,1024]{1,0:T(8,128)S(1)}, u32[]{:S(2)}, u32[]{:S(2)}) collective-permute-start(f32[16,1024]{1,0:T(8,128)S(1)} %shard_map.77.own_ref), channel_id=1, source_target_pairs={{0,6},{1,193},{2,0},{3,195},{4,2},{5,197},{6,4},{7,199},{8,14},{9,... | collective-permute-start | bytes 196616 | tf_op jit(solution)/shard_map/ppermute | solution.py:358
  89.6 1.8 %collective-permute-done.32.c_ref = f32[16,1024]{1,0:T(8,128)S(1)} collective-permute-done((f32[16,1024]{1,0:T(8,128)S(1)}, f32[16,1024]{1,0:T(8,128)S(1)}, u32[]{:S(2)}, u32[]{:S(2)}) %collective-permute-start.32) | collective-permute-done | bytes 65568 | tf_op jit(solution)/shard_map/ppermute | solution.py:358
  94.4 1.9 %collective-permute-start.35 = (f32[64,1024]{1,0:T(8,128)S(1)}, f32[64,1024]{1,0:T(8,128)S(1)}, u32[]{:S(2)}, u32[]{:S(2)}) collective-permute-start(f32[64,1024]{1,0:T(8,128)S(1)} %shard_map.79.block_ref), channel_id=1, source_target_pairs={{0,64},{1,7},{2,66},{3,1},{4,68},{5,3},{6,70},{7,5},{8,72},{9,15},... | collective-permute-start | bytes 786440 | tf_op jit(solution)/shard_map/ppermute | solution.py:358
  96.5 6.2 %collective-permute-start.33 = (f32[64,64]{1,0:T(8,128)S(1)}, f32[64,64]{1,0:T(8,128)S(1)}, u32[]{:S(2)}, u32[]{:S(2)}) collective-permute-start(f32[64,64]{1,0:T(8,128)S(1)} %shard_map.78.own_ref), channel_id=1, source_target_pairs={{0,1},{1,0},{2,3},{3,2},{4,5},{5,4},{6,7},{7,6},{8,9},{9,8},{10,11... | collective-permute-start | bytes 49160 | tf_op jit(solution)/shard_map/ppermute | solution.py:347
  104.4 2.2 %collective-permute-start.39 = (f32[64,1024]{1,0:T(8,128)S(1)}, f32[64,1024]{1,0:T(8,128)S(1)}, u32[]{:S(2)}, u32[]{:S(2)}) collective-permute-start(f32[64,1024]{1,0:T(8,128)S(1)} %collective-permute-done.35.refs_2_), channel_id=1, source_target_pairs={{0,1},{1,0},{2,3},{3,2},{4,5},{5,4},{6,7},{7,6},{8,9},{9,8},{10,11... | collective-permute-start | bytes 786440 | tf_op jit(solution)/shard_map/ppermute | solution.py:347
  (81 shorter events, 39.3 us)
Async XLA Ops:
  13.4 6.2 %collective-permute-start.4 = (f32[16,1792]{1,0:T(8,128)S(1)}, f32[16,1792]{1,0:T(8,128)S(1)}, u32[]{:S(2)}, u32[]{:S(2)}) collective-permute-start(f32[16,1792]{1,0:T(8,128)S(1)} %get-tuple-element.42), channel_id=1, source_target_pairs={{0,64},{64,128},{128,192},{192,0},{1,65},{65,129},{129,193},{193,1... | collective-permute-start | bytes 344072 | tf_op jit(solution)/shard_map/ppermute | solution.py:380
  13.5 8.9 %collective-permute-start.3 = (f32[16,1792]{1,0:T(8,128)S(1)}, f32[16,1792]{1,0:T(8,128)S(1)}, u32[]{:S(2)}, u32[]{:S(2)}) collective-permute-start(f32[16,1792]{1,0:T(8,128)S(1)} %get-tuple-element.41), channel_id=1, source_target_pairs={{0,128},{64,192},{128,0},{192,64},{1,129},{65,193},{129,1},{193,65... | collective-permute-start | bytes 344072 | tf_op jit(solution)/shard_map/ppermute | solution.py:380
  15.7 6.7 %collective-permute-start.5 = (f32[16,1792]{1,0:T(8,128)S(1)}, f32[16,1792]{1,0:T(8,128)S(1)}, u32[]{:S(2)}, u32[]{:S(2)}) collective-permute-start(f32[16,1792]{1,0:T(8,128)S(1)} %get-tuple-element.43), channel_id=1, source_target_pairs={{0,192},{64,0},{128,64},{192,128},{1,193},{65,1},{129,65},{193,129... | collective-permute-start | bytes 344072 | tf_op jit(solution)/shard_map/ppermute | solution.py:380
  19.6 15.9 %collective-permute-start.10 = (bf16[64,1024]{1,0:T(8,128)(2,1)S(1)}, bf16[64,1024]{1,0:T(8,128)(2,1)S(1)}, u32[]{:S(2)}, u32[]{:S(2)}) collective-permute-start(bf16[64,1024]{1,0:T(8,128)(2,1)S(1)} %get-tuple-element.48), channel_id=1, source_target_pairs={{0,2},{2,4},{4,6},{6,0},{1,3},{3,5},{5,7},{7,1},{8,10},{10,12},{12... | collective-permute-start | bytes 393224 | tf_op jit(solution)/shard_map/ppermute | solution.py:380
  19.7 15.8 %collective-permute-start.11 = (bf16[64,1024]{1,0:T(8,128)(2,1)S(1)}, bf16[64,1024]{1,0:T(8,128)(2,1)S(1)}, u32[]{:S(2)}, u32[]{:S(2)}) collective-permute-start(bf16[64,1024]{1,0:T(8,128)(2,1)S(1)} %get-tuple-element.49), channel_id=1, source_target_pairs={{0,6},{2,0},{4,2},{6,4},{1,7},{3,1},{5,3},{7,5},{8,14},{10,8},{12,... | collective-permute-start | bytes 393224 | tf_op jit(solution)/shard_map/ppermute | solution.py:380
  25.6 7.0 %collective-permute-start.9 = (f32[8,1792]{1,0:T(8,128)S(1)}, f32[8,1792]{1,0:T(8,128)S(1)}, u32[]{:S(2)}, u32[]{:S(2)}) collective-permute-start(f32[8,1792]{1,0:T(8,128)S(1)} %shard_map.66.own_ref), channel_id=1, source_target_pairs={{0,32},{8,40},{16,48},{24,56},{32,0},{40,8},{48,16},{56,24},{1,33}... | collective-permute-start | bytes 172040 | tf_op jit(solution)/shard_map/ppermute | solution.py:380
  30.1 5.4 %collective-permute-start.7 = (f32[8,1792]{1,0:T(8,128)S(1)}, f32[8,1792]{1,0:T(8,128)S(1)}, u32[]{:S(2)}, u32[]{:S(2)}) collective-permute-start(f32[8,1792]{1,0:T(8,128)S(1)} %shard_map.66.own_ref), channel_id=1, source_target_pairs={{0,16},{8,24},{16,32},{24,40},{32,48},{40,56},{48,0},{56,8},{1,17}... | collective-permute-start | bytes 172040 | tf_op jit(solution)/shard_map/ppermute | solution.py:380
  37.0 6.4 %collective-permute-start.16 = (bf16[64,1024]{1,0:T(8,128)(2,1)S(1)}, bf16[64,1024]{1,0:T(8,128)(2,1)S(1)}, u32[]{:S(2)}, u32[]{:S(2)}) collective-permute-start(bf16[64,1024]{1,0:T(8,128)(2,1)S(1)} %get-tuple-element.50), channel_id=1, source_target_pairs={{0,4},{2,6},{4,0},{6,2},{1,5},{3,7},{5,1},{7,3},{8,12},{10,14},{12... | collective-permute-start | bytes 393224 | tf_op jit(solution)/shard_map/ppermute | solution.py:380
  39.9 5.2 %collective-permute-start.15 = (f32[16,1792]{1,0:T(8,128)S(1)}, f32[16,1792]{1,0:T(8,128)S(1)}, u32[]{:S(2)}, u32[]{:S(2)}) collective-permute-start(f32[16,1792]{1,0:T(8,128)S(1)} %shard_map.68.own_ref), channel_id=1, source_target_pairs={{0,128},{64,192},{128,0},{192,64},{1,129},{65,193},{129,1},{193,65... | collective-permute-start | bytes 344072 | tf_op jit(solution)/shard_map/ppermute | solution.py:380
  43.0 4.9 %collective-permute-start.13 = (f32[16,1792]{1,0:T(8,128)S(1)}, f32[16,1792]{1,0:T(8,128)S(1)}, u32[]{:S(2)}, u32[]{:S(2)}) collective-permute-start(f32[16,1792]{1,0:T(8,128)S(1)} %shard_map.68.own_ref), channel_id=1, source_target_pairs={{0,64},{64,128},{128,192},{192,0},{1,65},{65,129},{129,193},{193,1... | collective-permute-start | bytes 344072 | tf_op jit(solution)/shard_map/ppermute | solution.py:380
  48.9 10.0 %collective-permute-start.17 = (f32[224,128]{1,0:T(8,128)S(1)}, f32[224,128]{1,0:T(8,128)S(1)}, u32[]{:S(2)}, u32[]{:S(2)}) collective-permute-start(f32[224,128]{1,0:T(8,128)S(1)} %get-tuple-element.51.a_ref), channel_id=1, source_target_pairs={{0,1},{1,0},{2,3},{3,2},{4,5},{5,4},{6,7},{7,6},{8,9},{9,8},{10,11... | collective-permute-start | bytes 344072 | tf_op jit(solution)/shard_map/ppermute | solution.py:347
  58.9 5.2 %collective-permute-start.20 = (f32[224,128]{1,0:T(8,128)S(1)}, f32[224,128]{1,0:T(8,128)S(1)}, u32[]{:S(2)}, u32[]{:S(2)}) collective-permute-start(f32[224,128]{1,0:T(8,128)S(1)} %shard_map.70.own_ref), channel_id=1, source_target_pairs={{0,192},{1,5},{2,194},{3,7},{4,196},{5,1},{6,198},{7,3},{8,200},{9... | collective-permute-start | bytes 344072 | tf_op jit(solution)/shard_map/ppermute | solution.py:358
  60.4 5.3 %collective-permute-start.19 = (f32[224,128]{1,0:T(8,128)S(1)}, f32[224,128]{1,0:T(8,128)S(1)}, u32[]{:S(2)}, u32[]{:S(2)}) collective-permute-start(f32[224,128]{1,0:T(8,128)S(1)} %shard_map.70.own_ref), channel_id=1, source_target_pairs={{0,64},{1,7},{2,66},{3,1},{4,68},{5,3},{6,70},{7,5},{8,72},{9,15},... | collective-permute-start | bytes 344072 | tf_op jit(solution)/shard_map/ppermute | solution.py:358
  66.7 5.7 %collective-permute-start.21 = (f32[16,1024]{1,0:T(8,128)S(1)}, f32[16,1024]{1,0:T(8,128)S(1)}, u32[]{:S(2)}, u32[]{:S(2)}) collective-permute-start(f32[16,1024]{1,0:T(8,128)S(1)} %get-tuple-element.54), channel_id=1, source_target_pairs={{0,4},{1,129},{2,6},{3,131},{4,0},{5,133},{6,2},{7,135},{8,12},{9,... | collective-permute-start | bytes 196616 | tf_op jit(solution)/shard_map/ppermute | solution.py:358
  66.9 5.6 %collective-permute-start.22 = (f32[16,1024]{1,0:T(8,128)S(1)}, f32[16,1024]{1,0:T(8,128)S(1)}, u32[]{:S(2)}, u32[]{:S(2)}) collective-permute-start(f32[16,1024]{1,0:T(8,128)S(1)} %get-tuple-element.55), channel_id=1, source_target_pairs={{0,2},{1,65},{2,4},{3,67},{4,6},{5,69},{6,0},{7,71},{8,10},{9,73},... | collective-permute-start | bytes 196616 | tf_op jit(solution)/shard_map/ppermute | solution.py:358
  67.3 5.2 %collective-permute-start.23 = (f32[16,1024]{1,0:T(8,128)S(1)}, f32[16,1024]{1,0:T(8,128)S(1)}, u32[]{:S(2)}, u32[]{:S(2)}) collective-permute-start(f32[16,1024]{1,0:T(8,128)S(1)} %get-tuple-element.56), channel_id=1, source_target_pairs={{0,6},{1,193},{2,0},{3,195},{4,2},{5,197},{6,4},{7,199},{8,14},{9,... | collective-permute-start | bytes 196616 | tf_op jit(solution)/shard_map/ppermute | solution.py:358
  75.8 10.9 %collective-permute-start.28 = (f32[16,1024]{1,0:T(8,128)S(1)}, f32[16,1024]{1,0:T(8,128)S(1)}, u32[]{:S(2)}, u32[]{:S(2)}) collective-permute-start(f32[16,1024]{1,0:T(8,128)S(1)} %shard_map.75.after_ref.own_ref), channel_id=1, source_target_pairs={{0,6},{1,33},{2,0},{3,35},{4,2},{5,37},{6,4},{7,39},{8,14},{9,41},... | collective-permute-start | bytes 196616 | tf_op jit(solution)/shard_map/ppermute | solution.py:358
  79.9 6.7 %collective-permute-start.27 = (f32[16,1024]{1,0:T(8,128)S(1)}, f32[16,1024]{1,0:T(8,128)S(1)}, u32[]{:S(2)}, u32[]{:S(2)}) collective-permute-start(f32[16,1024]{1,0:T(8,128)S(1)} %shard_map.75.after_ref.own_ref), channel_id=1, source_target_pairs={{0,2},{1,49},{2,4},{3,51},{4,6},{5,53},{6,0},{7,55},{8,10},{9,57},... | collective-permute-start | bytes 196616 | tf_op jit(solution)/shard_map/ppermute | solution.py:358
  80.7 5.9 %collective-permute-start.26 = (f32[16,1024]{1,0:T(8,128)S(1)}, f32[16,1024]{1,0:T(8,128)S(1)}, u32[]{:S(2)}, u32[]{:S(2)}) collective-permute-start(f32[16,1024]{1,0:T(8,128)S(1)} %shard_map.75.after_ref.own_ref), channel_id=1, source_target_pairs={{0,6},{1,17},{2,0},{3,19},{4,2},{5,21},{6,4},{7,23},{8,14},{9,25},... | collective-permute-start | bytes 196616 | tf_op jit(solution)/shard_map/ppermute | solution.py:358
  87.3 5.0 %collective-permute-start.31 = (f32[16,1024]{1,0:T(8,128)S(1)}, f32[16,1024]{1,0:T(8,128)S(1)}, u32[]{:S(2)}, u32[]{:S(2)}) collective-permute-start(f32[16,1024]{1,0:T(8,128)S(1)} %shard_map.77.own_ref), channel_id=1, source_target_pairs={{0,6},{1,193},{2,0},{3,195},{4,2},{5,197},{6,4},{7,199},{8,14},{9,... | collective-permute-start | bytes 196616 | tf_op jit(solution)/shard_map/ppermute | solution.py:358
  93.7 10.4 %collective-permute-start.36 = (f32[64,1024]{1,0:T(8,128)S(1)}, f32[64,1024]{1,0:T(8,128)S(1)}, u32[]{:S(2)}, u32[]{:S(2)}) collective-permute-start(f32[64,1024]{1,0:T(8,128)S(1)} %shard_map.79.block_ref), channel_id=1, source_target_pairs={{0,192},{1,5},{2,194},{3,7},{4,196},{5,1},{6,198},{7,3},{8,200},{9... | collective-permute-start | bytes 786440 | tf_op jit(solution)/shard_map/ppermute | solution.py:358
  94.4 10.0 %collective-permute-start.35 = (f32[64,1024]{1,0:T(8,128)S(1)}, f32[64,1024]{1,0:T(8,128)S(1)}, u32[]{:S(2)}, u32[]{:S(2)}) collective-permute-start(f32[64,1024]{1,0:T(8,128)S(1)} %shard_map.79.block_ref), channel_id=1, source_target_pairs={{0,64},{1,7},{2,66},{3,1},{4,68},{5,3},{6,70},{7,5},{8,72},{9,15},... | collective-permute-start | bytes 786440 | tf_op jit(solution)/shard_map/ppermute | solution.py:358
  96.2 10.3 %collective-permute-start.34 = (f32[64,1024]{1,0:T(8,128)S(1)}, f32[64,1024]{1,0:T(8,128)S(1)}, u32[]{:S(2)}, u32[]{:S(2)}) collective-permute-start(f32[64,1024]{1,0:T(8,128)S(1)} %shard_map.79.block_ref), channel_id=1, source_target_pairs={{0,192},{1,3},{2,194},{3,5},{4,196},{5,7},{6,198},{7,1},{8,200},{9... | collective-permute-start | bytes 786440 | tf_op jit(solution)/shard_map/ppermute | solution.py:358
  96.5 7.1 %collective-permute-start.33 = (f32[64,64]{1,0:T(8,128)S(1)}, f32[64,64]{1,0:T(8,128)S(1)}, u32[]{:S(2)}, u32[]{:S(2)}) collective-permute-start(f32[64,64]{1,0:T(8,128)S(1)} %shard_map.78.own_ref), channel_id=1, source_target_pairs={{0,1},{1,0},{2,3},{3,2},{4,5},{5,4},{6,7},{7,6},{8,9},{9,8},{10,11... | collective-permute-start | bytes 49160 | tf_op jit(solution)/shard_map/ppermute | solution.py:347
  (17 other events, 60.9 us)

commit v5 on v4

--- a/solution.py
+++ b/solution.py
@@ -358,13 +358,21 @@
     return lax.ppermute(a, ("y", "z", "x", "c"), pairs)
 
 
+def one_hop(first, second, k):
+    axis, hop = {1: (first, 1), 3: (first, -1), 2: (second, 1)}[k]
+    return lambda y, z, x: ((y + hop * (axis == "y")) % NY, (z + hop * (axis == "z")) % NZ, (x + hop * (axis == "x")) % NX)
+
+
 def lead_shift(a, axis, k):
-    hop = 1 if k == 3 else -1
     if axis == "x":
-        return lead(a, lambda y, z, x: (y, z, (x + k) % NX), lambda y, z, x: ((y + hop) % NY, z, x))
+        return lead(a, lambda y, z, x: (y, z, (x + k) % NX), one_hop("y", "z", k))
     if axis == "y":
-        return lead(a, lambda y, z, x: ((y + k) % NY, z, x), lambda y, z, x: (y, z, (x + k) % NX))
-    return lead(a, lambda y, z, x: (y, (z + 2 * k) % NZ, x), lambda y, z, x: (y, z, (x + hop) % NX))
+        return lead(a, lambda y, z, x: ((y + k) % NY, z, x), one_hop("x", "z", k))
+    return lead(a, lambda y, z, x: (y, (z + 2 * k) % NZ, x), one_hop("x", "y", k))
+
+
+def both_shift(a, axis, k):
+    return lead(a, lambda y, z, x: ((y + k) % NY, z, x), lambda y, z, x: (y, z, (x + k) % NX))
 
 
 def lead_swap_z(a):
@@ -437,7 +445,7 @@
     s = call(add_after_kernel, piece, s, lead_swap_z(s), inverse, unread=(2,))
     b3, gram = call(basis_kernel, [((3 * RANK, FB), bf16), small], inverse, p3, s, unread=(2,))
     s = call(sum_z_gram_kernel, piece, *share(s, "z", lead_shift), gram, swap(gram), scratch=[slots])
-    quarters, square, whole = share(s, "y", lead_shift), ((RANK, RANK), f32), ((RANK, CB), f32)
+    quarters, square, whole = share(s, "y", both_shift), ((RANK, RANK), f32), ((RANK, CB), f32)
     s = call(block_kernel, whole, *quarters)
     second = call(second_kernel, square, *quarters, scratch=[pltpu.VMEM((4, RANK // NY, 4 * RANK), f32)])
     total, second, own = call(total_kernel, [square, square, whole], second, swap(second), inverse, s)

time: 110 us -> 111 us (level); the launches traced: 110 us -> 109 us
  starting transfers between devices: 65 us -> 57.3 us
  waiting for transfers between devices: 33.2 us -> 39.8 us
    ppermute x16, waiting for transfers between devices: 9.22 us -> 16.2 us  [lead(): return lax.ppermute(a, ('y', 'z', 'x', 'c'), pairs)]
    ppermute x9, starting transfers between devices: 26 us -> 19.3 us  [swap(): return lax.ppermute(a, 'c', [(0, 1), (1, 0)])]
    ppermute x16, starting transfers between devices: 18.5 us -> 17.3 us  [lead(): return lax.ppermute(a, ('y', 'z', 'x', 'c'), pairs)]
  transfers between devices with their start and end apart: 41 -> 41, of which waited for: 24 -> 27; matrix products, arithmetic and copies ran while one was open for 0% -> 0% of each run, Pallas kernels for 5% -> 5%
where the time goes in v5:
time: 111 us; the launch traced here: 109 us
  starting transfers between devices  57.3 us (52%)
  waiting for transfers between devices  39.8 us (36%)
  Pallas kernels  10.7 us (10%)
    ppermute x9, starting transfers between devices, swap(): return lax.ppermute(a, 'c', [(0, 1), (1, 0)])  19.3 us
    ppermute x12, starting transfers between devices, shift(): lax.ppermute(a, axis, [(i, (i + k * step) % size) for i in range(size)])  18.3 us
    ppermute x16, starting transfers between devices, lead(): return lax.ppermute(a, ('y', 'z', 'x', 'c'), pairs)  17.3 us
    ppermute x16, waiting for transfers between devices, lead(): return lax.ppermute(a, ('y', 'z', 'x', 'c'), pairs)  16.2 us
    pallas_call x23, Pallas kernels, call(): pl.pallas_call(kernel, out_shape=shapes if many else shapes[0], in_specs=...  10.7 us
    ppermute x12, waiting for transfers between devices, shift(): lax.ppermute(a, axis, [(i, (i + k * step) % size) for i in range(size)])  10.3 us
    ppermute x9, waiting for transfers between devices, swap(): return lax.ppermute(a, 'c', [(0, 1), (1, 0)])  4.69 us
    ppermute x2, waiting for transfers between devices, pair_x(): return lax.ppermute(a, 'x', [(x, partner(x)) for x in range(NX)])  4.49 us
  transfers between devices with their start and end apart: 41, of which 27 were waited for; matrix products, arithmetic and copies ran while one was open for 0% of the time, Pallas kernels for 5%

profile of v5, /device:TPU:1, one launch (start us, length us, event | category | flops | bytes accessed | tf_op | source)
XLA Modules:
  0.0 108.8 jit_solution(18340620827165691395)
XLA Ops:
  0.6 3.3 %collective-permute-start = (bf16[32,4096]{1,0:T(8,128)(2,1)}, bf16[32,4096]{1,0:T(8,128)(2,1)S(1)}, u32[]{:S(2)}, u32[]{:S(2)}) collective-permute-start(bf16[32,4096]{1,0:T(8,128)(2,1)} %cot_ref.1), channel_id=1, source_target_pairs={{0,1},{1,0},{2,3},{3,2},{4,5},{5,4},{6,7},{7,6},{8,9},{9,8},{10,11... | collective-permute-start | bytes 786440 | tf_op jit(solution)/shard_map/ppermute | solution.py:347
  6.2 2.6 %collective-permute-done.1.other_ref = f32[32,128]{1,0:T(8,128)S(1)} collective-permute-done((f32[32,128]{1,0:T(8,128)S(1)}, f32[32,128]{1,0:T(8,128)S(1)}, u32[]{:S(2)}, u32[]{:S(2)}) %collective-permute-start.1) | collective-permute-done | bytes 16416 | tf_op jit(solution)/shard_map/ppermute | solution.py:351
  10.9 1.9 %collective-permute-done.2.far_ref = f32[2,32,128]{2,1,0:T(8,128)S(1)} collective-permute-done((f32[2,32,128]{2,1,0:T(8,128)S(1)}, f32[2,32,128]{2,1,0:T(8,128)S(1)}, u32[]{:S(2)}, u32[]{:S(2)}) %collective-permute-start.2) | collective-permute-done | bytes 32800 | tf_op jit(solution)/shard_map/ppermute | solution.py:351
  13.5 2.2 %collective-permute-start.3 = (f32[16,1792]{1,0:T(8,128)S(1)}, f32[16,1792]{1,0:T(8,128)S(1)}, u32[]{:S(2)}, u32[]{:S(2)}) collective-permute-start(f32[16,1792]{1,0:T(8,128)S(1)} %get-tuple-element.41), channel_id=1, source_target_pairs={{0,128},{64,192},{128,0},{192,64},{1,129},{65,193},{129,1},{193,65... | collective-permute-start | bytes 344072 | tf_op jit(solution)/shard_map/ppermute | solution.py:388
  16.7 2.8 %collective-permute-done.4.after_ref.b_ref = f32[16,1792]{1,0:T(8,128)S(1)} collective-permute-done((f32[16,1792]{1,0:T(8,128)S(1)}, f32[16,1792]{1,0:T(8,128)S(1)}, u32[]{:S(2)}, u32[]{:S(2)}) %collective-permute-start.4) | collective-permute-done | bytes 114720 | tf_op jit(solution)/shard_map/ppermute | solution.py:388
  19.7 2.7 %collective-permute-start.11 = (bf16[64,1024]{1,0:T(8,128)(2,1)S(1)}, bf16[64,1024]{1,0:T(8,128)(2,1)S(1)}, u32[]{:S(2)}, u32[]{:S(2)}) collective-permute-start(bf16[64,1024]{1,0:T(8,128)(2,1)S(1)} %get-tuple-element.49), channel_id=1, source_target_pairs={{0,6},{2,0},{4,2},{6,4},{1,7},{3,1},{5,3},{7,5},{8,14},{10,8},{12,... | collective-permute-start | bytes 393224 | tf_op jit(solution)/shard_map/ppermute | solution.py:388
  22.5 3.0 %collective-permute-done.6.b_ref = f32[8,1792]{1,0:T(8,128)S(1)} collective-permute-done((f32[8,1792]{1,0:T(8,128)S(1)}, f32[8,1792]{1,0:T(8,128)S(1)}, u32[]{:S(2)}, u32[]{:S(2)}) %collective-permute-start.6) | collective-permute-done | bytes 57376 | tf_op jit(solution)/shard_map/ppermute | solution.py:383
  25.6 4.6 %collective-permute-start.9 = (f32[8,1792]{1,0:T(8,128)S(1)}, f32[8,1792]{1,0:T(8,128)S(1)}, u32[]{:S(2)}, u32[]{:S(2)}) collective-permute-start(f32[8,1792]{1,0:T(8,128)S(1)} %shard_map.66.own_ref), channel_id=1, source_target_pairs={{0,32},{8,40},{16,48},{24,56},{32,0},{40,8},{48,16},{56,24},{1,33}... | collective-permute-start | bytes 172040 | tf_op jit(solution)/shard_map/ppermute | solution.py:388
  30.1 2.4 %collective-permute-start.7 = (f32[8,1792]{1,0:T(8,128)S(1)}, f32[8,1792]{1,0:T(8,128)S(1)}, u32[]{:S(2)}, u32[]{:S(2)}) collective-permute-start(f32[8,1792]{1,0:T(8,128)S(1)} %shard_map.66.own_ref), channel_id=1, source_target_pairs={{0,16},{8,24},{16,32},{24,40},{32,48},{40,56},{48,0},{56,8},{1,17}... | collective-permute-start | bytes 172040 | tf_op jit(solution)/shard_map/ppermute | solution.py:388
  32.6 2.1 %collective-permute-done.8.b_ref = f32[8,1792]{1,0:T(8,128)S(1)} collective-permute-done((f32[8,1792]{1,0:T(8,128)S(1)}, f32[8,1792]{1,0:T(8,128)S(1)}, u32[]{:S(2)}, u32[]{:S(2)}) %collective-permute-start.8) | collective-permute-done | bytes 57376 | tf_op jit(solution)/shard_map/ppermute | solution.py:388
  37.0 1.8 %collective-permute-start.16 = (bf16[64,1024]{1,0:T(8,128)(2,1)S(1)}, bf16[64,1024]{1,0:T(8,128)(2,1)S(1)}, u32[]{:S(2)}, u32[]{:S(2)}) collective-permute-start(bf16[64,1024]{1,0:T(8,128)(2,1)S(1)} %get-tuple-element.50), channel_id=1, source_target_pairs={{0,4},{2,6},{4,0},{6,2},{1,5},{3,7},{5,1},{7,3},{8,12},{10,14},{12... | collective-permute-start | bytes 393224 | tf_op jit(solution)/shard_map/ppermute | solution.py:388
  39.9 2.0 %collective-permute-start.15 = (f32[16,1792]{1,0:T(8,128)S(1)}, f32[16,1792]{1,0:T(8,128)S(1)}, u32[]{:S(2)}, u32[]{:S(2)}) collective-permute-start(f32[16,1792]{1,0:T(8,128)S(1)} %shard_map.68.own_ref), channel_id=1, source_target_pairs={{0,128},{64,192},{128,0},{192,64},{1,129},{65,193},{129,1},{193,65... | collective-permute-start | bytes 344072 | tf_op jit(solution)/shard_map/ppermute | solution.py:388
  43.4 1.7 %collective-permute-done.15.c_ref = f32[16,1792]{1,0:T(8,128)S(1)} collective-permute-done((f32[16,1792]{1,0:T(8,128)S(1)}, f32[16,1792]{1,0:T(8,128)S(1)}, u32[]{:S(2)}, u32[]{:S(2)}) %collective-permute-start.15) | collective-permute-done | bytes 114720 | tf_op jit(solution)/shard_map/ppermute | solution.py:388
  48.9 9.0 %collective-permute-start.17 = (f32[224,128]{1,0:T(8,128)S(1)}, f32[224,128]{1,0:T(8,128)S(1)}, u32[]{:S(2)}, u32[]{:S(2)}) collective-permute-start(f32[224,128]{1,0:T(8,128)S(1)} %get-tuple-element.51.a_ref), channel_id=1, source_target_pairs={{0,1},{1,0},{2,3},{3,2},{4,5},{5,4},{6,7},{7,6},{8,9},{9,8},{10,11... | collective-permute-start | bytes 344072 | tf_op jit(solution)/shard_map/ppermute | solution.py:347
  62.0 2.1 %collective-permute-done.20.c_ref = f32[224,128]{1,0:T(8,128)S(1)} collective-permute-done((f32[224,128]{1,0:T(8,128)S(1)}, f32[224,128]{1,0:T(8,128)S(1)}, u32[]{:S(2)}, u32[]{:S(2)}) %collective-permute-start.20) | collective-permute-done | bytes 114720 | tf_op jit(solution)/shard_map/ppermute | solution.py:358
  67.2 2.3 %collective-permute-start.23 = (f32[16,1024]{1,0:T(8,128)S(1)}, f32[16,1024]{1,0:T(8,128)S(1)}, u32[]{:S(2)}, u32[]{:S(2)}) collective-permute-start(f32[16,1024]{1,0:T(8,128)S(1)} %get-tuple-element.56), channel_id=1, source_target_pairs={{0,6},{1,193},{2,0},{3,195},{4,2},{5,197},{6,4},{7,199},{8,14},{9,... | collective-permute-start | bytes 196616 | tf_op jit(solution)/shard_map/ppermute | solution.py:358
  69.6 2.4 %collective-permute-start.24 = (f32[32,128]{1,0:T(8,128)S(1)}, f32[32,128]{1,0:T(8,128)S(1)}, u32[]{:S(2)}, u32[]{:S(2)}) collective-permute-start(f32[32,128]{1,0:T(8,128)S(1)} %get-tuple-element.57.own_ref), channel_id=1, source_target_pairs={{0,1},{1,0},{2,3},{3,2},{4,5},{5,4},{6,7},{7,6},{8,9},{9,8},{10,11... | collective-permute-start | bytes 49160 | tf_op jit(solution)/shard_map/ppermute | solution.py:347
  73.4 1.9 %shard_map.74.after_ref.inv_ref = f32[64,64]{1,0:T(8,128)S(1)} custom-call(f32[32,128]{1,0:T(8,128)S(1)} %get-tuple-element.57.own_ref, f32[32,128]{1,0:T(8,128)S(1)} %collective-permute-done.24.after_ref.other_ref, f32[16,1024]{1,0:T(8,128)S(1)} %shard_map.73.after_ref.a_ref), custom_call_target="tpu_custom_call" | custom-call | tf_op jit(solution)/shard_map/pallas_call | solution.py:121
  76.1 3.4 %collective-permute-start.28 = (f32[16,1024]{1,0:T(8,128)S(1)}, f32[16,1024]{1,0:T(8,128)S(1)}, u32[]{:S(2)}, u32[]{:S(2)}) collective-permute-start(f32[16,1024]{1,0:T(8,128)S(1)} %shard_map.75.after_ref.own_ref), channel_id=1, source_target_pairs={{0,64},{1,33},{2,66},{3,35},{4,68},{5,37},{6,70},{7,39},{8,72},{9,... | collective-permute-start | bytes 196616 | tf_op jit(solution)/shard_map/ppermute | solution.py:358
  79.5 2.5 %collective-permute-start.27 = (f32[16,1024]{1,0:T(8,128)S(1)}, f32[16,1024]{1,0:T(8,128)S(1)}, u32[]{:S(2)}, u32[]{:S(2)}) collective-permute-start(f32[16,1024]{1,0:T(8,128)S(1)} %shard_map.75.after_ref.own_ref), channel_id=1, source_target_pairs={{0,6},{1,49},{2,0},{3,51},{4,2},{5,53},{6,4},{7,55},{8,14},{9,57},... | collective-permute-start | bytes 196616 | tf_op jit(solution)/shard_map/ppermute | solution.py:358
  84.7 2.5 %collective-permute-done.26.a_ref = f32[16,1024]{1,0:T(8,128)S(1)} collective-permute-done((f32[16,1024]{1,0:T(8,128)S(1)}, f32[16,1024]{1,0:T(8,128)S(1)}, u32[]{:S(2)}, u32[]{:S(2)}) %collective-permute-start.26) | collective-permute-done | bytes 65568 | tf_op jit(solution)/shard_map/ppermute | solution.py:358
  88.0 2.3 %collective-permute-start.31 = (f32[16,1024]{1,0:T(8,128)S(1)}, f32[16,1024]{1,0:T(8,128)S(1)}, u32[]{:S(2)}, u32[]{:S(2)}) collective-permute-start(f32[16,1024]{1,0:T(8,128)S(1)} %shard_map.77.own_ref), channel_id=1, source_target_pairs={{0,6},{1,193},{2,0},{3,195},{4,2},{5,197},{6,4},{7,199},{8,14},{9,... | collective-permute-start | bytes 196616 | tf_op jit(solution)/shard_map/ppermute | solution.py:358
  90.4 1.9 %collective-permute-done.32.c_ref = f32[16,1024]{1,0:T(8,128)S(1)} collective-permute-done((f32[16,1024]{1,0:T(8,128)S(1)}, f32[16,1024]{1,0:T(8,128)S(1)}, u32[]{:S(2)}, u32[]{:S(2)}) %collective-permute-start.32) | collective-permute-done | bytes 65568 | tf_op jit(solution)/shard_map/ppermute | solution.py:358
  92.3 2.7 %collective-permute-done.30.a_ref = f32[16,1024]{1,0:T(8,128)S(1)} collective-permute-done((f32[16,1024]{1,0:T(8,128)S(1)}, f32[16,1024]{1,0:T(8,128)S(1)}, u32[]{:S(2)}, u32[]{:S(2)}) %collective-permute-start.30) | collective-permute-done | bytes 65568 | tf_op jit(solution)/shard_map/ppermute | solution.py:358
  (81 shorter events, 41.7 us)
Async XLA Ops:
  13.4 6.2 %collective-permute-start.4 = (f32[16,1792]{1,0:T(8,128)S(1)}, f32[16,1792]{1,0:T(8,128)S(1)}, u32[]{:S(2)}, u32[]{:S(2)}) collective-permute-start(f32[16,1792]{1,0:T(8,128)S(1)} %get-tuple-element.42), channel_id=1, source_target_pairs={{0,64},{64,128},{128,192},{192,0},{1,65},{65,129},{129,193},{193,1... | collective-permute-start | bytes 344072 | tf_op jit(solution)/shard_map/ppermute | solution.py:388
  13.5 8.9 %collective-permute-start.3 = (f32[16,1792]{1,0:T(8,128)S(1)}, f32[16,1792]{1,0:T(8,128)S(1)}, u32[]{:S(2)}, u32[]{:S(2)}) collective-permute-start(f32[16,1792]{1,0:T(8,128)S(1)} %get-tuple-element.41), channel_id=1, source_target_pairs={{0,128},{64,192},{128,0},{192,64},{1,129},{65,193},{129,1},{193,65... | collective-permute-start | bytes 344072 | tf_op jit(solution)/shard_map/ppermute | solution.py:388
  15.7 6.7 %collective-permute-start.5 = (f32[16,1792]{1,0:T(8,128)S(1)}, f32[16,1792]{1,0:T(8,128)S(1)}, u32[]{:S(2)}, u32[]{:S(2)}) collective-permute-start(f32[16,1792]{1,0:T(8,128)S(1)} %get-tuple-element.43), channel_id=1, source_target_pairs={{0,192},{64,0},{128,64},{192,128},{1,193},{65,1},{129,65},{193,129... | collective-permute-start | bytes 344072 | tf_op jit(solution)/shard_map/ppermute | solution.py:388
  19.6 15.9 %collective-permute-start.10 = (bf16[64,1024]{1,0:T(8,128)(2,1)S(1)}, bf16[64,1024]{1,0:T(8,128)(2,1)S(1)}, u32[]{:S(2)}, u32[]{:S(2)}) collective-permute-start(bf16[64,1024]{1,0:T(8,128)(2,1)S(1)} %get-tuple-element.48), channel_id=1, source_target_pairs={{0,2},{2,4},{4,6},{6,0},{1,3},{3,5},{5,7},{7,1},{8,10},{10,12},{12... | collective-permute-start | bytes 393224 | tf_op jit(solution)/shard_map/ppermute | solution.py:388
  19.7 15.8 %collective-permute-start.11 = (bf16[64,1024]{1,0:T(8,128)(2,1)S(1)}, bf16[64,1024]{1,0:T(8,128)(2,1)S(1)}, u32[]{:S(2)}, u32[]{:S(2)}) collective-permute-start(bf16[64,1024]{1,0:T(8,128)(2,1)S(1)} %get-tuple-element.49), channel_id=1, source_target_pairs={{0,6},{2,0},{4,2},{6,4},{1,7},{3,1},{5,3},{7,5},{8,14},{10,8},{12,... | collective-permute-start | bytes 393224 | tf_op jit(solution)/shard_map/ppermute | solution.py:388
  25.6 7.0 %collective-permute-start.9 = (f32[8,1792]{1,0:T(8,128)S(1)}, f32[8,1792]{1,0:T(8,128)S(1)}, u32[]{:S(2)}, u32[]{:S(2)}) collective-permute-start(f32[8,1792]{1,0:T(8,128)S(1)} %shard_map.66.own_ref), channel_id=1, source_target_pairs={{0,32},{8,40},{16,48},{24,56},{32,0},{40,8},{48,16},{56,24},{1,33}... | collective-permute-start | bytes 172040 | tf_op jit(solution)/shard_map/ppermute | solution.py:388
  30.1 5.4 %collective-permute-start.7 = (f32[8,1792]{1,0:T(8,128)S(1)}, f32[8,1792]{1,0:T(8,128)S(1)}, u32[]{:S(2)}, u32[]{:S(2)}) collective-permute-start(f32[8,1792]{1,0:T(8,128)S(1)} %shard_map.66.own_ref), channel_id=1, source_target_pairs={{0,16},{8,24},{16,32},{24,40},{32,48},{40,56},{48,0},{56,8},{1,17}... | collective-permute-start | bytes 172040 | tf_op jit(solution)/shard_map/ppermute | solution.py:388
  37.0 6.4 %collective-permute-start.16 = (bf16[64,1024]{1,0:T(8,128)(2,1)S(1)}, bf16[64,1024]{1,0:T(8,128)(2,1)S(1)}, u32[]{:S(2)}, u32[]{:S(2)}) collective-permute-start(bf16[64,1024]{1,0:T(8,128)(2,1)S(1)} %get-tuple-element.50), channel_id=1, source_target_pairs={{0,4},{2,6},{4,0},{6,2},{1,5},{3,7},{5,1},{7,3},{8,12},{10,14},{12... | collective-permute-start | bytes 393224 | tf_op jit(solution)/shard_map/ppermute | solution.py:388
  39.9 5.2 %collective-permute-start.15 = (f32[16,1792]{1,0:T(8,128)S(1)}, f32[16,1792]{1,0:T(8,128)S(1)}, u32[]{:S(2)}, u32[]{:S(2)}) collective-permute-start(f32[16,1792]{1,0:T(8,128)S(1)} %shard_map.68.own_ref), channel_id=1, source_target_pairs={{0,128},{64,192},{128,0},{192,64},{1,129},{65,193},{129,1},{193,65... | collective-permute-start | bytes 344072 | tf_op jit(solution)/shard_map/ppermute | solution.py:388
  43.0 4.9 %collective-permute-start.13 = (f32[16,1792]{1,0:T(8,128)S(1)}, f32[16,1792]{1,0:T(8,128)S(1)}, u32[]{:S(2)}, u32[]{:S(2)}) collective-permute-start(f32[16,1792]{1,0:T(8,128)S(1)} %shard_map.68.own_ref), channel_id=1, source_target_pairs={{0,64},{64,128},{128,192},{192,0},{1,65},{65,129},{129,193},{193,1... | collective-permute-start | bytes 344072 | tf_op jit(solution)/shard_map/ppermute | solution.py:388
  48.9 10.0 %collective-permute-start.17 = (f32[224,128]{1,0:T(8,128)S(1)}, f32[224,128]{1,0:T(8,128)S(1)}, u32[]{:S(2)}, u32[]{:S(2)}) collective-permute-start(f32[224,128]{1,0:T(8,128)S(1)} %get-tuple-element.51.a_ref), channel_id=1, source_target_pairs={{0,1},{1,0},{2,3},{3,2},{4,5},{5,4},{6,7},{7,6},{8,9},{9,8},{10,11... | collective-permute-start | bytes 344072 | tf_op jit(solution)/shard_map/ppermute | solution.py:347
  58.9 5.2 %collective-permute-start.20 = (f32[224,128]{1,0:T(8,128)S(1)}, f32[224,128]{1,0:T(8,128)S(1)}, u32[]{:S(2)}, u32[]{:S(2)}) collective-permute-start(f32[224,128]{1,0:T(8,128)S(1)} %shard_map.70.own_ref), channel_id=1, source_target_pairs={{0,8},{1,5},{2,10},{3,7},{4,12},{5,1},{6,14},{7,3},{8,16},{9,13},{... | collective-permute-start | bytes 344072 | tf_op jit(solution)/shard_map/ppermute | solution.py:358
  60.4 5.3 %collective-permute-start.19 = (f32[224,128]{1,0:T(8,128)S(1)}, f32[224,128]{1,0:T(8,128)S(1)}, u32[]{:S(2)}, u32[]{:S(2)}) collective-permute-start(f32[224,128]{1,0:T(8,128)S(1)} %shard_map.70.own_ref), channel_id=1, source_target_pairs={{0,192},{1,7},{2,194},{3,1},{4,196},{5,3},{6,198},{7,5},{8,200},{9... | collective-permute-start | bytes 344072 | tf_op jit(solution)/shard_map/ppermute | solution.py:358
  66.7 6.1 %collective-permute-start.21 = (f32[16,1024]{1,0:T(8,128)S(1)}, f32[16,1024]{1,0:T(8,128)S(1)}, u32[]{:S(2)}, u32[]{:S(2)}) collective-permute-start(f32[16,1024]{1,0:T(8,128)S(1)} %get-tuple-element.54), channel_id=1, source_target_pairs={{0,8},{1,129},{2,10},{3,131},{4,12},{5,133},{6,14},{7,135},{8,16},... | collective-permute-start | bytes 196616 | tf_op jit(solution)/shard_map/ppermute | solution.py:358
  66.9 6.0 %collective-permute-start.22 = (f32[16,1024]{1,0:T(8,128)S(1)}, f32[16,1024]{1,0:T(8,128)S(1)}, u32[]{:S(2)}, u32[]{:S(2)}) collective-permute-start(f32[16,1024]{1,0:T(8,128)S(1)} %get-tuple-element.55), channel_id=1, source_target_pairs={{0,2},{1,65},{2,4},{3,67},{4,6},{5,69},{6,0},{7,71},{8,10},{9,73},... | collective-permute-start | bytes 196616 | tf_op jit(solution)/shard_map/ppermute | solution.py:358
  67.2 5.6 %collective-permute-start.23 = (f32[16,1024]{1,0:T(8,128)S(1)}, f32[16,1024]{1,0:T(8,128)S(1)}, u32[]{:S(2)}, u32[]{:S(2)}) collective-permute-start(f32[16,1024]{1,0:T(8,128)S(1)} %get-tuple-element.56), channel_id=1, source_target_pairs={{0,6},{1,193},{2,0},{3,195},{4,2},{5,197},{6,4},{7,199},{8,14},{9,... | collective-permute-start | bytes 196616 | tf_op jit(solution)/shard_map/ppermute | solution.py:358
  76.1 8.2 %collective-permute-start.28 = (f32[16,1024]{1,0:T(8,128)S(1)}, f32[16,1024]{1,0:T(8,128)S(1)}, u32[]{:S(2)}, u32[]{:S(2)}) collective-permute-start(f32[16,1024]{1,0:T(8,128)S(1)} %shard_map.75.after_ref.own_ref), channel_id=1, source_target_pairs={{0,64},{1,33},{2,66},{3,35},{4,68},{5,37},{6,70},{7,39},{8,72},{9,... | collective-permute-start | bytes 196616 | tf_op jit(solution)/shard_map/ppermute | solution.py:358
  79.5 5.3 %collective-permute-start.27 = (f32[16,1024]{1,0:T(8,128)S(1)}, f32[16,1024]{1,0:T(8,128)S(1)}, u32[]{:S(2)}, u32[]{:S(2)}) collective-permute-start(f32[16,1024]{1,0:T(8,128)S(1)} %shard_map.75.after_ref.own_ref), channel_id=1, source_target_pairs={{0,6},{1,49},{2,0},{3,51},{4,2},{5,53},{6,4},{7,55},{8,14},{9,57},... | collective-permute-start | bytes 196616 | tf_op jit(solution)/shard_map/ppermute | solution.py:358
  82.0 5.3 %collective-permute-start.26 = (f32[16,1024]{1,0:T(8,128)S(1)}, f32[16,1024]{1,0:T(8,128)S(1)}, u32[]{:S(2)}, u32[]{:S(2)}) collective-permute-start(f32[16,1024]{1,0:T(8,128)S(1)} %shard_map.75.after_ref.own_ref), channel_id=1, source_target_pairs={{0,2},{1,17},{2,4},{3,19},{4,6},{5,21},{6,0},{7,23},{8,10},{9,25},... | collective-permute-start | bytes 196616 | tf_op jit(solution)/shard_map/ppermute | solution.py:358
  87.3 4.9 %collective-permute-start.32 = (f32[16,1024]{1,0:T(8,128)S(1)}, f32[16,1024]{1,0:T(8,128)S(1)}, u32[]{:S(2)}, u32[]{:S(2)}) collective-permute-start(f32[16,1024]{1,0:T(8,128)S(1)} %shard_map.77.own_ref), channel_id=1, source_target_pairs={{0,4},{1,129},{2,6},{3,131},{4,0},{5,133},{6,2},{7,135},{8,12},{9,... | collective-permute-start | bytes 196616 | tf_op jit(solution)/shard_map/ppermute | solution.py:358
  94.9 6.9 %collective-permute-start.36 = (f32[64,1024]{1,0:T(8,128)S(1)}, f32[64,1024]{1,0:T(8,128)S(1)}, u32[]{:S(2)}, u32[]{:S(2)}) collective-permute-start(f32[64,1024]{1,0:T(8,128)S(1)} %shard_map.79.block_ref), channel_id=1, source_target_pairs={{0,8},{1,5},{2,10},{3,7},{4,12},{5,1},{6,14},{7,3},{8,16},{9,13},{... | collective-permute-start | bytes 786440 | tf_op jit(solution)/shard_map/ppermute | solution.py:358
  95.4 8.0 %collective-permute-start.35 = (f32[64,1024]{1,0:T(8,128)S(1)}, f32[64,1024]{1,0:T(8,128)S(1)}, u32[]{:S(2)}, u32[]{:S(2)}) collective-permute-start(f32[64,1024]{1,0:T(8,128)S(1)} %shard_map.79.block_ref), channel_id=1, source_target_pairs={{0,192},{1,7},{2,194},{3,1},{4,196},{5,3},{6,198},{7,5},{8,200},{9... | collective-permute-start | bytes 786440 | tf_op jit(solution)/shard_map/ppermute | solution.py:358
  96.1 8.8 %collective-permute-start.34 = (f32[64,1024]{1,0:T(8,128)S(1)}, f32[64,1024]{1,0:T(8,128)S(1)}, u32[]{:S(2)}, u32[]{:S(2)}) collective-permute-start(f32[64,1024]{1,0:T(8,128)S(1)} %shard_map.79.block_ref), channel_id=1, source_target_pairs={{0,64},{1,3},{2,66},{3,5},{4,68},{5,7},{6,70},{7,1},{8,72},{9,11},... | collective-permute-start | bytes 786440 | tf_op jit(solution)/shard_map/ppermute | solution.py:358
  99.8 6.0 %collective-permute-start.37 = (f32[64,1024]{1,0:T(8,128)S(1)}, f32[64,1024]{1,0:T(8,128)S(1)}, u32[]{:S(2)}, u32[]{:S(2)}) collective-permute-start(f32[64,1024]{1,0:T(8,128)S(1)} %get-tuple-element.60.refs_0_), channel_id=1, source_target_pairs={{0,1},{1,0},{2,3},{3,2},{4,5},{5,4},{6,7},{7,6},{8,9},{9,8},{10,11... | collective-permute-start | bytes 786440 | tf_op jit(solution)/shard_map/ppermute | solution.py:347
  (17 other events, 59.7 us)
